TPU v7x, 256 devices: a whole 4x4x8 slice. The times are simulated.
256 devices in a mesh: ctx: 32 (over x, y, core), head: 8 (over z).
Axes of the slice: x: 4, y: 4, z: 8, core: 2. Of those that a mesh axis runs over, the one named last changes fastest.
Arguments:
- q_latent: bfloat16 [4096, 36864], P('ctx', 'head'), may hold values from -4 to 4
- kv_latent: bfloat16 [4096, 576], P('ctx'), may hold values from -3 to 3
- out_grad: bfloat16 [4096, 32768], P('ctx', 'head'), may hold values from -48 to 48
- saved_out: bfloat16 [4096, 32768], P('ctx', 'head'), may hold values from -3 to 3
- group_order: int32 [64], replicated, may hold values from 0 to 63, as said below
Outputs:
- q_grad: bfloat16 [4096, 36864], P('ctx', 'head')
- kv_grad: float32 [4096, 576], P(('ctx', 'head'))
Inputs may be any that keep to these rules, and one draw needn't show every extreme that they name: `group_order`: stored group slots 2 i and 2 i + 1 hold sequence groups c and 63 - c with c < 32; every group appears once.
All inputs are finite; a program needn't handle non-finite values.
Results may differ from a plain program's by a relative error of at most 0.0049.
Values may be sent and summed in bfloat16 or wider, within the bound.
No kernel may reach another device: no remote copies, remote signals or barrier semaphores. Data moves between devices by JAX's collectives and lax.ppermute only.
A program may use at most 128 MiB of HBM per device.

v0:
```python
import jax
import jax.numpy as jnp
from jax import lax
from jax.sharding import PartitionSpec as P

LATENT = 512
ROPE = 64


score_scale = 192.0 ** (-0.5)
neg_fill = -1e30


def tile_scores(queries, key_tile, query_pos, offset):
    key_pos = offset + jnp.arange(key_tile.shape[0], dtype=jnp.int32)
    visible = key_pos[None, :] <= query_pos[:, None]
    raw = lax.dot_general(
        queries, key_tile, (((1,), (1,)), ((), ())), preferred_element_type=jnp.float32
    )
    return (jnp.where(visible, raw * score_scale, neg_fill), visible)


def shards(q_latent, kv_latent, out_grad, saved_out, group_order):
    row_width = LATENT + ROPE
    local_tokens = q_latent.shape[0]
    head_count = q_latent.shape[1] // row_width
    group_rows = local_tokens // 2
    ctx_count = lax.axis_size("ctx")
    seq_total = local_tokens * ctx_count
    key_block = min(256, seq_total)
    my_rank = lax.axis_index("ctx")
    slot_ids = jnp.arange(2 * ctx_count, dtype=jnp.int32)
    inverse = jnp.zeros((2 * ctx_count,), jnp.int32).at[group_order].set(slot_ids)
    positions = jnp.arange(seq_total, dtype=jnp.int32)
    source_rows = inverse[positions // group_rows] * group_rows + positions % group_rows
    gathered = lax.all_gather(kv_latent, "ctx", axis=0, tiled=True)
    ordered = jnp.take(gathered, source_rows, axis=0)
    key_grad = jnp.zeros((seq_total, row_width), jnp.float32)
    query_rows = group_rows * head_count
    q_pieces = []
    for which_half in range(2):
        seq_group = group_order[2 * my_rank + which_half]
        lower_row = which_half * group_rows
        queries = q_latent[lower_row : lower_row + group_rows].reshape(query_rows, row_width)
        cotangent = out_grad[lower_row : lower_row + group_rows].reshape(query_rows, LATENT)
        outputs = saved_out[lower_row : lower_row + group_rows].reshape(query_rows, LATENT)
        deltas = jnp.sum(
            cotangent.astype(jnp.float32) * outputs.astype(jnp.float32), axis=1, keepdims=True
        )
        query_pos = seq_group * group_rows + jnp.arange(query_rows, dtype=jnp.int32) // head_count
        needed = (seq_group * group_rows + group_rows - 1) // key_block + 1

        def stat_step(block_index, carried):
            running_max, running_sum = carried
            offset = block_index * key_block
            key_tile = lax.dynamic_slice_in_dim(ordered, offset, key_block, 0)
            scores, visible = tile_scores(queries, key_tile, query_pos, offset)
            new_max = jnp.maximum(running_max, jnp.max(scores, axis=1, keepdims=True))
            tile_sum = jnp.sum(
                jnp.where(visible, jnp.exp(scores - new_max), 0.0), axis=1, keepdims=True
            )
            return (new_max, running_sum * jnp.exp(running_max - new_max) + tile_sum)

        start_max = jnp.full((query_rows, 1), neg_fill, jnp.float32)
        start_sum = jnp.zeros((query_rows, 1), jnp.float32)
        final_max, final_sum = lax.fori_loop(0, needed, stat_step, (start_max, start_sum))
        log_norm = final_max + jnp.log(final_sum)

        def grad_step(block_index, carried):
            q_acc, grads = carried
            offset = block_index * key_block
            key_tile = lax.dynamic_slice_in_dim(ordered, offset, key_block, 0)
            scores, visible = tile_scores(queries, key_tile, query_pos, offset)
            weights = jnp.where(visible, jnp.exp(scores - log_norm), 0.0)
            dweights = lax.dot_general(
                cotangent,
                key_tile[:, :LATENT],
                (((1,), (1,)), ((), ())),
                preferred_element_type=jnp.float32,
            )
            dscores = (weights * (dweights - deltas) * score_scale).astype(jnp.bfloat16)
            q_acc = q_acc + jnp.dot(dscores, key_tile, preferred_element_type=jnp.float32)
            key_term = lax.dot_general(
                dscores, queries, (((0,), (0,)), ((), ())), preferred_element_type=jnp.float32
            )
            value_term = lax.dot_general(
                weights.astype(jnp.bfloat16),
                cotangent,
                (((0,), (0,)), ((), ())),
                preferred_element_type=jnp.float32,
            )
            key_term = key_term + jnp.pad(value_term, ((0, 0), (0, ROPE)))
            current = lax.dynamic_slice_in_dim(grads, offset, key_block, 0)
            grads = lax.dynamic_update_slice_in_dim(grads, current + key_term, offset, 0)
            return (q_acc, grads)

        start_q = jnp.zeros((query_rows, row_width), jnp.float32)
        q_acc, key_grad = lax.fori_loop(0, needed, grad_step, (start_q, key_grad))
        q_pieces.append(q_acc.astype(jnp.bfloat16).reshape(group_rows, head_count * row_width))
    q_grad = jnp.concatenate(q_pieces, axis=0)
    stored = jnp.arange(seq_total, dtype=jnp.int32)
    stored_pos = group_order[stored // group_rows] * group_rows + stored % group_rows
    partial_rows = jnp.take(key_grad, stored_pos, axis=0)
    kv_grad = lax.psum_scatter(partial_rows, ("ctx", "head"), scatter_dimension=0, tiled=True)
    return (q_grad, kv_grad)


def solution(mesh):
    placed = (P("ctx", "head"), P("ctx", None), P("ctx", "head"), P("ctx", "head"), P())
    return jax.shard_map(
        shards,
        mesh=mesh,
        in_specs=placed,
        out_specs=(P("ctx", "head"), P(("ctx", "head"), None)),
        check_vma=False,
    )
```

profile of v0, /device:TPU:32, one launch (start us, length us, event | category | flops | bytes accessed | tf_op | source)
XLA Modules:
  0.0 1633.3 jit_solution(5602431222604448166)
XLA Ops:
  16.1 2.8 slice_convert_fusion
  18.8 2.4 reshape.173
  21.3 2.4 reshape.172
  35.7 4.4 compare_select_fusion.7
  40.1 35.7 %compare_and_fusion.1 = (pred[4096]{0:T(1024)(128)(4,1)S(1)}, s32[4096]{0:T(1024)S(1)}) fusion(pred[4096]{0:T(1024)(128)(4,1)S(1)} %compare_reduce_fusion, pred[4096]{0:T(1024)(128)(4,1)S(1)} %compare_reduce_fusion.1, pred[4096]{0:T(1024)(128)(4,1)S(1)} %compare_reduce_fusion.2, pred[4096]{0:T(1024)(128)(4,1)S(1)} %compare_reduce_fusion.3, ...), kind=kLoop, calls=%fused_computation.199 | loop fusion | flops 290816 | bytes 270564 | tf_op jit(solution)/shard_map/jit(_take)/and | solution.py:37
  75.9 4.3 compare_select_fusion.8
  80.2 36.0 %compare_and_fusion = (pred[4096]{0:T(1024)(128)(4,1)S(1)}, s32[4096]{0:T(1024)S(1)}) fusion(pred[4096]{0:T(1024)(128)(4,1)S(1)} %compare_reduce_fusion, pred[4096]{0:T(1024)(128)(4,1)S(1)} %compare_reduce_fusion.1, pred[4096]{0:T(1024)(128)(4,1)S(1)} %compare_reduce_fusion.2, pred[4096]{0:T(1024)(128)(4,1)S(1)} %compare_reduce_fusion.3, ...), kind=kLoop, calls=%fused_computation.198 | loop fusion | flops 290816 | bytes 270564 | tf_op jit(solution)/shard_map/jit(_take)/and | solution.py:103
  116.3 21.2 %gather_fusion = bf16[4096,576]{1,0:T(8,128)(2,1)} fusion(bf16[4096,576]{1,0:T(8,128)(2,1)} %all-gather.2.cloned.1.call-done, s32[4096]{0:T(1024)S(1)} %broadcast_clamp_fusion.1), kind=kCustom, calls=%fused_computation | custom fusion | bytes 9453568 | tf_op jit(solution)/shard_map/jit(_take)/gather | solution.py:37
  137.4 6.9 broadcast_select_fusion.1
  144.3 26.2 %while.58 = (s32[]{:T(128)}, f32[512,1]{0,1:T(1,128)S(1)}, f32[512,1]{0,1:T(1,128)S(1)}, s32[]{:T(128)}, bf16[4096,576]{1,0:T(8,128)(2,1)}, /*index=5*/bf16[512,...) while((s32[]{:T(128)}, f32[512,1]{0,1:T(1,128)S(1)}, ...), condition=%wide.region_11.12_spmd.clone, body=%wide.region_8.11_spmd.clone.sunk | while | flops 152049408 | bytes 2002087 | solution.py:66
  173.2 4.8 broadcast_in_dim.91
  178.0 6.8 while.57
  182.5 2.3 fusion.159
  185.0 113.9 %while.59 = (s32[]{:T(128)}, f32[512,576]{0,1:T(8,128)S(1)}, f32[4096,576]{0,1:T(8,128)}, s32[]{:T(128)}, bf16[4096,576]{1,0:T(8,128)(2,1)}, /*index=5*/bf16[512...) while((s32[]{:T(128)}, f32[512,576]{0,1:T(8,128)S(1)}, ...), condition=%wide.region_14.15_spmd.clone, body=%wide.region_13.14_spmd.clone.sunk | while | flops 723325696 | bytes 12527847 | solution.py:98
  189.8 2.3 fusion.178
  192.1 1.7 fusion.175
  196.9 2.3 fusion.178
  199.2 1.7 fusion.175
  204.0 2.3 fusion.178
  206.3 1.7 fusion.175
  211.1 2.3 fusion.178
  213.4 1.7 fusion.175
  218.2 2.3 fusion.178
  220.6 1.7 fusion.175
  225.4 2.4 fusion.178
  227.7 1.7 fusion.175
  232.5 2.3 fusion.178
  234.8 1.7 fusion.175
  239.6 2.3 fusion.178
  242.0 1.7 fusion.175
  246.8 2.3 fusion.178
  249.1 1.7 fusion.175
  253.9 2.3 fusion.178
  256.2 1.7 fusion.175
  261.0 2.3 fusion.178
  263.3 1.7 fusion.175
  268.1 2.3 fusion.178
  270.4 1.7 fusion.175
  275.2 2.3 fusion.178
  282.3 2.3 fusion.178
  284.7 1.7 fusion.175
  289.5 2.3 fusion.178
  291.8 1.7 fusion.175
  296.6 2.3 fusion.178
  298.9 10.7 copy.18
  309.5 22.9 %gather_fusion.1 = f32[4096,576]{1,0:T(8,128)} fusion(f32[4096,576]{1,0:T(8,128)} %copy.18, s32[4096]{0:T(1024)S(1)} %broadcast_clamp_fusion), kind=kCustom, calls=%fused_computation.1 | custom fusion | bytes 18890752 | tf_op jit(solution)/shard_map/jit(_take)/gather | solution.py:103
  332.4 9.7 broadcast_select_fusion
  346.7 1279.8 %reduce-scatter.2.cloned.1.call-done = f32[16,576]{1,0:T(8,128)} async-done(((f32[4096,576]{1,0:T(8,128)}), f32[16,576]{1,0:T(8,128)}) %reduce-scatter.2.cloned.1.call-update) | async-done | bytes 36880 | tf_op jit(solution)/shard_map/reduce_scatter | solution.py:104
  (345 shorter events, 110.5 us)
Async XLA Ops:
  7.2 109.1 %all-gather.2.cloned.1.call-start = ((), (), s32[]{:S(2)}) async-start(), calls=%async_computation.1 | async-start | bytes 5406720 | tf_op jit(solution)/shard_map/all_gather | solution.py:36
  8.9 1617.6 %reduce-scatter.2.cloned.1.call-start = ((), (), s32[]{:S(2)}) async-start(), calls=%async_computation.2 | async-start | bytes 10526720 | tf_op jit(solution)/shard_map/reduce_scatter | solution.py:104
  15.0 8.6 copy-start.2
  170.6 0.8 copy-start
  185.0 4.8 copy-start.1
  192.1 4.8 copy-start.1
  199.2 4.8 copy-start.1
  206.3 4.8 copy-start.1
  213.4 4.8 copy-start.1
  220.5 4.8 copy-start.1
  227.7 4.8 copy-start.1
  234.8 4.8 copy-start.1
  242.0 4.8 copy-start.1
  249.1 4.8 copy-start.1
  256.2 4.8 copy-start.1
  263.3 4.8 copy-start.1
  270.4 4.8 copy-start.1
  277.5 4.8 copy-start.1
  284.7 4.8 copy-start.1
  291.8 4.8 copy-start.1
Sparse Core Ops, SparseCore 0:
  10.5 55.1 all-gather.1
  342.2 1284.2 reduce-scatter.1
where the time goes:
time: 1640 us; the launch traced here: 1630 us
  waiting for transfers between devices  1280 us (78%)
  matrix products  144 us (9%)
  other arithmetic  111 us (7%)
  local copies, waits for them, and re-layouts  81.4 us (5%)
    reduce_scatter x1, waiting for transfers between devices, shards(): lax.psum_scatter(partial_rows, ('ctx', 'head'), scatter_dimension=0, tile...  1280 us
    dot_general x34, matrix products, tile_scores(): lax.dot_general(queries, key_tile, (((1,), (1,)), ((), ())), preferred_el...  52.9 us
    dot_general x17, matrix products, grad_step(): lax.dot_general(dscores, queries, (((0,), (0,)), ((), ())), preferred_ele...  39.2 us
    and x1, other arithmetic, shards(): partial_rows = jnp.take(key_grad, stored_pos, axis=0)  36 us
    and x1, other arithmetic, shards(): ordered = jnp.take(gathered, source_rows, axis=0)  35.7 us
  transfers between devices with their start and end apart: 2, of which 1 were waited for; matrix products, arithmetic and copies ran while one was open for 7% of the time, Pallas kernels for 0%

commit v1 on v0

v1 whole, which is shorter than its diff:
```python
import functools
import math

import jax
import jax.numpy as jnp
from jax import lax
from jax.experimental import pallas as pl
from jax.experimental.pallas import tpu as pltpu
from jax.sharding import Mesh, PartitionSpec as P

LATENT = 512
ROPE = 64
WIDTH = LATENT + ROPE
GROUP = 64
BLOCK = 256
PAIR = 2 * GROUP

score_scale = 192.0 ** (-0.5)
log2_scale = score_scale * math.log2(math.e)
neg_fill = -1e30

NT = (((1,), (1,)), ((), ()))


def mm(a, b):
    return jnp.dot(a, b, preferred_element_type=jnp.float32)


def twice(a):
    return jnp.concatenate([a, a], axis=1)


def grad_kernel(
    order, place, q_rows, q_cols, g_rows, g_cols, deltas, *rest, pieces, piece_y, sides, rows
):
    piece_refs = rest[:pieces]
    dq_out, keep_out, send_out = rest[pieces : pieces + 3]
    stage, keys, scores, top, total, dq_acc, dk_acc, slot_of, sem = rest[pieces + 3 :]
    pairs = stage.shape[0]
    groups = 2 * pairs
    blocks = groups * GROUP // BLOCK
    items = blocks + 1
    per_block = BLOCK // GROUP
    my_x, my_y, my_c = place[0], place[1], place[2]
    rank = (my_x * sides + my_y) * 2 + my_c

    copies = []
    for at, ref in enumerate(piece_refs):
        step_x, step_c = at // 2, at % 2
        for step_y in range(piece_y):
            at_x = lax.rem(my_x + step_x, sides)
            at_y = lax.rem(my_y + step_y, sides)
            at_c = lax.rem(my_c + step_c, 2)
            pair = (at_x * sides + at_y) * 2 + at_c
            copy = pltpu.make_async_copy(
                ref.at[step_y], stage.at[pair], sem.at[at * piece_y + step_y]
            )
            copy.start()
            copies.append(copy)

    def note(p, carry):
        slot_of[order[2 * p]] = p
        return carry

    lax.fori_loop(0, pairs, note, 0)
    top[...] = jnp.full(top.shape, neg_fill, jnp.float32)
    total[...] = jnp.zeros(total.shape, jnp.float32)
    dq_acc[...] = jnp.zeros(dq_acc.shape, jnp.float32)
    for copy in copies:
        copy.wait()

    def place_low(i, carry):
        first = stage[slot_of[2 * i]]
        second = stage[slot_of[2 * i + 1]]
        at = pl.multiple_of(i * PAIR, PAIR)
        keys[:, pl.ds(at, PAIR)] = jnp.concatenate([first[:, :GROUP], second[:, :GROUP]], axis=1)
        return carry

    def place_high(i, carry):
        first = stage[slot_of[groups - 1 - 2 * i]]
        second = stage[slot_of[groups - 2 - 2 * i]]
        at = pl.multiple_of(i * PAIR, PAIR)
        keys[:, pl.ds(at, PAIR)] = jnp.concatenate([first[:, GROUP:], second[:, GROUP:]], axis=1)
        return carry

    lax.fori_loop(0, pairs // 2, place_low, 0)
    lax.fori_loop(pairs // 2, pairs, place_high, 0)

    low_group = order[2 * rank]
    high_group = order[2 * rank + 1]
    high_blocks = lax.div(high_group, per_block) + 1

    def item(i):
        is_low = (i >= high_blocks).astype(jnp.int32)
        block = i - is_low * high_blocks
        row0 = pl.multiple_of((1 - is_low) * rows, rows)
        key0 = pl.multiple_of(block * BLOCK, BLOCK)
        return is_low, block, row0, key0

    def score_step(i, carry):
        is_low, block, row0, key0 = item(i)
        group = jnp.where(is_low == 1, low_group, high_group)
        raw = mm(q_rows[pl.ds(row0, rows), :], keys[:, pl.ds(key0, BLOCK)]) * log2_scale
        token = lax.broadcasted_iota(jnp.int32, (rows, BLOCK), 0) % GROUP
        lane = lax.broadcasted_iota(jnp.int32, (rows, BLOCK), 1)
        visible = lane - token <= group * GROUP - block * BLOCK
        t = jnp.where(visible, raw, neg_fill)
        scores[i] = t
        left, right = t[:, : BLOCK // 2], t[:, BLOCK // 2 :]
        old_top = top[pl.ds(row0, rows), :]
        new_top = jnp.maximum(old_top, jnp.maximum(left, right))
        added = jnp.exp2(left - new_top) + jnp.exp2(right - new_top)
        total[pl.ds(row0, rows), :] = total[pl.ds(row0, rows), :] * jnp.exp2(old_top - new_top) + added
        top[pl.ds(row0, rows), :] = new_top
        return carry

    lax.fori_loop(0, items, score_step, 0)

    lane_top = top[...]
    row_top = jnp.max(lane_top, axis=1, keepdims=True)
    row_sum = jnp.sum(total[...] * jnp.exp2(lane_top - row_top), axis=1, keepdims=True)
    top[...] = jnp.broadcast_to(row_top + jnp.log2(row_sum), top.shape)

    def clear(b, carry):
        at = pl.multiple_of(b * BLOCK, BLOCK)
        dk_acc[:, pl.ds(at, BLOCK)] = jnp.zeros((WIDTH, BLOCK), jnp.float32)
        return carry

    lax.fori_loop(high_blocks, blocks, clear, 0)

    def grad_step(i, carry):
        is_low, block, row0, key0 = item(i)
        key_tile = keys[:, pl.ds(key0, BLOCK)]
        weights = jnp.exp2(scores[i] - twice(top[pl.ds(row0, rows), :]))
        dweights = mm(g_rows[pl.ds(row0, rows), :], key_tile[:LATENT])
        dscores = weights * (dweights - twice(deltas[pl.ds(row0, rows), :])) * score_scale
        low = dscores.astype(jnp.bfloat16)
        weights_low = weights.astype(jnp.bfloat16)
        dq_acc[pl.ds(row0, rows), :] += lax.dot_general(
            low, key_tile, NT, preferred_element_type=jnp.float32
        )
        from_scores = mm(q_cols[:, pl.ds(row0, rows)], low)
        from_values = mm(g_cols[:, pl.ds(row0, rows)], weights_low)
        old = dk_acc[:, pl.ds(key0, BLOCK)]
        old = jnp.where(is_low == 1, old, 0.0)
        dk_acc[:LATENT, pl.ds(key0, BLOCK)] = old[:LATENT] + from_scores[:LATENT] + from_values
        dk_acc[LATENT:, pl.ds(key0, BLOCK)] = old[LATENT:] + from_scores[LATENT:]
        return carry

    lax.fori_loop(0, items, grad_step, 0)

    dq_out[...] = dq_acc[...].astype(jnp.bfloat16)

    def emit(p, carry):
        group = order[2 * p]
        low_at = pl.multiple_of(lax.div(group, 2) * PAIR, PAIR)
        high_at = pl.multiple_of(lax.div(groups - 1 - group, 2) * PAIR, PAIR)
        low_tile = dk_acc[:, pl.ds(low_at, PAIR)]
        high_tile = dk_acc[:, pl.ds(high_at, PAIR)]
        odd = lax.rem(group, 2) == 1
        mine = lax.rem(p, 2) == my_c

        def put(tile):
            tile = tile.astype(jnp.bfloat16)

            @pl.when(mine)
            def _():
                keep_out[lax.div(p, 2)] = tile

            @pl.when(jnp.logical_not(mine))
            def _():
                send_out[lax.div(p, 2)] = tile

        @pl.when(odd)
        def _():
            put(jnp.concatenate([low_tile[:, GROUP:], high_tile[:, :GROUP]], axis=1))

        @pl.when(jnp.logical_not(odd))
        def _():
            lane = lax.broadcasted_iota(jnp.int32, (WIDTH, PAIR), 1)
            put(jnp.where(lane < GROUP, low_tile, high_tile))

        return carry

    lax.fori_loop(0, pairs, emit, 0)


def run_grads(order, place, q_rows, q_cols, g_rows, g_cols, deltas, pieces, sides):
    rows = q_rows.shape[0] // 2
    piece_y = pieces[0].shape[0]
    pairs = len(pieces) * piece_y
    items = pairs * PAIR // BLOCK + 1
    vmem = pl.BlockSpec(memory_space=pltpu.VMEM)
    smem = pl.BlockSpec(memory_space=pltpu.SMEM)
    half = pairs // 2
    return pl.pallas_call(
        functools.partial(
            grad_kernel, pieces=len(pieces), piece_y=piece_y, sides=sides, rows=rows
        ),
        out_shape=(
            jax.ShapeDtypeStruct((2 * rows, WIDTH), jnp.bfloat16),
            jax.ShapeDtypeStruct((half, WIDTH, PAIR), jnp.bfloat16),
            jax.ShapeDtypeStruct((half, WIDTH, PAIR), jnp.bfloat16),
        ),
        in_specs=[smem, smem] + [vmem] * 5 + [pl.BlockSpec(memory_space=pl.ANY)] * len(pieces),
        out_specs=(vmem, vmem, vmem),
        scratch_shapes=[
            pltpu.VMEM((pairs, WIDTH, PAIR), jnp.bfloat16),
            pltpu.VMEM((WIDTH, pairs * PAIR), jnp.bfloat16),
            pltpu.VMEM((items, rows, BLOCK), jnp.float32),
            pltpu.VMEM((2 * rows, 128), jnp.float32),
            pltpu.VMEM((2 * rows, 128), jnp.float32),
            pltpu.VMEM((2 * rows, WIDTH), jnp.float32),
            pltpu.VMEM((WIDTH, pairs * PAIR), jnp.float32),
            pltpu.SMEM((2 * pairs,), jnp.int32),
            pltpu.SemaphoreType.DMA((pairs,)),
        ],
        compiler_params=pltpu.CompilerParams(vmem_limit_bytes=60 * 1024 * 1024),
        cost_estimate=pl.CostEstimate(
            flops=items * rows * BLOCK * 2 * 2752, bytes_accessed=24 << 20, transcendentals=0
        ),
        name="latent_grads",
    )(order, place, q_rows, q_cols, g_rows, g_cols, deltas, *pieces)


def shift(a, axis, size, step):
    return lax.ppermute(a, axis, [(i, (i - step) % size) for i in range(size)])


def head_rows(a, width):
    tokens = a.shape[0]
    heads = a.shape[1] // width
    a = a.reshape(2, tokens // 2, heads, width).transpose(0, 2, 1, 3)
    return a.reshape(tokens * heads, width)


def shards(q_latent, kv_latent, out_grad, saved_out, group_order, *, sides, depth):
    tokens = q_latent.shape[0]
    heads = q_latent.shape[1] // WIDTH
    place = jnp.stack([lax.axis_index("x"), lax.axis_index("y"), lax.axis_index("c")]).astype(jnp.int32)

    own = kv_latent.T
    along_y = jnp.stack([own] + [shift(own, "y", sides, d) for d in range(1, sides)])
    along_x = [along_y] + [shift(along_y, "x", sides, d) for d in range(1, sides)]
    pieces = []
    for piece in along_x:
        pieces += [piece, shift(piece, "c", 2, 1)]

    q_rows = head_rows(q_latent, WIDTH)
    g_rows = head_rows(out_grad, LATENT)
    delta = jnp.sum(
        (out_grad.astype(jnp.float32) * saved_out.astype(jnp.float32)).reshape(
            2, tokens // 2, heads, LATENT
        ),
        axis=3,
    )
    delta = delta.transpose(0, 2, 1).reshape(tokens * heads, 1)
    deltas = jnp.broadcast_to(delta, (tokens * heads, 128))

    dq, keep, send = run_grads(
        group_order, place, q_rows, q_rows.T, g_rows, g_rows.T, deltas, pieces, sides
    )
    q_grad = dq.reshape(2, heads, tokens // 2, WIDTH).transpose(0, 2, 1, 3)
    q_grad = q_grad.reshape(tokens, heads * WIDTH)

    def added(parts):
        return jnp.sum(parts.astype(jnp.float32), axis=0)

    received = lax.ppermute(send, "c", [(0, 1), (1, 0)])
    both = (keep.astype(jnp.float32) + received.astype(jnp.float32)).astype(jnp.bfloat16)
    parts = lax.all_to_all(both, ("x", "y"), 0, 0, tiled=True)
    summed = added(parts)
    by_head = summed.reshape(WIDTH, depth, PAIR // depth).transpose(1, 2, 0)
    parts = lax.all_to_all(by_head.astype(jnp.bfloat16), "z", 0, 0, tiled=True)
    return q_grad, added(parts)


def solution(mesh):
    ctx, depth = mesh.shape["ctx"], mesh.shape["head"]
    sides = math.isqrt(ctx // 2)
    finer = Mesh(mesh.devices.reshape(sides, sides, 2, depth), ("x", "y", "c", "z"))
    ctx_axes = ("x", "y", "c")
    placed = (P(ctx_axes, "z"), P(ctx_axes, None), P(ctx_axes, "z"), P(ctx_axes, "z"), P())
    return jax.shard_map(
        functools.partial(shards, sides=sides, depth=depth),
        mesh=finer,
        in_specs=placed,
        out_specs=(P(ctx_axes, "z"), P(("x", "y", "c", "z"), None)),
        check_vma=False,
    )
```

time: 1640 us -> 164 us (0.10)
  waiting for transfers between devices: 1280 us -> 38.4 us
  matrix products: 144 us -> 0 us
  other arithmetic: 111 us -> 7.76 us
  local copies, waits for them, and re-layouts: 81.4 us -> 15.9 us
  Pallas kernels: 0 us -> 43 us
  blocking collectives: 0 us -> 37.9 us
  starting transfers between devices: 0.08 us -> 20.1 us
    reduce_scatter x1 -> x0, waiting for transfers between devices: 1280 us -> none  [shards(): lax.psum_scatter(partial_rows, ('ctx', 'head'), scatter_dimension=0, tile...]
    dot_general x102 -> x0, matrix products: 144 us -> none  [the longest x34 52.9 us: tile_scores(): lax.dot_general(queries, key_tile, (((1,), (1,)), ((), ())), preferred_el...]
    and x2 -> x0, other arithmetic: 71.7 us -> none  [the longest x1 36 us: shards(): partial_rows = jnp.take(key_grad, stored_pos, axis=0)]
    gather x10 -> x0, local copies, waits for them, and re-layouts: 50.8 us -> none  [the longest x1 22.9 us: shards(): partial_rows = jnp.take(key_grad, stored_pos, axis=0)]
    pallas_call x0 -> x1, Pallas kernels: none -> 43 us  [run_grads(): pl.pallas_call(functools.partial(grad_kernel, pieces=len(pieces), piece_y...]
    all_to_all x0 -> x1, blocking collectives: none -> 37.9 us  [shards(): parts = lax.all_to_all(both, ('x', 'y'), 0, 0, tiled=True)]
    ppermute x0 -> x11, waiting for transfers between devices: none -> 34.2 us  [the longest x10 29.4 us: shift(): return lax.ppermute(a, axis, [(i, (i - step) % size) for i in range(size)])]
    select_n x5 -> x0, other arithmetic: 16.6 us -> none  [the longest x2 9.7 us: shards(): partial_rows = jnp.take(key_grad, stored_pos, axis=0)]
  transfers between devices with their start and end apart: 2 -> 12, of which waited for: 1 -> 7; matrix products, arithmetic and copies ran while one was open for 7% -> 10% of each run, Pallas kernels for 0% -> 0%
where the time goes in v1:
time: 164 us
  Pallas kernels  43 us (26%)
  waiting for transfers between devices  38.4 us (23%)
  blocking collectives  37.9 us (23%)
  starting transfers between devices  20.1 us (12%)
  local copies, waits for them, and re-layouts  15.9 us (10%)
  other arithmetic  7.76 us (5%)
    pallas_call x1, Pallas kernels, run_grads(): pl.pallas_call(functools.partial(grad_kernel, pieces=len(pieces), piece_y...  43 us
    all_to_all x1, blocking collectives, shards(): parts = lax.all_to_all(both, ('x', 'y'), 0, 0, tiled=True)  37.9 us
    ppermute x10, waiting for transfers between devices, shift(): return lax.ppermute(a, axis, [(i, (i - step) % size) for i in range(size)])  29.4 us
    ppermute x10, starting transfers between devices, shift(): return lax.ppermute(a, axis, [(i, (i - step) % size) for i in range(size)])  11.5 us
    all_to_all x1, starting transfers between devices, shards(): parts = lax.all_to_all(by_head.astype(jnp.bfloat16), 'z', 0, 0, tiled=True)  8.57 us
    reshape x2, local copies, waits for them, and re-layouts, head_rows(): a = a.reshape(2, tokens // 2, heads, width).transpose(0, 2, 1, 3)  4.96 us
    ppermute x1, waiting for transfers between devices, shards(): received = lax.ppermute(send, 'c', [(0, 1), (1, 0)])  4.73 us
    all_to_all x1, waiting for transfers between devices, shards(): parts = lax.all_to_all(by_head.astype(jnp.bfloat16), 'z', 0, 0, tiled=True)  4.2 us
  transfers between devices with their start and end apart: 12, of which 7 were waited for; matrix products, arithmetic and copies ran while one was open for 10% of the time, Pallas kernels for 0%

profile of v1, /device:TPU:32, one launch (start us, length us, event | category | flops | bytes accessed | tf_op | source)
XLA Modules:
  0.0 163.8 jit_solution(18019850277507258145)
XLA Ops:
  0.6 3.3 %collective-permute-start.1 = (bf16[576,128]{1,0:T(8,128)(2,1)}, bf16[576,128]{1,0:T(8,128)(2,1)S(1)}, u32[]{:S(2)}, u32[]{:S(2)}) collective-permute-start(bf16[576,128]{1,0:T(8,128)(2,1)} %bitcast.48), channel_id=1, source_target_pairs={{0,32},{16,48},{32,0},{48,16},{1,33},{17,49},{33,1},{49,17},{2,34}... | collective-permute-start | bytes 442376 | tf_op jit(solution)/shard_map/ppermute | solution.py:227
  3.9 1.1 collective-permute-start
  5.0 1.0 collective-permute-start.2
  5.9 3.1 %collective-permute-done.1 = bf16[576,128]{1,0:T(8,128)(2,1)S(1)} collective-permute-done((bf16[576,128]{1,0:T(8,128)(2,1)}, bf16[576,128]{1,0:T(8,128)(2,1)S(1)}, u32[]{:S(2)}, u32[]{:S(2)}) %collective-permute-start.1) | collective-permute-done | bytes 147488 | tf_op jit(solution)/shard_map/ppermute | solution.py:227
  9.0 2.5 %collective-permute-done = bf16[576,128]{1,0:T(8,128)(2,1)S(1)} collective-permute-done((bf16[576,128]{1,0:T(8,128)(2,1)}, bf16[576,128]{1,0:T(8,128)(2,1)S(1)}, u32[]{:S(2)}, u32[]{:S(2)}) %collective-permute-start) | collective-permute-done | bytes 147488 | tf_op jit(solution)/shard_map/ppermute | solution.py:227
  11.5 0.3 collective-permute-done.2
  11.8 1.8 %pad_maximum_fusion.rest_0_ = bf16[4,576,128]{2,1,0:T(8,128)(2,1)} fusion(bf16[1,576,128]{2,1,0:T(8,128)(2,1)S(1)} %bitcast.54, bf16[1,576,128]{2,1,0:T(8,128)(2,1)S(1)} %bitcast.52, bf16[1,576,128]{2,1,0:T(8,128)(2,1)S(1)} %bitcast.53, bf16[1,576,128]{2,1,0:T(8,128)(2,1)} %bitcast.51), kind=kLoop, calls=%fused_computation.4 | loop fusion | flops 884736 | bytes 1179648 | tf_op jit(solution)/shard_map/stack | solution.py:243
  13.6 1.5 collective-permute-start.8
  15.1 2.7 %collective-permute-start.6 = (bf16[4,576,128]{2,1,0:T(8,128)(2,1)}, bf16[4,576,128]{2,1,0:T(8,128)(2,1)}, u32[]{:S(2)}, u32[]{:S(2)}) collective-permute-start(bf16[4,576,128]{2,1,0:T(8,128)(2,1)} %pad_maximum_fusion.rest_0_), channel_id=1, source_target_pairs={{0,128},{64,192},{128,0},{192,64},{1,129},{65,193},{129,1},{193,65... | collective-permute-start | bytes 1769480 | tf_op jit(solution)/shard_map/ppermute | solution.py:227
  17.8 1.4 collective-permute-start.4
  19.3 0.0 collective-permute-start.3
  19.3 11.1 %collective-permute-done.8.rest_6_ = bf16[4,576,128]{2,1,0:T(8,128)(2,1)} collective-permute-done((bf16[4,576,128]{2,1,0:T(8,128)(2,1)}, bf16[4,576,128]{2,1,0:T(8,128)(2,1)}, u32[]{:S(2)}, u32[]{:S(2)}) %collective-permute-start.8) | collective-permute-done | bytes 589856 | tf_op jit(solution)/shard_map/ppermute | solution.py:227
  30.4 0.0 collective-permute-start.9
  30.4 12.4 %collective-permute-done.6.rest_4_ = bf16[4,576,128]{2,1,0:T(8,128)(2,1)} collective-permute-done((bf16[4,576,128]{2,1,0:T(8,128)(2,1)}, bf16[4,576,128]{2,1,0:T(8,128)(2,1)}, u32[]{:S(2)}, u32[]{:S(2)}) %collective-permute-start.6) | collective-permute-done | bytes 589856 | tf_op jit(solution)/shard_map/ppermute | solution.py:227
  42.8 0.0 collective-permute-start.7
  42.8 0.0 collective-permute-done.4.rest_2_
  42.8 0.5 collective-permute-start.5
  43.3 1.8 %convert_multiply_fusion = f32[128,4096]{1,0:T(8,128)S(1)} fusion(bf16[128,4096]{1,0:T(8,128)(2,1)} %param.8, bf16[128,4096]{1,0:T(8,128)(2,1)} %param.7), kind=kLoop, calls=%fused_computation.2 | loop fusion | flops 1572864 | bytes 4194304 | tf_op jit(solution)/shard_map/mul | solution.py:252
  45.2 0.4 copy.28
  45.6 0.1 bitcast_bitcast_fusion
  45.6 0.3 copy.23
  46.0 1.4 copy.24
  47.4 3.4 %reshape.29 = bf16[2,64,8,576]{3,2,1,0:T(8,128)(2,1)} reshape(bf16[128,4608]{1,0:T(8,128)(2,1)} %param.5) | data formatting | bytes 2359296 | tf_op jit(solution)/shard_map/reshape | solution.py:233
  50.8 1.5 copy.21
  52.3 0.0 copy-start
  52.3 1.5 copy.22
  53.8 1.6 copy.29
  55.5 0.2 bitcast_reduce_fusion
  55.7 0.1 copy.25
  55.8 0.1 broadcast_in_dim.7
  55.8 0.7 pad_add_fusion.place
  56.5 0.0 collective-permute-done.3.rest_1_
  56.5 0.0 collective-permute-done.9.rest_7_
  56.5 0.0 collective-permute-done.7.rest_5_
  56.5 0.0 collective-permute-done.5.rest_3_
  56.5 1.0 broadcast_in_dim.8.deltas
  57.5 43.0 %latent_grads.1 = (bf16[1024,576]{1,0:T(8,128)(2,1)}, bf16[16,576,128]{2,1,0:T(8,128)(2,1)}, bf16[16,576,128]{2,1,0:T(8,128)(2,1)}) custom-call(s32[64]{0:T(128)} %order.1, s32[3]{0:T(128)} %pad_add_fusion.place, bf16[1024,576]{1,0:T(8,128)(2,1)} %bitcast.39, bf16[576,1024]{1,0:T(8,128)(2,1)} %bitcast.45, bf16[1024,512]{1,0:T(8,128)(2,1)} %bitcast.41, ...), custom_call_target="tpu_custom_call" | custom-call | flops 12264144896 | bytes 25165824 | tf_op jit(solution)/shard_map/latent_grads/pallas_call | solution.py:196
  100.5 0.1 collective-permute-start.10
  100.6 4.7 %collective-permute-done.10 = bf16[16,576,128]{2,1,0:T(8,128)(2,1)S(1)} collective-permute-done((bf16[16,576,128]{2,1,0:T(8,128)(2,1)}, bf16[16,576,128]{2,1,0:T(8,128)(2,1)S(1)}, u32[]{:S(2)}, u32[]{:S(2)}) %collective-permute-start.10) | collective-permute-done | bytes 2359328 | tf_op jit(solution)/shard_map/ppermute | solution.py:269
  105.3 2.3 %add_convert_fusion = bf16[16,576,128]{2,1,0:T(8,128)(2,1)S(1)} fusion(bf16[16,576,128]{2,1,0:T(8,128)(2,1)S(1)} %collective-permute-done.10, bf16[16,576,128]{2,1,0:T(8,128)(2,1)} %get-tuple-element.6), kind=kLoop, calls=%fused_computation | loop fusion | flops 4718592 | bytes 7077888 | tf_op jit(solution)/shard_map/convert_element_type | solution.py:270
  107.6 37.9 %all_to_all.10 = bf16[16,576,128]{2,1,0:T(8,128)(2,1)S(1)} all-to-all(bf16[16,576,128]{2,1,0:T(8,128)(2,1)S(1)} %add_convert_fusion), channel_id=1, replica_groups=mesh['x'=4,'y'=4,'c'=2,'z'=8] {'x','y'}, dimensions={0} | all-to-all | bytes 4718592 | tf_op jit(solution)/shard_map/all_to_all | solution.py:271
  145.5 0.3 reduce_sum.31
  145.8 0.8 copy.27
  146.6 8.6 %all-to-all-start.1 = ((bf16[8,16,576]{2,1,0:T(8,128)(2,1)}), bf16[8,16,576]{2,1,0:T(8,128)(2,1)S(1)}, u32[]{:S(2)}, u32[]{:S(2)}) async-start(bf16[8,16,576]{2,1,0:T(8,128)(2,1)} %bitcast.19), calls=%async_computation.1 | async-start | bytes 327680 | tf_op jit(solution)/shard_map/all_to_all | solution.py:274
  155.2 2.1 %copy.26 = bf16[2,64,8,576]{3,2,1,0:T(8,128)(2,1)S(1)} copy(bf16[2,64,8,576]{3,1,2,0:T(8,128)(2,1)} %bitcast.44) | data formatting | bytes 2359296 | tf_op jit(solution)/shard_map/transpose | solution.py:263
  157.3 1.7 %reshape.35 = bf16[128,4608]{1,0:T(8,128)(2,1)} reshape(bf16[2,64,8,576]{3,2,1,0:T(8,128)(2,1)S(1)} %copy.26) | data formatting | bytes 2359296 | tf_op jit(solution)/shard_map/reshape | solution.py:264
  159.0 4.2 %all-to-all-done.1 = bf16[8,16,576]{2,1,0:T(8,128)(2,1)S(1)} async-done(((bf16[8,16,576]{2,1,0:T(8,128)(2,1)}), bf16[8,16,576]{2,1,0:T(8,128)(2,1)S(1)}, u32[]{:S(2)}, u32[]{:S(2)}) %all-to-all-start.1) | async-done | bytes 147488 | tf_op jit(solution)/shard_map/all_to_all | solution.py:274
  163.2 0.6 convert_reduce_fusion
  (5 shorter events, 0.0 us)
Async XLA Ops:
  0.6 8.4 %collective-permute-start.1 = (bf16[576,128]{1,0:T(8,128)(2,1)}, bf16[576,128]{1,0:T(8,128)(2,1)S(1)}, u32[]{:S(2)}, u32[]{:S(2)}) collective-permute-start(bf16[576,128]{1,0:T(8,128)(2,1)} %bitcast.48), channel_id=1, source_target_pairs={{0,32},{16,48},{32,0},{48,16},{1,33},{17,49},{33,1},{49,17},{2,34}... | collective-permute-start | bytes 442376 | tf_op jit(solution)/shard_map/ppermute | solution.py:227
  3.9 7.6 %collective-permute-start = (bf16[576,128]{1,0:T(8,128)(2,1)}, bf16[576,128]{1,0:T(8,128)(2,1)S(1)}, u32[]{:S(2)}, u32[]{:S(2)}) collective-permute-start(bf16[576,128]{1,0:T(8,128)(2,1)} %bitcast.49), channel_id=1, source_target_pairs={{0,48},{16,0},{32,16},{48,32},{1,49},{17,1},{33,17},{49,33},{2,50}... | collective-permute-start | bytes 442376 | tf_op jit(solution)/shard_map/ppermute | solution.py:227
  5.0 6.8 %collective-permute-start.2 = (bf16[576,128]{1,0:T(8,128)(2,1)}, bf16[576,128]{1,0:T(8,128)(2,1)S(1)}, u32[]{:S(2)}, u32[]{:S(2)}) collective-permute-start(bf16[576,128]{1,0:T(8,128)(2,1)} %bitcast.50), channel_id=1, source_target_pairs={{0,16},{16,32},{32,48},{48,0},{1,17},{17,33},{33,49},{49,1},{2,18}... | collective-permute-start | bytes 442376 | tf_op jit(solution)/shard_map/ppermute | solution.py:227
  13.6 31.5 %copy-start.2 = (bf16[128,4096]{1,0:T(8,128)(2,1)S(1)}, bf16[128,4096]{1,0:T(8,128)(2,1)}, u32[]{:S(2)}) copy-start(bf16[128,4096]{1,0:T(8,128)(2,1)} %param.7) | copy-start | bytes 3145732
  13.6 16.8 %collective-permute-start.8 = (bf16[4,576,128]{2,1,0:T(8,128)(2,1)}, bf16[4,576,128]{2,1,0:T(8,128)(2,1)}, u32[]{:S(2)}, u32[]{:S(2)}) collective-permute-start(bf16[4,576,128]{2,1,0:T(8,128)(2,1)} %pad_maximum_fusion.rest_0_), channel_id=1, source_target_pairs={{0,64},{64,128},{128,192},{192,0},{1,65},{65,129},{129,193},{193,1... | collective-permute-start | bytes 1769480 | tf_op jit(solution)/shard_map/ppermute | solution.py:227
  15.1 27.7 %collective-permute-start.6 = (bf16[4,576,128]{2,1,0:T(8,128)(2,1)}, bf16[4,576,128]{2,1,0:T(8,128)(2,1)}, u32[]{:S(2)}, u32[]{:S(2)}) collective-permute-start(bf16[4,576,128]{2,1,0:T(8,128)(2,1)} %pad_maximum_fusion.rest_0_), channel_id=1, source_target_pairs={{0,128},{64,192},{128,0},{192,64},{1,129},{65,193},{129,1},{193,65... | collective-permute-start | bytes 1769480 | tf_op jit(solution)/shard_map/ppermute | solution.py:227
  17.8 25.0 %collective-permute-start.4 = (bf16[4,576,128]{2,1,0:T(8,128)(2,1)}, bf16[4,576,128]{2,1,0:T(8,128)(2,1)}, u32[]{:S(2)}, u32[]{:S(2)}) collective-permute-start(bf16[4,576,128]{2,1,0:T(8,128)(2,1)} %pad_maximum_fusion.rest_0_), channel_id=1, source_target_pairs={{0,192},{64,0},{128,64},{192,128},{1,193},{65,1},{129,65},{193,129... | collective-permute-start | bytes 1769480 | tf_op jit(solution)/shard_map/ppermute | solution.py:227
  19.3 37.2 %collective-permute-start.3 = (bf16[4,576,128]{2,1,0:T(8,128)(2,1)}, bf16[4,576,128]{2,1,0:T(8,128)(2,1)}, u32[]{:S(2)}, u32[]{:S(2)}) collective-permute-start(bf16[4,576,128]{2,1,0:T(8,128)(2,1)} %pad_maximum_fusion.rest_0_), channel_id=1, source_target_pairs={{0,8},{8,0},{1,9},{9,1},{2,10},{10,2},{3,11},{11,3},{4,12},{12,4},... | collective-permute-start | bytes 1769480 | tf_op jit(solution)/shard_map/ppermute | solution.py:227
  30.4 26.1 %collective-permute-start.9 = (bf16[4,576,128]{2,1,0:T(8,128)(2,1)}, bf16[4,576,128]{2,1,0:T(8,128)(2,1)}, u32[]{:S(2)}, u32[]{:S(2)}) collective-permute-start(bf16[4,576,128]{2,1,0:T(8,128)(2,1)} %collective-permute-done.8.rest_6_), channel_id=1, source_target_pairs={{0,8},{8,0},{1,9},{9,1},{2,10},{10,2},{3,11},{11,3},{4,12},{12,4},... | collective-permute-start | bytes 1769480 | tf_op jit(solution)/shard_map/ppermute | solution.py:227
  42.8 13.7 %collective-permute-start.7 = (bf16[4,576,128]{2,1,0:T(8,128)(2,1)}, bf16[4,576,128]{2,1,0:T(8,128)(2,1)}, u32[]{:S(2)}, u32[]{:S(2)}) collective-permute-start(bf16[4,576,128]{2,1,0:T(8,128)(2,1)} %collective-permute-done.6.rest_4_), channel_id=1, source_target_pairs={{0,8},{8,0},{1,9},{9,1},{2,10},{10,2},{3,11},{11,3},{4,12},{12,4},... | collective-permute-start | bytes 1769480 | tf_op jit(solution)/shard_map/ppermute | solution.py:227
  42.8 13.7 %collective-permute-start.5 = (bf16[4,576,128]{2,1,0:T(8,128)(2,1)}, bf16[4,576,128]{2,1,0:T(8,128)(2,1)}, u32[]{:S(2)}, u32[]{:S(2)}) collective-permute-start(bf16[4,576,128]{2,1,0:T(8,128)(2,1)} %collective-permute-done.4.rest_2_), channel_id=1, source_target_pairs={{0,8},{8,0},{1,9},{9,1},{2,10},{10,2},{3,11},{11,3},{4,12},{12,4},... | collective-permute-start | bytes 1769480 | tf_op jit(solution)/shard_map/ppermute | solution.py:227
  46.0 1.4 copy-start.1
  52.3 3.1 %copy-start = (bf16[2,64,8,576]{3,1,2,0:T(8,128)(2,1)}, bf16[2,64,8,576]{3,1,2,0:T(8,128)(2,1)S(1)}, u32[]{:S(2)}) copy-start(bf16[2,64,8,576]{3,1,2,0:T(8,128)(2,1)S(1)} %copy.21) | copy-start | bytes 3538948
  100.5 4.8 %collective-permute-start.10 = (bf16[16,576,128]{2,1,0:T(8,128)(2,1)}, bf16[16,576,128]{2,1,0:T(8,128)(2,1)S(1)}, u32[]{:S(2)}, u32[]{:S(2)}) collective-permute-start(bf16[16,576,128]{2,1,0:T(8,128)(2,1)} %get-tuple-element.7), channel_id=1, source_target_pairs={{0,8},{8,0},{1,9},{9,1},{2,10},{10,2},{3,11},{11,3},{4,12},{12,4},... | collective-permute-start | bytes 7077896 | tf_op jit(solution)/shard_map/ppermute | solution.py:269
  146.6 16.5 %all-to-all-start.1 = ((bf16[8,16,576]{2,1,0:T(8,128)(2,1)}), bf16[8,16,576]{2,1,0:T(8,128)(2,1)S(1)}, u32[]{:S(2)}, u32[]{:S(2)}) async-start(bf16[8,16,576]{2,1,0:T(8,128)(2,1)} %bitcast.19), calls=%async_computation.1 | async-start | bytes 327680 | tf_op jit(solution)/shard_map/all_to_all | solution.py:274

commit v2 on v1

--- a/solution.py
+++ b/solution.py
@@ -11,6 +11,7 @@
 LATENT = 512
 ROPE = 64
 WIDTH = LATENT + ROPE
+HALF = WIDTH // 2
 GROUP = 64
 BLOCK = 256
 PAIR = 2 * GROUP
@@ -31,11 +32,12 @@
 
 
 def grad_kernel(
-    order, place, q_rows, q_cols, g_rows, g_cols, deltas, *rest, pieces, piece_y, sides, rows
+    order, place, q_rows, q_cols, g_rows, g_cols, deltas, *rest, sides, rows
 ):
+    pieces = 4 * sides
     piece_refs = rest[:pieces]
-    dq_out, keep_out, send_out = rest[pieces : pieces + 3]
-    stage, keys, scores, top, total, dq_acc, dk_acc, slot_of, sem = rest[pieces + 3 :]
+    dq_out, keep_a, keep_b, send_a, send_b = rest[pieces : pieces + 5]
+    stage, keys, scores, top, total, dq_acc, dk_acc, slot_of, sem = rest[pieces + 5 :]
     pairs = stage.shape[0]
     groups = 2 * pairs
     blocks = groups * GROUP // BLOCK
@@ -46,14 +48,18 @@
 
     copies = []
     for at, ref in enumerate(piece_refs):
-        step_x, step_c = at // 2, at % 2
-        for step_y in range(piece_y):
+        part, rest_at = at // (2 * sides), at % (2 * sides)
+        first, step_c = rest_at // 2, rest_at % 2
+        for second in range(sides):
+            step_x, step_y = (first, second) if part == 0 else (second, first)
             at_x = lax.rem(my_x + step_x, sides)
             at_y = lax.rem(my_y + step_y, sides)
             at_c = lax.rem(my_c + step_c, 2)
             pair = (at_x * sides + at_y) * 2 + at_c
             copy = pltpu.make_async_copy(
-                ref.at[step_y], stage.at[pair], sem.at[at * piece_y + step_y]
+                ref.at[second],
+                stage.at[pair, pl.ds(part * HALF, HALF)],
+                sem.at[at * sides + second],
             )
             copy.start()
             copies.append(copy)
@@ -159,17 +165,21 @@
         high_tile = dk_acc[:, pl.ds(high_at, PAIR)]
         odd = lax.rem(group, 2) == 1
         mine = lax.rem(p, 2) == my_c
+        step_x = lax.rem(lax.div(p, 2 * sides) - my_x + sides, sides)
+        step_y = lax.rem(lax.rem(lax.div(p, 2), sides) - my_y + sides, sides)
 
         def put(tile):
             tile = tile.astype(jnp.bfloat16)
 
             @pl.when(mine)
             def _():
-                keep_out[lax.div(p, 2)] = tile
+                keep_a[step_x, step_y] = tile[:HALF]
+                keep_b[step_y, step_x] = tile[HALF:]
 
             @pl.when(jnp.logical_not(mine))
             def _():
-                send_out[lax.div(p, 2)] = tile
+                send_a[step_x, step_y] = tile[:HALF]
+                send_b[step_y, step_x] = tile[HALF:]
 
         @pl.when(odd)
         def _():
@@ -187,23 +197,16 @@
 
 def run_grads(order, place, q_rows, q_cols, g_rows, g_cols, deltas, pieces, sides):
     rows = q_rows.shape[0] // 2
-    piece_y = pieces[0].shape[0]
-    pairs = len(pieces) * piece_y
+    pairs = 2 * sides * sides
     items = pairs * PAIR // BLOCK + 1
     vmem = pl.BlockSpec(memory_space=pltpu.VMEM)
     smem = pl.BlockSpec(memory_space=pltpu.SMEM)
-    half = pairs // 2
+    part = jax.ShapeDtypeStruct((sides, sides, HALF, PAIR), jnp.bfloat16)
     return pl.pallas_call(
-        functools.partial(
-            grad_kernel, pieces=len(pieces), piece_y=piece_y, sides=sides, rows=rows
-        ),
-        out_shape=(
-            jax.ShapeDtypeStruct((2 * rows, WIDTH), jnp.bfloat16),
-            jax.ShapeDtypeStruct((half, WIDTH, PAIR), jnp.bfloat16),
-            jax.ShapeDtypeStruct((half, WIDTH, PAIR), jnp.bfloat16),
-        ),
+        functools.partial(grad_kernel, sides=sides, rows=rows),
+        out_shape=(jax.ShapeDtypeStruct((2 * rows, WIDTH), jnp.bfloat16), part, part, part, part),
         in_specs=[smem, smem] + [vmem] * 5 + [pl.BlockSpec(memory_space=pl.ANY)] * len(pieces),
-        out_specs=(vmem, vmem, vmem),
+        out_specs=(vmem,) * 5,
         scratch_shapes=[
             pltpu.VMEM((pairs, WIDTH, PAIR), jnp.bfloat16),
             pltpu.VMEM((WIDTH, pairs * PAIR), jnp.bfloat16),
@@ -213,7 +216,7 @@
             pltpu.VMEM((2 * rows, WIDTH), jnp.float32),
             pltpu.VMEM((WIDTH, pairs * PAIR), jnp.float32),
             pltpu.SMEM((2 * pairs,), jnp.int32),
-            pltpu.SemaphoreType.DMA((pairs,)),
+            pltpu.SemaphoreType.DMA((2 * pairs,)),
         ],
         compiler_params=pltpu.CompilerParams(vmem_limit_bytes=60 * 1024 * 1024),
         cost_estimate=pl.CostEstimate(
@@ -239,12 +242,12 @@
     heads = q_latent.shape[1] // WIDTH
     place = jnp.stack([lax.axis_index("x"), lax.axis_index("y"), lax.axis_index("c")]).astype(jnp.int32)
 
+    def spread(a, axis):
+        return [a] + [shift(a, axis, sides, d) for d in range(1, sides)]
+
     own = kv_latent.T
-    along_y = jnp.stack([own] + [shift(own, "y", sides, d) for d in range(1, sides)])
-    along_x = [along_y] + [shift(along_y, "x", sides, d) for d in range(1, sides)]
-    pieces = []
-    for piece in along_x:
-        pieces += [piece, shift(piece, "c", 2, 1)]
+    part_a = spread(jnp.stack(spread(own[:HALF], "y")), "x")
+    part_b = spread(jnp.stack(spread(own[HALF:], "x")), "y")
 
     q_rows = head_rows(q_latent, WIDTH)
     g_rows = head_rows(out_grad, LATENT)
@@ -256,23 +259,33 @@
     )
     delta = delta.transpose(0, 2, 1).reshape(tokens * heads, 1)
     deltas = jnp.broadcast_to(delta, (tokens * heads, 128))
-
-    dq, keep, send = run_grads(
-        group_order, place, q_rows, q_rows.T, g_rows, g_rows.T, deltas, pieces, sides
-    )
+    local = (q_rows, q_rows.T, g_rows, g_rows.T, deltas)
+    arrived, local = lax.optimization_barrier((part_a[1:] + part_b[1:], local))
+    pieces = []
+    for piece in [part_a[0]] + arrived[: sides - 1] + [part_b[0]] + arrived[sides - 1 :]:
+        pieces += [piece, shift(piece, "c", 2, 1)]
+
+    dq, keep_a, keep_b, send_a, send_b = run_grads(group_order, place, *local, pieces, sides)
     q_grad = dq.reshape(2, heads, tokens // 2, WIDTH).transpose(0, 2, 1, 3)
     q_grad = q_grad.reshape(tokens, heads * WIDTH)
 
-    def added(parts):
-        return jnp.sum(parts.astype(jnp.float32), axis=0)
-
-    received = lax.ppermute(send, "c", [(0, 1), (1, 0)])
-    both = (keep.astype(jnp.float32) + received.astype(jnp.float32)).astype(jnp.bfloat16)
-    parts = lax.all_to_all(both, ("x", "y"), 0, 0, tiled=True)
-    summed = added(parts)
+    def reduce_to_owner(keep, send, axes):
+        received = shift(send, "c", 2, 1)
+        total = keep.astype(jnp.float32) + received.astype(jnp.float32)
+        for axis in axes:
+            low = total.astype(jnp.bfloat16)
+            moved = [shift(low[d], axis, sides, -d) for d in range(1, sides)]
+            total = total[0]
+            for part in moved:
+                total = total + part.astype(jnp.float32)
+        return total
+
+    summed = jnp.concatenate(
+        [reduce_to_owner(keep_a, send_a, ("x", "y")), reduce_to_owner(keep_b, send_b, ("y", "x"))]
+    )
     by_head = summed.reshape(WIDTH, depth, PAIR // depth).transpose(1, 2, 0)
     parts = lax.all_to_all(by_head.astype(jnp.bfloat16), "z", 0, 0, tiled=True)
-    return q_grad, added(parts)
+    return q_grad, jnp.sum(parts.astype(jnp.float32), axis=0)
 
 
 def solution(mesh):

time: 164 us -> 152 us (0.927)
  blocking collectives: 37.9 us -> 0 us
  starting transfers between devices: 20.1 us -> 46.9 us
  waiting for transfers between devices: 38.4 us -> 36.1 us
    all_to_all x1 -> x0, blocking collectives: 37.9 us -> none  [shards(): parts = lax.all_to_all(both, ('x', 'y'), 0, 0, tiled=True)]
    ppermute x10 -> x34, starting transfers between devices: 11.5 us -> 38.4 us  [shift(): return lax.ppermute(a, axis, [(i, (i - step) % size) for i in range(size)])]
    ppermute x1 -> x0, waiting for transfers between devices: 4.73 us -> none  [shards(): received = lax.ppermute(send, 'c', [(0, 1), (1, 0)])]
    add x0 -> x2, other arithmetic: none -> 2.09 us  [reduce_to_owner(): total = keep.astype(jnp.float32) + received.astype(jnp.float32)]
    convert_element_type x1 -> x2, other arithmetic: 2.28 us -> 0.3 us  [reduce_to_owner(): low = total.astype(jnp.bfloat16)]
    ppermute x10 -> x34, waiting for transfers between devices: 29.4 us -> 30.6 us  [shift(): return lax.ppermute(a, axis, [(i, (i - step) % size) for i in range(size)])]
  transfers between devices with their start and end apart: 12 -> 35, of which waited for: 7 -> 12; matrix products, arithmetic and copies ran while one was open for 10% -> 14% of each run, Pallas kernels for 0% -> 0%
where the time goes in v2:
time: 152 us; the launch traced here: 151 us
  starting transfers between devices  46.9 us (31%)
  Pallas kernels  43.1 us (28%)
  waiting for transfers between devices  36.1 us (24%)
  local copies, waits for them, and re-layouts  16.8 us (11%)
  other arithmetic  7.24 us (5%)
    pallas_call x1, Pallas kernels, run_grads(): pl.pallas_call(functools.partial(grad_kernel, sides=sides, rows=rows), ou...  43.1 us
    ppermute x34, starting transfers between devices, shift(): return lax.ppermute(a, axis, [(i, (i - step) % size) for i in range(size)])  38.4 us
    ppermute x34, waiting for transfers between devices, shift(): return lax.ppermute(a, axis, [(i, (i - step) % size) for i in range(size)])  30.6 us
    all_to_all x1, starting transfers between devices, shards(): parts = lax.all_to_all(by_head.astype(jnp.bfloat16), 'z', 0, 0, tiled=True)  8.57 us
    all_to_all x1, waiting for transfers between devices, shards(): parts = lax.all_to_all(by_head.astype(jnp.bfloat16), 'z', 0, 0, tiled=True)  5.51 us
    reshape x2, local copies, waits for them, and re-layouts, head_rows(): a = a.reshape(2, tokens // 2, heads, width).transpose(0, 2, 1, 3)  4.96 us
    unnamed x32, local copies, waits for them, and re-layouts  3.05 us
  transfers between devices with their start and end apart: 35, of which 12 were waited for; matrix products, arithmetic and copies ran while one was open for 14% of the time, Pallas kernels for 0%

profile of v2, /device:TPU:32, one launch (start us, length us, event | category | flops | bytes accessed | tf_op | source)
XLA Modules:
  0.0 151.2 jit_solution(12639856249705273616)
XLA Ops:
  0.6 1.0 slice_bitcast_fusion.16
  1.6 3.3 %collective-permute-start.1 = (bf16[288,128]{1,0:T(8,128)(2,1)S(1)}, bf16[288,128]{1,0:T(8,128)(2,1)S(1)}, u32[]{:S(2)}, u32[]{:S(2)}) collective-permute-start(bf16[288,128]{1,0:T(8,128)(2,1)S(1)} %get-tuple-element.57), channel_id=1, source_target_pairs={{0,32},{16,48},{32,0},{48,16},{1,33},{17,49},{33,1},{49,17},{2,34}... | collective-permute-start | bytes 221192 | tf_op jit(solution)/shard_map/ppermute | solution.py:230
  4.9 1.1 collective-permute-start
  5.9 1.0 collective-permute-start.2
  6.9 3.0 %collective-permute-start.7 = (bf16[288,128]{1,0:T(8,128)(2,1)S(1)}, bf16[288,128]{1,0:T(8,128)(2,1)S(1)}, u32[]{:S(2)}, u32[]{:S(2)}) collective-permute-start(bf16[288,128]{1,0:T(8,128)(2,1)S(1)} %get-tuple-element.56), channel_id=1, source_target_pairs={{0,128},{64,192},{128,0},{192,64},{1,129},{65,193},{129,1},{193,65... | collective-permute-start | bytes 221192 | tf_op jit(solution)/shard_map/ppermute | solution.py:230
  9.9 1.1 collective-permute-start.6
  11.1 0.9 collective-permute-start.8
  12.0 0.8 pad_maximum_fusion.rest_0_
  12.7 1.0 collective-permute-start.5
  13.7 1.8 %convert_multiply_fusion = f32[128,4096]{1,0:T(8,128)S(1)} fusion(bf16[128,4096]{1,0:T(8,128)(2,1)} %param.8, bf16[128,4096]{1,0:T(8,128)(2,1)} %param.7), kind=kLoop, calls=%fused_computation.3 | loop fusion | flops 1572864 | bytes 4194304 | tf_op jit(solution)/shard_map/mul | solution.py:255
  16.0 2.9 %collective-permute-start.4 = (bf16[4,288,128]{2,1,0:T(8,128)(2,1)}, bf16[4,288,128]{2,1,0:T(8,128)(2,1)}, u32[]{:S(2)}, u32[]{:S(2)}) collective-permute-start(bf16[4,288,128]{2,1,0:T(8,128)(2,1)} %pad_maximum_fusion.rest_0_), channel_id=1, source_target_pairs={{0,128},{64,192},{128,0},{192,64},{1,129},{65,193},{129,1},{193,65... | collective-permute-start | bytes 884744 | tf_op jit(solution)/shard_map/ppermute | solution.py:230
  18.8 1.4 collective-permute-start.3
  20.2 0.7 pad_maximum_fusion.1.rest_8_
  21.0 2.5 %collective-permute-start.10 = (bf16[4,288,128]{2,1,0:T(8,128)(2,1)}, bf16[4,288,128]{2,1,0:T(8,128)(2,1)}, u32[]{:S(2)}, u32[]{:S(2)}) collective-permute-start(bf16[4,288,128]{2,1,0:T(8,128)(2,1)} %pad_maximum_fusion.1.rest_8_), channel_id=1, source_target_pairs={{0,32},{16,48},{32,0},{48,16},{1,33},{17,49},{33,1},{49,17},{2,34}... | collective-permute-start | bytes 884744 | tf_op jit(solution)/shard_map/ppermute | solution.py:230
  23.4 4.9 %collective-permute-done.5.rest_6_ = bf16[4,288,128]{2,1,0:T(8,128)(2,1)S(1)} collective-permute-done((bf16[4,288,128]{2,1,0:T(8,128)(2,1)}, bf16[4,288,128]{2,1,0:T(8,128)(2,1)S(1)}, u32[]{:S(2)}, u32[]{:S(2)}) %collective-permute-start.5) | collective-permute-done | bytes 294944 | tf_op jit(solution)/shard_map/ppermute | solution.py:230
  28.3 2.3 %collective-permute-start.9 = (bf16[4,288,128]{2,1,0:T(8,128)(2,1)}, bf16[4,288,128]{2,1,0:T(8,128)(2,1)}, u32[]{:S(2)}, u32[]{:S(2)}) collective-permute-start(bf16[4,288,128]{2,1,0:T(8,128)(2,1)} %pad_maximum_fusion.1.rest_8_), channel_id=1, source_target_pairs={{0,48},{16,0},{32,16},{48,32},{1,49},{17,1},{33,17},{49,33},{2,50}... | collective-permute-start | bytes 884744 | tf_op jit(solution)/shard_map/ppermute | solution.py:230
  31.0 1.4 copy.26
  32.4 3.4 %reshape.29 = bf16[2,64,8,576]{3,2,1,0:T(8,128)(2,1)} reshape(bf16[128,4608]{1,0:T(8,128)(2,1)} %param.5) | data formatting | bytes 2359296 | tf_op jit(solution)/shard_map/reshape | solution.py:236
  35.8 1.5 %copy.23 = bf16[2,64,8,576]{3,1,2,0:T(8,128)(2,1)S(1)} copy(bf16[2,64,8,576]{3,2,1,0:T(8,128)(2,1)} %reshape.29) | data formatting | bytes 2359296 | tf_op jit(solution)/shard_map/reshape | solution.py:236
  37.4 1.5 %copy.24 = bf16[1024,576]{0,1:T(8,128)(2,1)} copy(bf16[1024,576]{1,0:T(8,128)(2,1)S(1)} %bitcast.105) | data formatting | bytes 2359296 | tf_op jit(solution)/shard_map/reshape | solution.py:237
  38.9 1.6 %copy.31 = f32[16,8,8,512]{3,2,1,0:T(8,128)S(1)} copy(f32[16,8,8,512]{3,1,2,0:T(8,128)S(1)} %bitcast.103) | data formatting | bytes 4194304
  40.9 0.5 collective-permute-start.16
  41.4 1.0 broadcast_in_dim.8.deltas
  43.6 0.7 collective-permute-done.13.rest_3_
  44.4 0.6 pad_add_fusion.place
  45.5 0.4 collective-permute-done.18.rest_13_
  45.9 0.4 collective-permute-done.19.rest_15_
  46.7 0.7 copy-done.14
  47.4 43.1 %latent_grads.1 = (bf16[1024,576]{1,0:T(8,128)(2,1)}, bf16[4,4,288,128]{3,2,1,0:T(8,128)(2,1)}, bf16[4,4,288,128]{3,2,1,0:T(8,128)(2,1)}, bf16[4,4,288,128]{3,2,1,0:T(8,128)(2,1)}, bf16[4,4,288,128]{3,2,1,0:T(8,128)(2,1)}) custom-call(s32[64]{0:T(128)} %order.1, s32[3]{0:T(128)} %pad_add_fusion.place, bf16[1024,576]{1,0:T(8,128)(2,1)} %bitcast.106, ...), custom_call_target="tpu_custom_call" | custom-call | flops 12264144896 | bytes 25165824 | tf_op jit(solution)/shard_map/latent_grads/pallas_call | solution.py:205
  91.2 2.4 %collective-permute-done.20 = bf16[4,4,288,128]{3,2,1,0:T(8,128)(2,1)S(1)} collective-permute-done((bf16[4,4,288,128]{3,2,1,0:T(8,128)(2,1)}, bf16[4,4,288,128]{3,2,1,0:T(8,128)(2,1)S(1)}, u32[]{:S(2)}, u32[]{:S(2)}) %collective-permute-start.20) | collective-permute-done | bytes 1179680 | tf_op jit(solution)/shard_map/ppermute | solution.py:230
  93.6 1.7 %convert_add_fusion.1 = (f32[4,4,288,128]{3,2,1,0:T(8,128)S(1)}, bf16[4,4,288,128]{3,2,1,0:T(8,128)(2,1)S(1)}) fusion(bf16[4,4,288,128]{3,2,1,0:T(8,128)(2,1)S(1)} %collective-permute-done.20, bf16[4,4,288,128]{3,2,1,0:T(8,128)(2,1)} %get-tuple-element.30), kind=kLoop, calls=%fused_computation.1 | loop fusion | flops 2359296 | bytes 5898240 | tf_op jit(solution)/shard_map/add | solution.py:274
  95.5 3.2 %collective-permute-start.23 = (bf16[4,288,128]{2,1,0:T(8,128)(2,1)S(1)}, bf16[4,288,128]{2,1,0:T(8,128)(2,1)S(1)}, u32[]{:S(2)}, u32[]{:S(2)}) collective-permute-start(bf16[4,288,128]{2,1,0:T(8,128)(2,1)S(1)} %get-tuple-element.43), channel_id=1, source_target_pairs={{0,192},{64,0},{128,64},{192,128},{1,193},{65,1},{129,65},{193,129... | collective-permute-start | bytes 884744 | tf_op jit(solution)/shard_map/ppermute | solution.py:230
  99.3 3.2 %collective-permute-start.30 = (bf16[4,288,128]{2,1,0:T(8,128)(2,1)S(1)}, bf16[4,288,128]{2,1,0:T(8,128)(2,1)S(1)}, u32[]{:S(2)}, u32[]{:S(2)}) collective-permute-start(bf16[4,288,128]{2,1,0:T(8,128)(2,1)S(1)} %get-tuple-element.46), channel_id=1, source_target_pairs={{0,48},{16,0},{32,16},{48,32},{1,49},{17,1},{33,17},{49,33},{2,50}... | collective-permute-start | bytes 884744 | tf_op jit(solution)/shard_map/ppermute | solution.py:230
  102.5 9.7 %collective-permute-done.21 = bf16[4,288,128]{2,1,0:T(8,128)(2,1)S(1)} collective-permute-done((bf16[4,288,128]{2,1,0:T(8,128)(2,1)S(1)}, bf16[4,288,128]{2,1,0:T(8,128)(2,1)S(1)}, u32[]{:S(2)}, u32[]{:S(2)}) %collective-permute-start.21) | collective-permute-done | bytes 294944 | tf_op jit(solution)/shard_map/ppermute | solution.py:230
  112.2 0.5 collective-permute-start.29
  112.8 0.6 collective-permute-start.24
  113.5 2.7 %collective-permute-start.26 = (bf16[288,128]{1,0:T(8,128)(2,1)S(1)}, bf16[288,128]{1,0:T(8,128)(2,1)S(1)}, u32[]{:S(2)}, u32[]{:S(2)}) collective-permute-start(bf16[288,128]{1,0:T(8,128)(2,1)S(1)} %get-tuple-element.49), channel_id=1, source_target_pairs={{0,48},{16,0},{32,16},{48,32},{1,49},{17,1},{33,17},{49,33},{2,50}... | collective-permute-start | bytes 221192 | tf_op jit(solution)/shard_map/ppermute | solution.py:230
  116.1 1.9 %collective-permute-start.25 = (bf16[288,128]{1,0:T(8,128)(2,1)S(1)}, bf16[288,128]{1,0:T(8,128)(2,1)S(1)}, u32[]{:S(2)}, u32[]{:S(2)}) collective-permute-start(bf16[288,128]{1,0:T(8,128)(2,1)S(1)} %get-tuple-element.50), channel_id=1, source_target_pairs={{0,32},{16,48},{32,0},{48,16},{1,33},{17,49},{33,1},{49,17},{2,34}... | collective-permute-start | bytes 221192 | tf_op jit(solution)/shard_map/ppermute | solution.py:230
  118.0 5.7 %collective-permute-done.29 = bf16[4,288,128]{2,1,0:T(8,128)(2,1)S(1)} collective-permute-done((bf16[4,288,128]{2,1,0:T(8,128)(2,1)S(1)}, bf16[4,288,128]{2,1,0:T(8,128)(2,1)S(1)}, u32[]{:S(2)}, u32[]{:S(2)}) %collective-permute-start.29) | collective-permute-done | bytes 294944 | tf_op jit(solution)/shard_map/ppermute | solution.py:230
  124.0 3.2 %collective-permute-start.33 = (bf16[288,128]{1,0:T(8,128)(2,1)S(1)}, bf16[288,128]{1,0:T(8,128)(2,1)S(1)}, u32[]{:S(2)}, u32[]{:S(2)}) collective-permute-start(bf16[288,128]{1,0:T(8,128)(2,1)S(1)} %get-tuple-element.52), channel_id=1, source_target_pairs={{0,192},{64,0},{128,64},{192,128},{1,193},{65,1},{129,65},{193,129... | collective-permute-start | bytes 221192 | tf_op jit(solution)/shard_map/ppermute | solution.py:230
  127.3 2.8 %collective-permute-done.31 = bf16[288,128]{1,0:T(8,128)(2,1)S(1)} collective-permute-done((bf16[288,128]{1,0:T(8,128)(2,1)S(1)}, bf16[288,128]{1,0:T(8,128)(2,1)S(1)}, u32[]{:S(2)}, u32[]{:S(2)}) %collective-permute-start.31) | collective-permute-done | bytes 73760 | tf_op jit(solution)/shard_map/ppermute | solution.py:230
  130.2 2.9 %collective-permute-done.32 = bf16[288,128]{1,0:T(8,128)(2,1)S(1)} collective-permute-done((bf16[288,128]{1,0:T(8,128)(2,1)S(1)}, bf16[288,128]{1,0:T(8,128)(2,1)S(1)}, u32[]{:S(2)}, u32[]{:S(2)}) %collective-permute-start.32) | collective-permute-done | bytes 73760 | tf_op jit(solution)/shard_map/ppermute | solution.py:230
  133.2 0.8 copy.29
  134.0 8.6 %all-to-all-start = ((bf16[8,16,576]{2,1,0:T(8,128)(2,1)}), bf16[8,16,576]{2,1,0:T(8,128)(2,1)S(1)}, u32[]{:S(2)}, u32[]{:S(2)}) async-start(bf16[8,16,576]{2,1,0:T(8,128)(2,1)} %bitcast.39), calls=%async_computation | async-start | bytes 327680 | tf_op jit(solution)/shard_map/all_to_all | solution.py:287
  142.6 0.7 copy.28
  143.3 1.7 %reshape.35 = bf16[128,4608]{1,0:T(8,128)(2,1)} reshape(bf16[2,64,8,576]{3,2,1,0:T(8,128)(2,1)S(1)} %copy.28) | data formatting | bytes 2359296 | tf_op jit(solution)/shard_map/reshape | solution.py:270
  145.0 5.5 %all-to-all-done = bf16[8,16,576]{2,1,0:T(8,128)(2,1)S(1)} async-done(((bf16[8,16,576]{2,1,0:T(8,128)(2,1)}), bf16[8,16,576]{2,1,0:T(8,128)(2,1)S(1)}, u32[]{:S(2)}, u32[]{:S(2)}) %all-to-all-start) | async-done | bytes 147488 | tf_op jit(solution)/shard_map/all_to_all | solution.py:287
  150.5 0.6 convert_reduce_fusion
  (85 shorter events, 5.2 us)
Async XLA Ops:
  1.6 9.5 %collective-permute-start.1 = (bf16[288,128]{1,0:T(8,128)(2,1)S(1)}, bf16[288,128]{1,0:T(8,128)(2,1)S(1)}, u32[]{:S(2)}, u32[]{:S(2)}) collective-permute-start(bf16[288,128]{1,0:T(8,128)(2,1)S(1)} %get-tuple-element.57), channel_id=1, source_target_pairs={{0,32},{16,48},{32,0},{48,16},{1,33},{17,49},{33,1},{49,17},{2,34}... | collective-permute-start | bytes 221192 | tf_op jit(solution)/shard_map/ppermute | solution.py:230
  4.9 7.1 %collective-permute-start = (bf16[288,128]{1,0:T(8,128)(2,1)S(1)}, bf16[288,128]{1,0:T(8,128)(2,1)S(1)}, u32[]{:S(2)}, u32[]{:S(2)}) collective-permute-start(bf16[288,128]{1,0:T(8,128)(2,1)S(1)} %get-tuple-element.57), channel_id=1, source_target_pairs={{0,48},{16,0},{32,16},{48,32},{1,49},{17,1},{33,17},{49,33},{2,50}... | collective-permute-start | bytes 221192 | tf_op jit(solution)/shard_map/ppermute | solution.py:230
  5.9 6.0 %collective-permute-start.2 = (bf16[288,128]{1,0:T(8,128)(2,1)S(1)}, bf16[288,128]{1,0:T(8,128)(2,1)S(1)}, u32[]{:S(2)}, u32[]{:S(2)}) collective-permute-start(bf16[288,128]{1,0:T(8,128)(2,1)S(1)} %get-tuple-element.57), channel_id=1, source_target_pairs={{0,16},{16,32},{32,48},{48,0},{1,17},{17,33},{33,49},{49,1},{2,18}... | collective-permute-start | bytes 221192 | tf_op jit(solution)/shard_map/ppermute | solution.py:230
  6.9 11.9 %collective-permute-start.7 = (bf16[288,128]{1,0:T(8,128)(2,1)S(1)}, bf16[288,128]{1,0:T(8,128)(2,1)S(1)}, u32[]{:S(2)}, u32[]{:S(2)}) collective-permute-start(bf16[288,128]{1,0:T(8,128)(2,1)S(1)} %get-tuple-element.56), channel_id=1, source_target_pairs={{0,128},{64,192},{128,0},{192,64},{1,129},{65,193},{129,1},{193,65... | collective-permute-start | bytes 221192 | tf_op jit(solution)/shard_map/ppermute | solution.py:230
  9.9 10.3 %collective-permute-start.6 = (bf16[288,128]{1,0:T(8,128)(2,1)S(1)}, bf16[288,128]{1,0:T(8,128)(2,1)S(1)}, u32[]{:S(2)}, u32[]{:S(2)}) collective-permute-start(bf16[288,128]{1,0:T(8,128)(2,1)S(1)} %get-tuple-element.56), channel_id=1, source_target_pairs={{0,192},{64,0},{128,64},{192,128},{1,193},{65,1},{129,65},{193,129... | collective-permute-start | bytes 221192 | tf_op jit(solution)/shard_map/ppermute | solution.py:230
  11.1 9.2 %collective-permute-start.8 = (bf16[288,128]{1,0:T(8,128)(2,1)S(1)}, bf16[288,128]{1,0:T(8,128)(2,1)S(1)}, u32[]{:S(2)}, u32[]{:S(2)}) collective-permute-start(bf16[288,128]{1,0:T(8,128)(2,1)S(1)} %get-tuple-element.56), channel_id=1, source_target_pairs={{0,64},{64,128},{128,192},{192,0},{1,65},{65,129},{129,193},{193,1... | collective-permute-start | bytes 221192 | tf_op jit(solution)/shard_map/ppermute | solution.py:230
  12.7 2.8 %copy-start.2 = (bf16[128,4096]{1,0:T(8,128)(2,1)S(1)}, bf16[128,4096]{1,0:T(8,128)(2,1)}, u32[]{:S(2)}) copy-start(bf16[128,4096]{1,0:T(8,128)(2,1)} %param.7) | copy-start | bytes 3145732
  12.7 15.6 %collective-permute-start.5 = (bf16[4,288,128]{2,1,0:T(8,128)(2,1)}, bf16[4,288,128]{2,1,0:T(8,128)(2,1)S(1)}, u32[]{:S(2)}, u32[]{:S(2)}) collective-permute-start(bf16[4,288,128]{2,1,0:T(8,128)(2,1)} %pad_maximum_fusion.rest_0_), channel_id=1, source_target_pairs={{0,64},{64,128},{128,192},{192,0},{1,65},{65,129},{129,193},{193,1... | collective-permute-start | bytes 884744 | tf_op jit(solution)/shard_map/ppermute | solution.py:230
  16.0 24.9 %collective-permute-start.4 = (bf16[4,288,128]{2,1,0:T(8,128)(2,1)}, bf16[4,288,128]{2,1,0:T(8,128)(2,1)}, u32[]{:S(2)}, u32[]{:S(2)}) collective-permute-start(bf16[4,288,128]{2,1,0:T(8,128)(2,1)} %pad_maximum_fusion.rest_0_), channel_id=1, source_target_pairs={{0,128},{64,192},{128,0},{192,64},{1,129},{65,193},{129,1},{193,65... | collective-permute-start | bytes 884744 | tf_op jit(solution)/shard_map/ppermute | solution.py:230
  18.8 22.1 %collective-permute-start.3 = (bf16[4,288,128]{2,1,0:T(8,128)(2,1)}, bf16[4,288,128]{2,1,0:T(8,128)(2,1)}, u32[]{:S(2)}, u32[]{:S(2)}) collective-permute-start(bf16[4,288,128]{2,1,0:T(8,128)(2,1)} %pad_maximum_fusion.rest_0_), channel_id=1, source_target_pairs={{0,192},{64,0},{128,64},{192,128},{1,193},{65,1},{129,65},{193,129... | collective-permute-start | bytes 884744 | tf_op jit(solution)/shard_map/ppermute | solution.py:230
  21.0 20.5 %collective-permute-start.11 = (bf16[4,288,128]{2,1,0:T(8,128)(2,1)}, bf16[4,288,128]{2,1,0:T(8,128)(2,1)}, u32[]{:S(2)}, u32[]{:S(2)}) collective-permute-start(bf16[4,288,128]{2,1,0:T(8,128)(2,1)} %pad_maximum_fusion.1.rest_8_), channel_id=1, source_target_pairs={{0,16},{16,32},{32,48},{48,0},{1,17},{17,33},{33,49},{49,1},{2,18}... | collective-permute-start | bytes 884744 | tf_op jit(solution)/shard_map/ppermute | solution.py:230
  21.0 20.5 %collective-permute-start.10 = (bf16[4,288,128]{2,1,0:T(8,128)(2,1)}, bf16[4,288,128]{2,1,0:T(8,128)(2,1)}, u32[]{:S(2)}, u32[]{:S(2)}) collective-permute-start(bf16[4,288,128]{2,1,0:T(8,128)(2,1)} %pad_maximum_fusion.1.rest_8_), channel_id=1, source_target_pairs={{0,32},{16,48},{32,0},{48,16},{1,33},{17,49},{33,1},{49,17},{2,34}... | collective-permute-start | bytes 884744 | tf_op jit(solution)/shard_map/ppermute | solution.py:230
  28.3 2.7 %copy-start.5 = (bf16[4,288,128]{2,1,0:T(8,128)(2,1)}, bf16[4,288,128]{2,1,0:T(8,128)(2,1)S(1)}, u32[]{:S(2)}) copy-start(bf16[4,288,128]{2,1,0:T(8,128)(2,1)S(1)} %collective-permute-done.5.rest_6_) | copy-start | bytes 884740
  28.3 13.1 %collective-permute-start.9 = (bf16[4,288,128]{2,1,0:T(8,128)(2,1)}, bf16[4,288,128]{2,1,0:T(8,128)(2,1)}, u32[]{:S(2)}, u32[]{:S(2)}) collective-permute-start(bf16[4,288,128]{2,1,0:T(8,128)(2,1)} %pad_maximum_fusion.1.rest_8_), channel_id=1, source_target_pairs={{0,48},{16,0},{32,16},{48,32},{1,49},{17,1},{33,17},{49,33},{2,50}... | collective-permute-start | bytes 884744 | tf_op jit(solution)/shard_map/ppermute | solution.py:230
  31.0 1.4 copy-start.1
  37.4 3.2 %copy-start = (bf16[2,64,8,576]{3,1,2,0:T(8,128)(2,1)}, bf16[2,64,8,576]{3,1,2,0:T(8,128)(2,1)S(1)}, u32[]{:S(2)}) copy-start(bf16[2,64,8,576]{3,1,2,0:T(8,128)(2,1)S(1)} %copy.23) | copy-start | bytes 3538948
  40.5 2.4 %copy-start.6 = (bf16[4,288,128]{2,1,0:T(8,128)(2,1)S(1)}, bf16[4,288,128]{2,1,0:T(8,128)(2,1)}, u32[]{:S(2)}) copy-start(bf16[4,288,128]{2,1,0:T(8,128)(2,1)} %copy-done.5) | copy-start | bytes 884740
  40.9 2.2 %collective-permute-start.12 = (bf16[4,288,128]{2,1,0:T(8,128)(2,1)}, bf16[4,288,128]{2,1,0:T(8,128)(2,1)S(1)}, u32[]{:S(2)}, u32[]{:S(2)}) collective-permute-start(bf16[4,288,128]{2,1,0:T(8,128)(2,1)} %pad_maximum_fusion.rest_0_), channel_id=1, source_target_pairs={{0,8},{8,0},{1,9},{9,1},{2,10},{10,2},{3,11},{11,3},{4,12},{12,4},... | collective-permute-start | bytes 884744 | tf_op jit(solution)/shard_map/ppermute | solution.py:230
  40.9 2.6 %collective-permute-start.16 = (bf16[4,288,128]{2,1,0:T(8,128)(2,1)}, bf16[4,288,128]{2,1,0:T(8,128)(2,1)S(1)}, u32[]{:S(2)}, u32[]{:S(2)}) collective-permute-start(bf16[4,288,128]{2,1,0:T(8,128)(2,1)} %pad_maximum_fusion.1.rest_8_), channel_id=1, source_target_pairs={{0,8},{8,0},{1,9},{9,1},{2,10},{10,2},{3,11},{11,3},{4,12},{12,4},... | collective-permute-start | bytes 884744 | tf_op jit(solution)/shard_map/ppermute | solution.py:230
  42.5 1.8 %collective-permute-start.13 = (bf16[4,288,128]{2,1,0:T(8,128)(2,1)}, bf16[4,288,128]{2,1,0:T(8,128)(2,1)S(1)}, u32[]{:S(2)}, u32[]{:S(2)}) collective-permute-start(bf16[4,288,128]{2,1,0:T(8,128)(2,1)} %collective-permute-done.3.rest_2_), channel_id=1, source_target_pairs={{0,8},{8,0},{1,9},{9,1},{2,10},{10,2},{3,11},{11,3},{4,12},{12,4},... | collective-permute-start | bytes 884744 | tf_op jit(solution)/shard_map/ppermute | solution.py:230
  42.6 2.4 %collective-permute-start.14 = (bf16[4,288,128]{2,1,0:T(8,128)(2,1)}, bf16[4,288,128]{2,1,0:T(8,128)(2,1)S(1)}, u32[]{:S(2)}, u32[]{:S(2)}) collective-permute-start(bf16[4,288,128]{2,1,0:T(8,128)(2,1)} %collective-permute-done.4.rest_4_), channel_id=1, source_target_pairs={{0,8},{8,0},{1,9},{9,1},{2,10},{10,2},{3,11},{11,3},{4,12},{12,4},... | collective-permute-start | bytes 884744 | tf_op jit(solution)/shard_map/ppermute | solution.py:230
  43.0 2.3 %collective-permute-start.15 = (bf16[4,288,128]{2,1,0:T(8,128)(2,1)S(1)}, bf16[4,288,128]{2,1,0:T(8,128)(2,1)S(1)}, u32[]{:S(2)}, u32[]{:S(2)}) collective-permute-start(bf16[4,288,128]{2,1,0:T(8,128)(2,1)S(1)} %copy-done.6), channel_id=1, source_target_pairs={{0,8},{8,0},{1,9},{9,1},{2,10},{10,2},{3,11},{11,3},{4,12},{12,4},... | collective-permute-start | bytes 884744 | tf_op jit(solution)/shard_map/ppermute | solution.py:230
  43.1 3.3 %copy-start.7 = (bf16[4,288,128]{2,1,0:T(8,128)(2,1)}, bf16[4,288,128]{2,1,0:T(8,128)(2,1)S(1)}, u32[]{:S(2)}) copy-start(bf16[4,288,128]{2,1,0:T(8,128)(2,1)S(1)} %collective-permute-done.12.rest_1_) | copy-start | bytes 884740
  43.1 2.4 %collective-permute-start.17 = (bf16[4,288,128]{2,1,0:T(8,128)(2,1)}, bf16[4,288,128]{2,1,0:T(8,128)(2,1)S(1)}, u32[]{:S(2)}, u32[]{:S(2)}) collective-permute-start(bf16[4,288,128]{2,1,0:T(8,128)(2,1)} %collective-permute-done.9.rest_10_), channel_id=1, source_target_pairs={{0,8},{8,0},{1,9},{9,1},{2,10},{10,2},{3,11},{11,3},{4,12},{12,4},... | collective-permute-start | bytes 884744 | tf_op jit(solution)/shard_map/ppermute | solution.py:230
  43.5 2.9 %copy-start.8 = (bf16[4,288,128]{2,1,0:T(8,128)(2,1)}, bf16[4,288,128]{2,1,0:T(8,128)(2,1)S(1)}, u32[]{:S(2)}) copy-start(bf16[4,288,128]{2,1,0:T(8,128)(2,1)S(1)} %collective-permute-done.16.rest_9_) | copy-start | bytes 884740
  43.5 2.4 %collective-permute-start.18 = (bf16[4,288,128]{2,1,0:T(8,128)(2,1)}, bf16[4,288,128]{2,1,0:T(8,128)(2,1)S(1)}, u32[]{:S(2)}, u32[]{:S(2)}) collective-permute-start(bf16[4,288,128]{2,1,0:T(8,128)(2,1)} %collective-permute-done.10.rest_12_), channel_id=1, source_target_pairs={{0,8},{8,0},{1,9},{9,1},{2,10},{10,2},{3,11},{11,3},{4,12},{12,4},... | collective-permute-start | bytes 884744 | tf_op jit(solution)/shard_map/ppermute | solution.py:230
  44.3 2.1 %copy-start.9 = (bf16[4,288,128]{2,1,0:T(8,128)(2,1)}, bf16[4,288,128]{2,1,0:T(8,128)(2,1)S(1)}, u32[]{:S(2)}) copy-start(bf16[4,288,128]{2,1,0:T(8,128)(2,1)S(1)} %collective-permute-done.13.rest_3_) | copy-start | bytes 884740
  44.3 2.1 %collective-permute-start.19 = (bf16[4,288,128]{2,1,0:T(8,128)(2,1)}, bf16[4,288,128]{2,1,0:T(8,128)(2,1)S(1)}, u32[]{:S(2)}, u32[]{:S(2)}) collective-permute-start(bf16[4,288,128]{2,1,0:T(8,128)(2,1)} %collective-permute-done.11.rest_14_), channel_id=1, source_target_pairs={{0,8},{8,0},{1,9},{9,1},{2,10},{10,2},{3,11},{11,3},{4,12},{12,4},... | collective-permute-start | bytes 884744 | tf_op jit(solution)/shard_map/ppermute | solution.py:230
  45.0 1.4 copy-start.10
  45.3 1.1 copy-start.11
  45.5 0.9 copy-start.12
  90.5 3.1 %collective-permute-start.20 = (bf16[4,4,288,128]{3,2,1,0:T(8,128)(2,1)}, bf16[4,4,288,128]{3,2,1,0:T(8,128)(2,1)S(1)}, u32[]{:S(2)}, u32[]{:S(2)}) collective-permute-start(bf16[4,4,288,128]{3,2,1,0:T(8,128)(2,1)} %get-tuple-element.31), channel_id=1, source_target_pairs={{0,8},{8,0},{1,9},{9,1},{2,10},{10,2},{3,11},{11,3},{4,12},{12,4},... | collective-permute-start | bytes 3538952 | tf_op jit(solution)/shard_map/ppermute | solution.py:230
  90.8 7.9 %collective-permute-start.27 = (bf16[4,4,288,128]{3,2,1,0:T(8,128)(2,1)}, bf16[4,4,288,128]{3,2,1,0:T(8,128)(2,1)S(1)}, u32[]{:S(2)}, u32[]{:S(2)}) collective-permute-start(bf16[4,4,288,128]{3,2,1,0:T(8,128)(2,1)} %get-tuple-element.33), channel_id=1, source_target_pairs={{0,8},{8,0},{1,9},{9,1},{2,10},{10,2},{3,11},{11,3},{4,12},{12,4},... | collective-permute-start | bytes 3538952 | tf_op jit(solution)/shard_map/ppermute | solution.py:230
  95.3 3.4 %copy-start.4 = (bf16[4,4,288,128]{3,2,1,0:T(8,128)(2,1)S(1)}, bf16[4,4,288,128]{3,2,1,0:T(8,128)(2,1)}, u32[]{:S(2)}) copy-start(bf16[4,4,288,128]{3,2,1,0:T(8,128)(2,1)} %get-tuple-element.32) | copy-start | bytes 3538948
  95.4 16.8 %collective-permute-start.21 = (bf16[4,288,128]{2,1,0:T(8,128)(2,1)S(1)}, bf16[4,288,128]{2,1,0:T(8,128)(2,1)S(1)}, u32[]{:S(2)}, u32[]{:S(2)}) collective-permute-start(bf16[4,288,128]{2,1,0:T(8,128)(2,1)S(1)} %get-tuple-element.42), channel_id=1, source_target_pairs={{0,64},{64,128},{128,192},{192,0},{1,65},{65,129},{129,193},{193,1... | collective-permute-start | bytes 884744 | tf_op jit(solution)/shard_map/ppermute | solution.py:230
  95.5 17.2 %collective-permute-start.23 = (bf16[4,288,128]{2,1,0:T(8,128)(2,1)S(1)}, bf16[4,288,128]{2,1,0:T(8,128)(2,1)S(1)}, u32[]{:S(2)}, u32[]{:S(2)}) collective-permute-start(bf16[4,288,128]{2,1,0:T(8,128)(2,1)S(1)} %get-tuple-element.43), channel_id=1, source_target_pairs={{0,192},{64,0},{128,64},{192,128},{1,193},{65,1},{129,65},{193,129... | collective-permute-start | bytes 884744 | tf_op jit(solution)/shard_map/ppermute | solution.py:230
  98.7 14.0 %collective-permute-start.22 = (bf16[4,288,128]{2,1,0:T(8,128)(2,1)S(1)}, bf16[4,288,128]{2,1,0:T(8,128)(2,1)S(1)}, u32[]{:S(2)}, u32[]{:S(2)}) collective-permute-start(bf16[4,288,128]{2,1,0:T(8,128)(2,1)S(1)} %get-tuple-element.44), channel_id=1, source_target_pairs={{0,128},{64,192},{128,0},{192,64},{1,129},{65,193},{129,1},{193,65... | collective-permute-start | bytes 884744 | tf_op jit(solution)/shard_map/ppermute | solution.py:230
  99.2 17.0 %collective-permute-start.28 = (bf16[4,288,128]{2,1,0:T(8,128)(2,1)S(1)}, bf16[4,288,128]{2,1,0:T(8,128)(2,1)S(1)}, u32[]{:S(2)}, u32[]{:S(2)}) collective-permute-start(bf16[4,288,128]{2,1,0:T(8,128)(2,1)S(1)} %get-tuple-element.45), channel_id=1, source_target_pairs={{0,16},{16,32},{32,48},{48,0},{1,17},{17,33},{33,49},{49,1},{2,18}... | collective-permute-start | bytes 884744 | tf_op jit(solution)/shard_map/ppermute | solution.py:230
  99.3 18.7 %collective-permute-start.30 = (bf16[4,288,128]{2,1,0:T(8,128)(2,1)S(1)}, bf16[4,288,128]{2,1,0:T(8,128)(2,1)S(1)}, u32[]{:S(2)}, u32[]{:S(2)}) collective-permute-start(bf16[4,288,128]{2,1,0:T(8,128)(2,1)S(1)} %get-tuple-element.46), channel_id=1, source_target_pairs={{0,48},{16,0},{32,16},{48,32},{1,49},{17,1},{33,17},{49,33},{2,50}... | collective-permute-start | bytes 884744 | tf_op jit(solution)/shard_map/ppermute | solution.py:230
  112.2 11.5 %collective-permute-start.29 = (bf16[4,288,128]{2,1,0:T(8,128)(2,1)S(1)}, bf16[4,288,128]{2,1,0:T(8,128)(2,1)S(1)}, u32[]{:S(2)}, u32[]{:S(2)}) collective-permute-start(bf16[4,288,128]{2,1,0:T(8,128)(2,1)S(1)} %get-tuple-element.47), channel_id=1, source_target_pairs={{0,32},{16,48},{32,0},{48,16},{1,33},{17,49},{33,1},{49,17},{2,34}... | collective-permute-start | bytes 884744 | tf_op jit(solution)/shard_map/ppermute | solution.py:230
  112.8 14.4 %collective-permute-start.24 = (bf16[288,128]{1,0:T(8,128)(2,1)S(1)}, bf16[288,128]{1,0:T(8,128)(2,1)S(1)}, u32[]{:S(2)}, u32[]{:S(2)}) collective-permute-start(bf16[288,128]{1,0:T(8,128)(2,1)S(1)} %get-tuple-element.48), channel_id=1, source_target_pairs={{0,16},{16,32},{32,48},{48,0},{1,17},{17,33},{33,49},{49,1},{2,18}... | collective-permute-start | bytes 221192 | tf_op jit(solution)/shard_map/ppermute | solution.py:230
  113.5 13.8 %collective-permute-start.26 = (bf16[288,128]{1,0:T(8,128)(2,1)S(1)}, bf16[288,128]{1,0:T(8,128)(2,1)S(1)}, u32[]{:S(2)}, u32[]{:S(2)}) collective-permute-start(bf16[288,128]{1,0:T(8,128)(2,1)S(1)} %get-tuple-element.49), channel_id=1, source_target_pairs={{0,48},{16,0},{32,16},{48,32},{1,49},{17,1},{33,17},{49,33},{2,50}... | collective-permute-start | bytes 221192 | tf_op jit(solution)/shard_map/ppermute | solution.py:230
  116.1 11.1 %collective-permute-start.25 = (bf16[288,128]{1,0:T(8,128)(2,1)S(1)}, bf16[288,128]{1,0:T(8,128)(2,1)S(1)}, u32[]{:S(2)}, u32[]{:S(2)}) collective-permute-start(bf16[288,128]{1,0:T(8,128)(2,1)S(1)} %get-tuple-element.50), channel_id=1, source_target_pairs={{0,32},{16,48},{32,0},{48,16},{1,33},{17,49},{33,1},{49,17},{2,34}... | collective-permute-start | bytes 221192 | tf_op jit(solution)/shard_map/ppermute | solution.py:230
  123.9 18.7 %copy-start.3 = (bf16[1024,576]{1,0:T(8,128)(2,1)S(1)}, bf16[1024,576]{1,0:T(8,128)(2,1)}, u32[]{:S(2)}) copy-start(bf16[1024,576]{1,0:T(8,128)(2,1)} %get-tuple-element.29) | copy-start | bytes 3538948
  123.9 6.2 %collective-permute-start.31 = (bf16[288,128]{1,0:T(8,128)(2,1)S(1)}, bf16[288,128]{1,0:T(8,128)(2,1)S(1)}, u32[]{:S(2)}, u32[]{:S(2)}) collective-permute-start(bf16[288,128]{1,0:T(8,128)(2,1)S(1)} %get-tuple-element.51), channel_id=1, source_target_pairs={{0,64},{64,128},{128,192},{192,0},{1,65},{65,129},{129,193},{193,1... | collective-permute-start | bytes 221192 | tf_op jit(solution)/shard_map/ppermute | solution.py:230
  124.0 6.1 %collective-permute-start.33 = (bf16[288,128]{1,0:T(8,128)(2,1)S(1)}, bf16[288,128]{1,0:T(8,128)(2,1)S(1)}, u32[]{:S(2)}, u32[]{:S(2)}) collective-permute-start(bf16[288,128]{1,0:T(8,128)(2,1)S(1)} %get-tuple-element.52), channel_id=1, source_target_pairs={{0,192},{64,0},{128,64},{192,128},{1,193},{65,1},{129,65},{193,129... | collective-permute-start | bytes 221192 | tf_op jit(solution)/shard_map/ppermute | solution.py:230
  127.3 5.9 %collective-permute-start.32 = (bf16[288,128]{1,0:T(8,128)(2,1)S(1)}, bf16[288,128]{1,0:T(8,128)(2,1)S(1)}, u32[]{:S(2)}, u32[]{:S(2)}) collective-permute-start(bf16[288,128]{1,0:T(8,128)(2,1)S(1)} %get-tuple-element.53), channel_id=1, source_target_pairs={{0,128},{64,192},{128,0},{192,64},{1,129},{65,193},{129,1},{193,65... | collective-permute-start | bytes 221192 | tf_op jit(solution)/shard_map/ppermute | solution.py:230
  134.0 16.5 %all-to-all-start = ((bf16[8,16,576]{2,1,0:T(8,128)(2,1)}), bf16[8,16,576]{2,1,0:T(8,128)(2,1)S(1)}, u32[]{:S(2)}, u32[]{:S(2)}) async-start(bf16[8,16,576]{2,1,0:T(8,128)(2,1)} %bitcast.39), calls=%async_computation | async-start | bytes 327680 | tf_op jit(solution)/shard_map/all_to_all | solution.py:287
  (2 other events, 1.4 us)

commit v3 on v2

v3 whole, which is shorter than its diff:
```python
import functools
import math

import jax
import jax.numpy as jnp
from jax import lax
from jax.experimental import pallas as pl
from jax.experimental.pallas import tpu as pltpu
from jax.sharding import Mesh, PartitionSpec as P

LATENT = 512
ROPE = 64
WIDTH = LATENT + ROPE
HALF = WIDTH // 2
GROUP = 64
BLOCK = 256
PAIR = 2 * GROUP

score_scale = 192.0 ** (-0.5)
log2_scale = score_scale * math.log2(math.e)
neg_fill = -1e30

NT = (((1,), (1,)), ((), ()))


def mm(a, b):
    return jnp.dot(a, b, preferred_element_type=jnp.float32)


def twice(a):
    return jnp.concatenate([a, a], axis=1)


def on_chip(a):
    return pltpu.with_memory_space_constraint(a, pltpu.VMEM)


def visit(items, step, pair_step):
    step(0)

    def body(j, carry):
        pair_step(2 * j + 1, 2 * j + 2)
        return carry

    lax.fori_loop(0, (items - 1) // 2, body, 0)


def key_sums(order, place, q_cols, g_cols, dscores, weights, tiles, fetch, *, sides, rows):
    width, latents = q_cols.shape[0], g_cols.shape[0]
    groups = 4 * sides * sides
    blocks = groups * GROUP // BLOCK
    rank = (place[0] * sides + place[1]) * 2 + place[2]
    high_blocks = lax.div(order[2 * rank + 1], BLOCK // GROUP) + 1
    low_blocks = blocks + 1 - high_blocks

    def term(i, half):
        if fetch is not None:
            fetch(i)
        at = half * rows
        from_scores = mm(q_cols[:, at : at + rows], dscores[i])
        from_values = mm(g_cols[:, at : at + rows], weights[i])
        if latents == width:
            return [from_scores + from_values]
        return [from_scores[:latents] + from_values, from_scores[latents:]]

    def put(b, parts):
        at = pl.multiple_of(b * BLOCK, BLOCK)
        row = 0
        for part in parts:
            tiles[row : row + part.shape[0], pl.ds(at, BLOCK)] = part.astype(jnp.bfloat16)
            row += part.shape[0]

    def both(b, carry):
        high = term(b, 1)
        low = term(high_blocks + b, 0)
        put(b, [h + l for h, l in zip(high, low)])
        return carry

    def two(j, carry):
        b = low_blocks + 1 + 2 * j
        first = term(b, 1)
        second = term(b + 1, 1)
        put(b, first)
        put(b + 1, second)
        return carry

    def clear(b, carry):
        at = pl.multiple_of(b * BLOCK, BLOCK)
        tiles[:, pl.ds(at, BLOCK)] = jnp.zeros((width, BLOCK), jnp.bfloat16)
        return carry

    lax.fori_loop(0, low_blocks, both, 0)
    put(low_blocks, term(low_blocks, 1))
    lax.fori_loop(0, lax.div(high_blocks - low_blocks - 1, 2), two, 0)
    lax.fori_loop(high_blocks, blocks, clear, 0)


def emit_tiles(order, place, tiles, keep, send, *, sides, swap):
    groups = 4 * sides * sides
    my_x, my_y, my_c = place[0], place[1], place[2]

    def owner(p, ref, at):
        group = order[2 * p]
        low_at = pl.multiple_of(lax.div(group, 2) * PAIR, PAIR)
        high_at = pl.multiple_of(lax.div(groups - 1 - group, 2) * PAIR, PAIR)
        low = tiles[:, pl.ds(low_at, PAIR)]
        high = tiles[:, pl.ds(high_at, PAIR)]
        odd = lax.rem(group, 2) == 1

        @pl.when(odd)
        def _():
            ref[at[0], at[1]] = jnp.concatenate([low[:, GROUP:], high[:, :GROUP]], axis=1)

        @pl.when(jnp.logical_not(odd))
        def _():
            ref[at[0], at[1]] = jnp.concatenate([low[:, :GROUP], high[:, GROUP:]], axis=1)

    def chip(i, carry):
        step_x = lax.rem(lax.div(i, sides) - my_x + sides, sides)
        step_y = lax.rem(lax.rem(i, sides) - my_y + sides, sides)
        at = (step_y, step_x) if swap else (step_x, step_y)
        owner(2 * i + 1 - my_c, send, at)
        owner(2 * i + my_c, keep, at)
        return carry

    lax.fori_loop(0, sides * sides, chip, 0)


def weights_kernel(order, place, q_in, g_in, q_cols_in, g_cols_in, deltas_in, *rest, sides, rows):
    pieces = 4 * sides
    piece_refs = rest[:pieces]
    keys, weights, dscores, keep, send = rest[pieces : pieces + 5]
    (
        stage, scores, dweights, top, total, q_rows, g_rows, q_cols, g_cols, deltas, tiles,
        slot_of, sem, own_sem,
    ) = rest[pieces + 5 :]
    pairs = stage.shape[0]
    groups = 2 * pairs
    blocks = groups * GROUP // BLOCK
    items = blocks + 1
    my_x, my_y, my_c = place[0], place[1], place[2]
    rank = (my_x * sides + my_y) * 2 + my_c

    copies = []
    for at, ref in enumerate(piece_refs):
        part, rest_at = at // (2 * sides), at % (2 * sides)
        first, step_c = rest_at // 2, rest_at % 2
        for second in range(sides):
            step_x, step_y = (first, second) if part == 0 else (second, first)
            at_x = lax.rem(my_x + step_x, sides)
            at_y = lax.rem(my_y + step_y, sides)
            at_c = lax.rem(my_c + step_c, 2)
            pair = (at_x * sides + at_y) * 2 + at_c
            copy = pltpu.make_async_copy(
                ref.at[second],
                stage.at[pair, pl.ds(part * HALF, HALF)],
                sem.at[at * sides + second],
            )
            copy.start()
            copies.append(copy)
    own = [
        pltpu.make_async_copy(src, dst, own_sem.at[at])
        for at, (src, dst) in enumerate(
            [
                (q_in, q_rows),
                (g_in, g_rows),
                (deltas_in, deltas),
                (q_cols_in.at[pl.ds(0, HALF)], q_cols),
                (g_cols_in.at[pl.ds(0, HALF)], g_cols),
            ]
        )
    ]
    for copy in own:
        copy.start()

    def note(p, carry):
        slot_of[order[2 * p]] = p
        return carry

    lax.fori_loop(0, pairs, note, 0)
    top[...] = jnp.full(top.shape, neg_fill, jnp.float32)
    total[...] = jnp.zeros(total.shape, jnp.float32)
    for copy in copies:
        copy.wait()

    def place_low(j, carry):
        for i in (2 * j, 2 * j + 1):
            first = stage[slot_of[2 * i]]
            second = stage[slot_of[2 * i + 1]]
            at = pl.multiple_of(i * PAIR, PAIR)
            keys[:, pl.ds(at, PAIR)] = jnp.concatenate([first[:, :GROUP], second[:, :GROUP]], axis=1)
        return carry

    def place_high(j, carry):
        for i in (2 * j, 2 * j + 1):
            first = stage[slot_of[groups - 1 - 2 * i]]
            second = stage[slot_of[groups - 2 - 2 * i]]
            at = pl.multiple_of(i * PAIR, PAIR)
            keys[:, pl.ds(at, PAIR)] = jnp.concatenate([first[:, GROUP:], second[:, GROUP:]], axis=1)
        return carry

    lax.fori_loop(0, pairs // 4, place_low, 0)
    lax.fori_loop(pairs // 4, pairs // 2, place_high, 0)
    for copy in own:
        copy.wait()

    low_group = order[2 * rank]
    high_group = order[2 * rank + 1]
    high_blocks = lax.div(high_group, BLOCK // GROUP) + 1

    def score_step(i):
        is_low = (i >= high_blocks).astype(jnp.int32)
        block = i - is_low * high_blocks
        row0 = pl.multiple_of((1 - is_low) * rows, rows)
        key0 = pl.multiple_of(block * BLOCK, BLOCK)
        group = jnp.where(is_low == 1, low_group, high_group)
        key_tile = keys[:, pl.ds(key0, BLOCK)]
        raw = mm(q_rows[pl.ds(row0, rows), :], key_tile) * log2_scale
        dweights[i] = mm(g_rows[pl.ds(row0, rows), :], key_tile[:LATENT])
        token = lax.broadcasted_iota(jnp.int32, (rows, BLOCK), 0) % GROUP
        lane = lax.broadcasted_iota(jnp.int32, (rows, BLOCK), 1)
        visible = lane - token <= group * GROUP - block * BLOCK
        t = jnp.where(visible, raw, neg_fill)
        scores[i] = t
        left, right = t[:, : BLOCK // 2], t[:, BLOCK // 2 :]
        old_top = top[pl.ds(row0, rows), :]
        new_top = jnp.maximum(old_top, jnp.maximum(left, right))
        added = jnp.exp2(left - new_top) + jnp.exp2(right - new_top)
        total[pl.ds(row0, rows), :] = total[pl.ds(row0, rows), :] * jnp.exp2(old_top - new_top) + added
        top[pl.ds(row0, rows), :] = new_top

    def score_pair(i, j):
        score_step(i)
        score_step(j)

    visit(items, score_step, score_pair)

    lane_top = top[...]
    row_top = jnp.max(lane_top, axis=1, keepdims=True)
    row_sum = jnp.sum(total[...] * jnp.exp2(lane_top - row_top), axis=1, keepdims=True)
    top[...] = jnp.broadcast_to(row_top + jnp.log2(row_sum), top.shape)

    def weigh(i):
        row0 = pl.multiple_of((i < high_blocks).astype(jnp.int32) * rows, rows)
        w = jnp.exp2(scores[i] - twice(top[pl.ds(row0, rows), :]))
        ds = w * (dweights[i] - twice(deltas[pl.ds(row0, rows), :])) * score_scale
        weights[i] = w.astype(jnp.bfloat16)
        dscores[i] = ds.astype(jnp.bfloat16)

    key_sums(
        order, place, q_cols, g_cols, dscores, weights, tiles, weigh, sides=sides, rows=rows
    )
    emit_tiles(order, place, tiles, keep, send, sides=sides, swap=False)


def keys_kernel(
    order, place, q_cols_in, g_cols_in, weights, dscores, keep, send, q_cols, g_cols, tiles,
    own_sem, *, sides, rows,
):
    own = [
        pltpu.make_async_copy(q_cols_in.at[pl.ds(HALF, HALF)], q_cols, own_sem.at[0]),
        pltpu.make_async_copy(g_cols_in.at[pl.ds(HALF, LATENT - HALF)], g_cols, own_sem.at[1]),
    ]
    for copy in own:
        copy.start()

    for copy in own:
        copy.wait()

    key_sums(
        order, place, q_cols, g_cols, dscores, weights, tiles, None, sides=sides, rows=rows
    )
    emit_tiles(order, place, tiles, keep, send, sides=sides, swap=True)


def query_kernel(order, place, dscores, keys, out, acc, *, sides, rows):
    items = dscores.shape[0]
    rank = (place[0] * sides + place[1]) * 2 + place[2]
    high_blocks = lax.div(order[2 * rank + 1], BLOCK // GROUP) + 1
    acc[...] = jnp.zeros(acc.shape, jnp.float32)

    def step(i):
        is_low = (i >= high_blocks).astype(jnp.int32)
        row0 = pl.multiple_of((1 - is_low) * rows, rows)
        key0 = pl.multiple_of((i - is_low * high_blocks) * BLOCK, BLOCK)
        acc[pl.ds(row0, rows), :] += lax.dot_general(
            dscores[i], keys[:, pl.ds(key0, BLOCK)], NT, preferred_element_type=jnp.float32
        )

    def pair_step(i, j):
        step(i)
        step(j)

    visit(items, step, pair_step)
    out[...] = acc[...].astype(jnp.bfloat16)


def run_weights(order, place, local, pieces, sides):
    rows = local[0].shape[0] // 2
    pairs = 2 * sides * sides
    items = pairs * PAIR // BLOCK + 1
    vmem = pl.BlockSpec(memory_space=pltpu.VMEM)
    smem = pl.BlockSpec(memory_space=pltpu.SMEM)
    hbm = pl.BlockSpec(memory_space=pl.ANY)
    bf16, f32 = jnp.bfloat16, jnp.float32
    part = jax.ShapeDtypeStruct((sides, sides, HALF, PAIR), bf16)
    block = pltpu.VMEM((items, rows, BLOCK), bf16)
    return pl.pallas_call(
        functools.partial(weights_kernel, sides=sides, rows=rows),
        out_shape=(pltpu.VMEM((WIDTH, pairs * PAIR), bf16), block, block, part, part),
        in_specs=[smem, smem] + [hbm] * (5 + len(pieces)),
        out_specs=(vmem,) * 5,
        scratch_shapes=[
            pltpu.VMEM((pairs, WIDTH, PAIR), bf16),
            pltpu.VMEM((items, rows, BLOCK), f32),
            pltpu.VMEM((items, rows, BLOCK), f32),
            pltpu.VMEM((2 * rows, 128), f32),
            pltpu.VMEM((2 * rows, 128), f32),
            pltpu.VMEM((2 * rows, WIDTH), bf16),
            pltpu.VMEM((2 * rows, LATENT), bf16),
            pltpu.VMEM((HALF, 2 * rows), bf16),
            pltpu.VMEM((HALF, 2 * rows), bf16),
            pltpu.VMEM((2 * rows, 128), f32),
            pltpu.VMEM((HALF, pairs * PAIR), bf16),
            pltpu.SMEM((2 * pairs,), jnp.int32),
            pltpu.SemaphoreType.DMA((2 * pairs,)),
            pltpu.SemaphoreType.DMA((5,)),
        ],
        compiler_params=pltpu.CompilerParams(vmem_limit_bytes=40 * 1024 * 1024),
        cost_estimate=pl.CostEstimate(
            flops=items * rows * BLOCK * 2 * 1664, bytes_accessed=24 << 20, transcendentals=0
        ),
        name="latent_weights",
    )(order, place, *local, *pieces)


def run_keys(order, place, q_cols, g_cols, weights, dscores, sides):
    items, rows = weights.shape[:2]
    pairs = 2 * sides * sides
    vmem = pl.BlockSpec(memory_space=pltpu.VMEM)
    smem = pl.BlockSpec(memory_space=pltpu.SMEM)
    hbm = pl.BlockSpec(memory_space=pl.ANY)
    bf16 = jnp.bfloat16
    part = jax.ShapeDtypeStruct((sides, sides, HALF, PAIR), bf16)
    return pl.pallas_call(
        functools.partial(keys_kernel, sides=sides, rows=rows),
        out_shape=(part, part),
        in_specs=[smem, smem, hbm, hbm, vmem, vmem],
        out_specs=(vmem, vmem),
        scratch_shapes=[
            pltpu.VMEM((HALF, 2 * rows), bf16),
            pltpu.VMEM((LATENT - HALF, 2 * rows), bf16),
            pltpu.VMEM((HALF, pairs * PAIR), bf16),
            pltpu.SemaphoreType.DMA((2,)),
        ],
        compiler_params=pltpu.CompilerParams(vmem_limit_bytes=24 * 1024 * 1024),
        cost_estimate=pl.CostEstimate(
            flops=items * rows * BLOCK * 2 * 512, bytes_accessed=12 << 20, transcendentals=0
        ),
        name="latent_keys",
    )(order, place, q_cols, g_cols, on_chip(weights), on_chip(dscores))


def run_queries(order, place, dscores, keys, sides):
    items, rows = dscores.shape[:2]
    vmem = pl.BlockSpec(memory_space=pltpu.VMEM)
    smem = pl.BlockSpec(memory_space=pltpu.SMEM)
    hbm = pl.BlockSpec(memory_space=pl.ANY)
    return pl.pallas_call(
        functools.partial(query_kernel, sides=sides, rows=rows),
        out_shape=jax.ShapeDtypeStruct((2 * rows, WIDTH), jnp.bfloat16),
        in_specs=[smem, smem, vmem, vmem],
        out_specs=vmem,
        scratch_shapes=[pltpu.VMEM((2 * rows, WIDTH), jnp.float32)],
        compiler_params=pltpu.CompilerParams(vmem_limit_bytes=24 * 1024 * 1024),
        cost_estimate=pl.CostEstimate(
            flops=items * rows * BLOCK * 2 * WIDTH, bytes_accessed=10 << 20, transcendentals=0
        ),
        name="latent_queries",
    )(order, place, on_chip(dscores), on_chip(keys))


def shift(a, axis, size, step):
    return lax.ppermute(a, axis, [(i, (i - step) % size) for i in range(size)])


def head_rows(a, width):
    tokens = a.shape[0]
    heads = a.shape[1] // width
    a = a.reshape(2, tokens // 2, heads, width).transpose(0, 2, 1, 3)
    return a.reshape(tokens * heads, width)


def shards(q_latent, kv_latent, out_grad, saved_out, group_order, *, sides, depth):
    tokens = q_latent.shape[0]
    heads = q_latent.shape[1] // WIDTH
    place = jnp.stack([lax.axis_index("x"), lax.axis_index("y"), lax.axis_index("c")]).astype(jnp.int32)

    def spread(a, axis):
        return [a] + [shift(a, axis, sides, d) for d in range(1, sides)]

    own = kv_latent.T
    part_a = spread(jnp.stack(spread(own[:HALF], "y")), "x")
    part_b = spread(jnp.stack(spread(own[HALF:], "x")), "y")

    q_rows = head_rows(q_latent, WIDTH)
    g_rows = head_rows(out_grad, LATENT)
    delta = jnp.sum(
        (out_grad.astype(jnp.float32) * saved_out.astype(jnp.float32)).reshape(
            2, tokens // 2, heads, LATENT
        ),
        axis=3,
    )
    delta = delta.transpose(0, 2, 1).reshape(tokens * heads, 1)
    deltas = jnp.broadcast_to(delta, (tokens * heads, 128))
    local = (q_rows, g_rows, q_rows.T, g_rows.T, deltas)
    arrived, local = lax.optimization_barrier((part_a[1:] + part_b[1:], local))
    pieces = []
    for piece in [part_a[0]] + arrived[: sides - 1] + [part_b[0]] + arrived[sides - 1 :]:
        pieces += [piece, shift(piece, "c", 2, 1)]

    keys, weights, dscores, keep_a, send_a = run_weights(group_order, place, local, pieces, sides)
    got_a = shift(send_a, "c", 2, 1)
    keep_b, send_b = run_keys(group_order, place, local[2], local[3], weights, dscores, sides)
    got_b = shift(send_b, "c", 2, 1)

    def first_sum(keep, got):
        total = keep.astype(jnp.float32) + got.astype(jnp.float32)
        return total[0], [total[d].astype(jnp.bfloat16) for d in range(1, sides)]

    def exchange(axis, total, low):
        for d in range(1, sides):
            total = total + shift(low[d - 1], axis, sides, -d).astype(jnp.float32)
        return total

    total_a, low_a = first_sum(keep_a, got_a)
    total_b, low_b = first_sum(keep_b, got_b)
    low_b, dscores = lax.optimization_barrier((low_b, dscores))
    dq = run_queries(group_order, place, dscores, keys, sides)
    q_grad = dq.reshape(2, heads, tokens // 2, WIDTH).transpose(0, 2, 1, 3)
    q_grad = q_grad.reshape(tokens, heads * WIDTH)
    total_a = exchange("x", total_a, low_a)
    total_b = exchange("y", total_b, low_b)
    total_a, total_b, q_grad = lax.optimization_barrier((total_a, total_b, q_grad))

    def last(total, axis):
        low = [total[d].astype(jnp.bfloat16) for d in range(1, sides)]
        return exchange(axis, total[0], low)

    summed = jnp.concatenate([last(total_a, "y"), last(total_b, "x")])
    by_head = summed.reshape(WIDTH, depth, PAIR // depth).transpose(1, 2, 0)
    parts = lax.all_to_all(by_head.astype(jnp.bfloat16), "z", 0, 0, tiled=True)
    return q_grad, jnp.sum(parts.astype(jnp.float32), axis=0)


def solution(mesh):
    ctx, depth = mesh.shape["ctx"], mesh.shape["head"]
    sides = math.isqrt(ctx // 2)
    finer = Mesh(mesh.devices.reshape(sides, sides, 2, depth), ("x", "y", "c", "z"))
    ctx_axes = ("x", "y", "c")
    placed = (P(ctx_axes, "z"), P(ctx_axes, None), P(ctx_axes, "z"), P(ctx_axes, "z"), P())
    return jax.shard_map(
        functools.partial(shards, sides=sides, depth=depth),
        mesh=finer,
        in_specs=placed,
        out_specs=(P(ctx_axes, "z"), P(("x", "y", "c", "z"), None)),
        check_vma=False,
    )
```

time: 152 us -> 147 us (0.967)
  waiting for transfers between devices: 36.1 us -> 19 us
  blocking collectives: 0 us -> 16.3 us
  starting transfers between devices: 46.9 us -> 37.7 us
  local copies, waits for them, and re-layouts: 16.8 us -> 20.1 us
  other arithmetic: 7.24 us -> 9.34 us
    all_to_all x0 -> x1, blocking collectives: none -> 16.3 us  [shards(): parts = lax.all_to_all(by_head.astype(jnp.bfloat16), 'z', 0, 0, tiled=True)]
    ppermute x34, waiting for transfers between devices: 30.6 us -> 19 us  [shift(): return lax.ppermute(a, axis, [(i, (i - step) % size) for i in range(size)])]
    all_to_all x1 -> x0, starting transfers between devices: 8.57 us -> none  [shards(): parts = lax.all_to_all(by_head.astype(jnp.bfloat16), 'z', 0, 0, tiled=True)]
    all_to_all x1 -> x0, waiting for transfers between devices: 5.51 us -> none  [shards(): parts = lax.all_to_all(by_head.astype(jnp.bfloat16), 'z', 0, 0, tiled=True)]
    another operation x2 -> x6, other arithmetic: 0.09 us -> 3.83 us
    reshape x2, local copies, waits for them, and re-layouts: 2.9 us -> 4.65 us  [head_rows(): return a.reshape(tokens * heads, width)]
    pallas_call x1 -> x3, Pallas kernels: 43.1 us -> 42.2 us  [the longest x1 26.5 us: run_weights(): pl.pallas_call(functools.partial(weights_kernel, sides=sides, rows=rows),...]
  transfers between devices with their start and end apart: 35 -> 34, of which waited for: 12 -> 12; matrix products, arithmetic and copies ran while one was open for 14% -> 17% of each run, Pallas kernels for 0% -> 5%
where the time goes in v3:
time: 147 us; the launch traced here: 146 us
  Pallas kernels  42.2 us (29%)
  starting transfers between devices  37.7 us (26%)
  local copies, waits for them, and re-layouts  20.1 us (14%)
  waiting for transfers between devices  19 us (13%)
  blocking collectives  16.3 us (11%)
  other arithmetic  9.34 us (6%)
    ppermute x34, starting transfers between devices, shift(): return lax.ppermute(a, axis, [(i, (i - step) % size) for i in range(size)])  37.7 us
    pallas_call x1, Pallas kernels, run_weights(): pl.pallas_call(functools.partial(weights_kernel, sides=sides, rows=rows),...  26.5 us
    ppermute x34, waiting for transfers between devices, shift(): return lax.ppermute(a, axis, [(i, (i - step) % size) for i in range(size)])  19 us
    all_to_all x1, blocking collectives, shards(): parts = lax.all_to_all(by_head.astype(jnp.bfloat16), 'z', 0, 0, tiled=True)  16.3 us
    pallas_call x1, Pallas kernels, run_keys(): pl.pallas_call(functools.partial(keys_kernel, sides=sides, rows=rows), ou...  8.64 us
    pallas_call x1, Pallas kernels, run_queries(): pl.pallas_call(functools.partial(query_kernel, sides=sides, rows=rows), o...  7.06 us
    reshape x2, local copies, waits for them, and re-layouts, head_rows(): a = a.reshape(2, tokens // 2, heads, width).transpose(0, 2, 1, 3)  6.08 us
    reshape x2, local copies, waits for them, and re-layouts, head_rows(): return a.reshape(tokens * heads, width)  4.65 us
  transfers between devices with their start and end apart: 34, of which 12 were waited for; matrix products, arithmetic and copies ran while one was open for 17% of the time, Pallas kernels for 5%

profile of v3, /device:TPU:32, one launch (start us, length us, event | category | flops | bytes accessed | tf_op | source)
XLA Modules:
  0.0 145.5 jit_solution(17880769137140825692)
XLA Ops:
  0.6 1.0 slice_bitcast_fusion.14
  1.6 3.3 %collective-permute-start.1 = (bf16[288,128]{1,0:T(8,128)(2,1)S(1)}, bf16[288,128]{1,0:T(8,128)(2,1)S(1)}, u32[]{:S(2)}, u32[]{:S(2)}) collective-permute-start(bf16[288,128]{1,0:T(8,128)(2,1)S(1)} %get-tuple-element.71), channel_id=1, source_target_pairs={{0,32},{16,48},{32,0},{48,16},{1,33},{17,49},{33,1},{49,17},{2,34}... | collective-permute-start | bytes 221192 | tf_op jit(solution)/shard_map/ppermute | solution.py:384
  4.9 1.1 collective-permute-start
  5.9 1.0 collective-permute-start.2
  6.9 3.0 %collective-permute-start.7 = (bf16[288,128]{1,0:T(8,128)(2,1)S(1)}, bf16[288,128]{1,0:T(8,128)(2,1)S(1)}, u32[]{:S(2)}, u32[]{:S(2)}) collective-permute-start(bf16[288,128]{1,0:T(8,128)(2,1)S(1)} %get-tuple-element.70), channel_id=1, source_target_pairs={{0,128},{64,192},{128,0},{192,64},{1,129},{65,193},{129,1},{193,65... | collective-permute-start | bytes 221192 | tf_op jit(solution)/shard_map/ppermute | solution.py:384
  9.9 1.1 collective-permute-start.6
  11.1 0.9 collective-permute-start.8
  12.0 1.1 collective-permute-start.5
  13.1 1.8 %convert_multiply_fusion = f32[128,4096]{1,0:T(8,128)S(1)} fusion(bf16[128,4096]{1,0:T(8,128)(2,1)} %param.8, bf16[128,4096]{1,0:T(8,128)(2,1)} %param.7), kind=kLoop, calls=%fused_computation.3 | loop fusion | flops 1572864 | bytes 4194304 | tf_op jit(solution)/shard_map/mul | solution.py:409
  15.3 2.9 %collective-permute-start.4 = (bf16[4,288,128]{2,1,0:T(8,128)(2,1)S(1)}, bf16[4,288,128]{2,1,0:T(8,128)(2,1)}, u32[]{:S(2)}, u32[]{:S(2)}) collective-permute-start(bf16[4,288,128]{2,1,0:T(8,128)(2,1)S(1)} %pad_maximum_fusion.rest_0_), channel_id=1, source_target_pairs={{0,128},{64,192},{128,0},{192,64},{1,129},{65,193},{129,1},{193,65... | collective-permute-start | bytes 884744 | tf_op jit(solution)/shard_map/ppermute | solution.py:384
  18.2 1.4 collective-permute-start.3
  19.7 2.4 %collective-permute-start.10 = (bf16[4,288,128]{2,1,0:T(8,128)(2,1)S(1)}, bf16[4,288,128]{2,1,0:T(8,128)(2,1)}, u32[]{:S(2)}, u32[]{:S(2)}) collective-permute-start(bf16[4,288,128]{2,1,0:T(8,128)(2,1)S(1)} %pad_maximum_fusion.1.rest_8_), channel_id=1, source_target_pairs={{0,32},{16,48},{32,0},{48,16},{1,33},{17,49},{33,1},{49,17},{2,34}... | collective-permute-start | bytes 884744 | tf_op jit(solution)/shard_map/ppermute | solution.py:384
  22.2 1.7 %collective-permute-done.5.rest_6_ = bf16[4,288,128]{2,1,0:T(8,128)(2,1)S(1)} collective-permute-done((bf16[4,288,128]{2,1,0:T(8,128)(2,1)S(1)}, bf16[4,288,128]{2,1,0:T(8,128)(2,1)S(1)}, u32[]{:S(2)}, u32[]{:S(2)}) %collective-permute-start.5) | collective-permute-done | bytes 294944 | tf_op jit(solution)/shard_map/ppermute | solution.py:384
  23.9 1.3 collective-permute-start.9
  25.3 1.3 copy.24
  26.6 2.3 %copy.26 = bf16[1024,512]{0,1:T(8,128)(2,1)} copy(bf16[1024,512]{1,0:T(8,128)(2,1)} %bitcast.106) | data formatting | bytes 2097152 | tf_op jit(solution)/shard_map/reshape | solution.py:391
  28.9 3.5 %reshape.41 = bf16[2,64,8,576]{3,2,1,0:T(8,128)(2,1)} reshape(bf16[128,4608]{1,0:T(8,128)(2,1)} %param.5) | data formatting | bytes 2359296 | tf_op jit(solution)/shard_map/reshape | solution.py:390
  32.4 2.6 %copy.23 = bf16[2,64,8,576]{3,1,2,0:T(8,128)(2,1)} copy(bf16[2,64,8,576]{3,2,1,0:T(8,128)(2,1)} %reshape.41) | data formatting | bytes 2359296 | tf_op jit(solution)/shard_map/reshape | solution.py:390
  35.0 2.4 %copy.25 = bf16[1024,576]{0,1:T(8,128)(2,1)} copy(bf16[1024,576]{1,0:T(8,128)(2,1)} %bitcast.104) | data formatting | bytes 2359296 | tf_op jit(solution)/shard_map/reshape | solution.py:391
  37.4 1.6 %copy.31 = f32[16,8,8,512]{3,2,1,0:T(8,128)S(1)} copy(f32[16,8,8,512]{3,1,2,0:T(8,128)S(1)} %bitcast.102) | data formatting | bytes 4194304
  39.9 1.0 broadcast_in_dim.8.deltas_in
  43.2 0.6 collective-permute-done.15.rest_7_
  45.2 0.7 copy-done.14
  45.9 26.5 %latent_weights.1 = (bf16[576,4096]{1,0:T(8,128)(2,1)S(1)}, bf16[17,512,256]{2,1,0:T(8,128)(2,1)S(1)}, bf16[17,512,256]{2,1,0:T(8,128)(2,1)S(1)}, bf16[4,4,288,1...) custom-call(s32[64]{0:T(128)S(1)} %copy-done.2, s32[3]{0:T(128)S(1)} %pad_add_fusion.place, bf16[1024,576]{1,0:T(8,128)(2,1)} %bitcast.105, ...), custom_call_target="tpu_custom_call" | custom-call | flops 7415529472 | bytes 25165824 | tf_op jit(solution)/shard_map/latent_weights/pallas_call | solution.py:308
  72.5 8.6 %latent_keys.1 = (bf16[4,4,288,128]{3,2,1,0:T(8,128)(2,1)S(1)}, bf16[4,4,288,128]{3,2,1,0:T(8,128)(2,1)S(1)}) custom-call(s32[64]{0:T(128)S(1)} %copy-done.2, s32[3]{0:T(128)S(1)} %pad_add_fusion.place, bf16[576,1024]{1,0:T(8,128)(2,1)S(1)} %bitcast.99, bf16[512,1024]{1,0:T(8,128)(2,1)S(1)} %bitcast.101, ...), custom_call_target="tpu_custom_call" | custom-call | flops 2281701376 | bytes 12582912 | tf_op jit(solution)/shard_map/latent_keys/pallas_call | solution.py:345
  81.7 2.3 %collective-permute-done.24 = bf16[4,4,288,128]{3,2,1,0:T(8,128)(2,1)S(1)} collective-permute-done((bf16[4,4,288,128]{3,2,1,0:T(8,128)(2,1)S(1)}, bf16[4,4,288,128]{3,2,1,0:T(8,128)(2,1)S(1)}, u32[]{:S(2)}, u32[]{:S(2)}) %collective-permute-start.24) | collective-permute-done | bytes 1179680 | tf_op jit(solution)/shard_map/ppermute | solution.py:384
  84.0 1.8 %fusion.13 = (bf16[4,4,288,128]{3,2,1,0:T(8,128)(2,1)S(1)}, f32[4,4,288,128]{3,2,1,0:T(8,128)}) fusion(bf16[4,4,288,128]{3,2,1,0:T(8,128)(2,1)S(1)} %collective-permute-done.24, bf16[4,4,288,128]{3,2,1,0:T(8,128)(2,1)S(1)} %get-tuple-element.42), kind=kLoop, calls=%fused_computation.41 | loop fusion | flops 2359296 | bytes 5898240 | tf_op jit(solution)/shard_map/convert.10
  85.9 0.6 collective-permute-start.25
  86.5 1.1 collective-permute-start.26
  87.6 1.7 %collective-permute-start.27 = (bf16[4,288,128]{2,1,0:T(8,128)(2,1)S(1)}, bf16[4,288,128]{2,1,0:T(8,128)(2,1)}, u32[]{:S(2)}, u32[]{:S(2)}) collective-permute-start(bf16[4,288,128]{2,1,0:T(8,128)(2,1)S(1)} %get-tuple-element.46), channel_id=1, source_target_pairs={{0,48},{16,0},{32,16},{48,32},{1,49},{17,1},{33,17},{49,33},{2,50}... | collective-permute-start | bytes 884744 | tf_op jit(solution)/shard_map/ppermute | solution.py:384
  89.3 1.9 %fusion.12 = (bf16[4,4,288,128]{3,2,1,0:T(8,128)(2,1)S(1)}, f32[4,4,288,128]{3,2,1,0:T(8,128)}) fusion(bf16[4,4,288,128]{3,2,1,0:T(8,128)(2,1)S(1)} %collective-permute-done.20, bf16[4,4,288,128]{3,2,1,0:T(8,128)(2,1)S(1)} %copy-done.4), kind=kLoop, calls=%fused_computation.40 | loop fusion | flops 2359296 | bytes 5898240 | tf_op jit(solution)/shard_map/convert.13
  91.2 0.9 collective-permute-start.21
  92.1 2.5 %collective-permute-start.23 = (bf16[4,288,128]{2,1,0:T(8,128)(2,1)S(1)}, bf16[4,288,128]{2,1,0:T(8,128)(2,1)}, u32[]{:S(2)}, u32[]{:S(2)}) collective-permute-start(bf16[4,288,128]{2,1,0:T(8,128)(2,1)S(1)} %get-tuple-element.60), channel_id=1, source_target_pairs={{0,192},{64,0},{128,64},{192,128},{1,193},{65,1},{129,65},{193,129... | collective-permute-start | bytes 884744 | tf_op jit(solution)/shard_map/ppermute | solution.py:384
  94.5 8.1 %collective-permute-done.25 = bf16[4,288,128]{2,1,0:T(8,128)(2,1)S(1)} collective-permute-done((bf16[4,288,128]{2,1,0:T(8,128)(2,1)S(1)}, bf16[4,288,128]{2,1,0:T(8,128)(2,1)S(1)}, u32[]{:S(2)}, u32[]{:S(2)}) %collective-permute-start.25) | collective-permute-done | bytes 294944 | tf_op jit(solution)/shard_map/ppermute | solution.py:384
  102.6 0.9 collective-permute-start.22
  103.4 7.1 %latent_queries.1 = bf16[1024,576]{1,0:T(8,128)(2,1)S(1)} custom-call(s32[64]{0:T(128)S(1)} %copy-done.2, s32[3]{0:T(128)S(1)} %pad_add_fusion.place, bf16[17,512,256]{2,1,0:T(8,128)(2,1)S(1)} %get-tuple-element.47.dscores, bf16[576,4096]{1,0:T(8,128)(2,1)S(1)} %get-tuple-element.48.keys), custom_call_target="tpu_custom_call" | custom-call | flops 2566914048 | bytes 10485760 | tf_op jit(solution)/shard_map/latent_queries/pallas_call | solution.py:369
  110.5 0.7 copy.28
  111.3 1.7 %reshape.47 = bf16[128,4608]{1,0:T(8,128)(2,1)} reshape(bf16[2,64,8,576]{3,2,1,0:T(8,128)(2,1)S(1)} %copy.28) | data formatting | bytes 2359296 | tf_op jit(solution)/shard_map/reshape | solution.py:441
  113.0 1.3 fusion.2
  114.3 1.4 fusion.5
  115.9 3.2 %collective-permute-start.30 = (bf16[288,128]{1,0:T(8,128)(2,1)S(1)}, bf16[288,128]{1,0:T(8,128)(2,1)S(1)}, u32[]{:S(2)}, u32[]{:S(2)}) collective-permute-start(bf16[288,128]{1,0:T(8,128)(2,1)S(1)} %get-tuple-element.63), channel_id=1, source_target_pairs={{0,48},{16,0},{32,16},{48,32},{1,49},{17,1},{33,17},{49,33},{2,50}... | collective-permute-start | bytes 221192 | tf_op jit(solution)/shard_map/ppermute | solution.py:384
  119.2 1.4 collective-permute-start.31
  120.6 1.9 %collective-permute-start.33 = (bf16[288,128]{1,0:T(8,128)(2,1)S(1)}, bf16[288,128]{1,0:T(8,128)(2,1)S(1)}, u32[]{:S(2)}, u32[]{:S(2)}) collective-permute-start(bf16[288,128]{1,0:T(8,128)(2,1)S(1)} %get-tuple-element.66), channel_id=1, source_target_pairs={{0,192},{64,0},{128,64},{192,128},{1,193},{65,1},{129,65},{193,129... | collective-permute-start | bytes 221192 | tf_op jit(solution)/shard_map/ppermute | solution.py:384
  122.5 1.6 %collective-permute-start.32 = (bf16[288,128]{1,0:T(8,128)(2,1)S(1)}, bf16[288,128]{1,0:T(8,128)(2,1)S(1)}, u32[]{:S(2)}, u32[]{:S(2)}) collective-permute-start(bf16[288,128]{1,0:T(8,128)(2,1)S(1)} %get-tuple-element.67), channel_id=1, source_target_pairs={{0,128},{64,192},{128,0},{192,64},{1,129},{65,193},{129,1},{193,65... | collective-permute-start | bytes 221192 | tf_op jit(solution)/shard_map/ppermute | solution.py:384
  124.1 0.9 collective-permute-done.29
  125.2 3.2 %collective-permute-done.32 = bf16[288,128]{1,0:T(8,128)(2,1)S(1)} collective-permute-done((bf16[288,128]{1,0:T(8,128)(2,1)S(1)}, bf16[288,128]{1,0:T(8,128)(2,1)S(1)}, u32[]{:S(2)}, u32[]{:S(2)}) %collective-permute-start.32) | collective-permute-done | bytes 73760 | tf_op jit(solution)/shard_map/ppermute | solution.py:384
  128.6 16.3 %all_to_all.5 = bf16[8,16,576]{2,1,0:T(8,128)(2,1)S(1)} all-to-all(bf16[8,16,576]{2,1,0:T(8,128)(2,1)S(1)} %bitcast.110), channel_id=1, replica_groups=mesh['x'=4,'y'=4,'c'=2,'z'=8] {'z'}, dimensions={0} | all-to-all | bytes 294912 | tf_op jit(solution)/shard_map/all_to_all | solution.py:452
  144.9 0.6 convert_reduce_fusion
  (88 shorter events, 6.5 us)
Async XLA Ops:
  1.6 9.5 %collective-permute-start.1 = (bf16[288,128]{1,0:T(8,128)(2,1)S(1)}, bf16[288,128]{1,0:T(8,128)(2,1)S(1)}, u32[]{:S(2)}, u32[]{:S(2)}) collective-permute-start(bf16[288,128]{1,0:T(8,128)(2,1)S(1)} %get-tuple-element.71), channel_id=1, source_target_pairs={{0,32},{16,48},{32,0},{48,16},{1,33},{17,49},{33,1},{49,17},{2,34}... | collective-permute-start | bytes 221192 | tf_op jit(solution)/shard_map/ppermute | solution.py:384
  4.9 7.1 %collective-permute-start = (bf16[288,128]{1,0:T(8,128)(2,1)S(1)}, bf16[288,128]{1,0:T(8,128)(2,1)S(1)}, u32[]{:S(2)}, u32[]{:S(2)}) collective-permute-start(bf16[288,128]{1,0:T(8,128)(2,1)S(1)} %get-tuple-element.71), channel_id=1, source_target_pairs={{0,48},{16,0},{32,16},{48,32},{1,49},{17,1},{33,17},{49,33},{2,50}... | collective-permute-start | bytes 221192 | tf_op jit(solution)/shard_map/ppermute | solution.py:384
  5.9 6.0 %collective-permute-start.2 = (bf16[288,128]{1,0:T(8,128)(2,1)S(1)}, bf16[288,128]{1,0:T(8,128)(2,1)S(1)}, u32[]{:S(2)}, u32[]{:S(2)}) collective-permute-start(bf16[288,128]{1,0:T(8,128)(2,1)S(1)} %get-tuple-element.71), channel_id=1, source_target_pairs={{0,16},{16,32},{32,48},{48,0},{1,17},{17,33},{33,49},{49,1},{2,18}... | collective-permute-start | bytes 221192 | tf_op jit(solution)/shard_map/ppermute | solution.py:384
  6.9 11.3 %collective-permute-start.7 = (bf16[288,128]{1,0:T(8,128)(2,1)S(1)}, bf16[288,128]{1,0:T(8,128)(2,1)S(1)}, u32[]{:S(2)}, u32[]{:S(2)}) collective-permute-start(bf16[288,128]{1,0:T(8,128)(2,1)S(1)} %get-tuple-element.70), channel_id=1, source_target_pairs={{0,128},{64,192},{128,0},{192,64},{1,129},{65,193},{129,1},{193,65... | collective-permute-start | bytes 221192 | tf_op jit(solution)/shard_map/ppermute | solution.py:384
  9.9 9.7 %collective-permute-start.6 = (bf16[288,128]{1,0:T(8,128)(2,1)S(1)}, bf16[288,128]{1,0:T(8,128)(2,1)S(1)}, u32[]{:S(2)}, u32[]{:S(2)}) collective-permute-start(bf16[288,128]{1,0:T(8,128)(2,1)S(1)} %get-tuple-element.70), channel_id=1, source_target_pairs={{0,192},{64,0},{128,64},{192,128},{1,193},{65,1},{129,65},{193,129... | collective-permute-start | bytes 221192 | tf_op jit(solution)/shard_map/ppermute | solution.py:384
  11.1 8.5 %collective-permute-start.8 = (bf16[288,128]{1,0:T(8,128)(2,1)S(1)}, bf16[288,128]{1,0:T(8,128)(2,1)S(1)}, u32[]{:S(2)}, u32[]{:S(2)}) collective-permute-start(bf16[288,128]{1,0:T(8,128)(2,1)S(1)} %get-tuple-element.70), channel_id=1, source_target_pairs={{0,64},{64,128},{128,192},{192,0},{1,65},{65,129},{129,193},{193,1... | collective-permute-start | bytes 221192 | tf_op jit(solution)/shard_map/ppermute | solution.py:384
  12.0 2.9 %copy-start.3 = (bf16[128,4096]{1,0:T(8,128)(2,1)S(1)}, bf16[128,4096]{1,0:T(8,128)(2,1)}, u32[]{:S(2)}) copy-start(bf16[128,4096]{1,0:T(8,128)(2,1)} %param.7) | copy-start | bytes 3145732
  12.0 11.9 %collective-permute-start.5 = (bf16[4,288,128]{2,1,0:T(8,128)(2,1)S(1)}, bf16[4,288,128]{2,1,0:T(8,128)(2,1)S(1)}, u32[]{:S(2)}, u32[]{:S(2)}) collective-permute-start(bf16[4,288,128]{2,1,0:T(8,128)(2,1)S(1)} %pad_maximum_fusion.rest_0_), channel_id=1, source_target_pairs={{0,64},{64,128},{128,192},{192,0},{1,65},{65,129},{129,193},{193,1... | collective-permute-start | bytes 884744 | tf_op jit(solution)/shard_map/ppermute | solution.py:384
  15.3 24.1 %collective-permute-start.4 = (bf16[4,288,128]{2,1,0:T(8,128)(2,1)S(1)}, bf16[4,288,128]{2,1,0:T(8,128)(2,1)}, u32[]{:S(2)}, u32[]{:S(2)}) collective-permute-start(bf16[4,288,128]{2,1,0:T(8,128)(2,1)S(1)} %pad_maximum_fusion.rest_0_), channel_id=1, source_target_pairs={{0,128},{64,192},{128,0},{192,64},{1,129},{65,193},{129,1},{193,65... | collective-permute-start | bytes 884744 | tf_op jit(solution)/shard_map/ppermute | solution.py:384
  18.2 21.2 %collective-permute-start.3 = (bf16[4,288,128]{2,1,0:T(8,128)(2,1)S(1)}, bf16[4,288,128]{2,1,0:T(8,128)(2,1)S(1)}, u32[]{:S(2)}, u32[]{:S(2)}) collective-permute-start(bf16[4,288,128]{2,1,0:T(8,128)(2,1)S(1)} %pad_maximum_fusion.rest_0_), channel_id=1, source_target_pairs={{0,192},{64,0},{128,64},{192,128},{1,193},{65,1},{129,65},{193,129... | collective-permute-start | bytes 884744 | tf_op jit(solution)/shard_map/ppermute | solution.py:384
  19.6 19.8 %copy-start.5 = (bf16[4,288,128]{2,1,0:T(8,128)(2,1)}, bf16[4,288,128]{2,1,0:T(8,128)(2,1)S(1)}, u32[]{:S(2)}) copy-start(bf16[4,288,128]{2,1,0:T(8,128)(2,1)S(1)} %pad_maximum_fusion.1.rest_8_) | copy-start | bytes 884740
  19.6 20.3 %collective-permute-start.11 = (bf16[4,288,128]{2,1,0:T(8,128)(2,1)S(1)}, bf16[4,288,128]{2,1,0:T(8,128)(2,1)}, u32[]{:S(2)}, u32[]{:S(2)}) collective-permute-start(bf16[4,288,128]{2,1,0:T(8,128)(2,1)S(1)} %pad_maximum_fusion.1.rest_8_), channel_id=1, source_target_pairs={{0,16},{16,32},{32,48},{48,0},{1,17},{17,33},{33,49},{49,1},{2,18}... | collective-permute-start | bytes 884744 | tf_op jit(solution)/shard_map/ppermute | solution.py:384
  19.7 20.2 %collective-permute-start.10 = (bf16[4,288,128]{2,1,0:T(8,128)(2,1)S(1)}, bf16[4,288,128]{2,1,0:T(8,128)(2,1)}, u32[]{:S(2)}, u32[]{:S(2)}) collective-permute-start(bf16[4,288,128]{2,1,0:T(8,128)(2,1)S(1)} %pad_maximum_fusion.1.rest_8_), channel_id=1, source_target_pairs={{0,32},{16,48},{32,0},{48,16},{1,33},{17,49},{33,1},{49,17},{2,34}... | collective-permute-start | bytes 884744 | tf_op jit(solution)/shard_map/ppermute | solution.py:384
  23.9 17.5 %copy-start.7 = (bf16[4,288,128]{2,1,0:T(8,128)(2,1)}, bf16[4,288,128]{2,1,0:T(8,128)(2,1)S(1)}, u32[]{:S(2)}) copy-start(bf16[4,288,128]{2,1,0:T(8,128)(2,1)S(1)} %collective-permute-done.5.rest_6_) | copy-start | bytes 884740
  23.9 16.0 %collective-permute-start.9 = (bf16[4,288,128]{2,1,0:T(8,128)(2,1)S(1)}, bf16[4,288,128]{2,1,0:T(8,128)(2,1)}, u32[]{:S(2)}, u32[]{:S(2)}) collective-permute-start(bf16[4,288,128]{2,1,0:T(8,128)(2,1)S(1)} %pad_maximum_fusion.1.rest_8_), channel_id=1, source_target_pairs={{0,48},{16,0},{32,16},{48,32},{1,49},{17,1},{33,17},{49,33},{2,50}... | collective-permute-start | bytes 884744 | tf_op jit(solution)/shard_map/ppermute | solution.py:384
  39.0 6.9 %copy-start.2 = (s32[64]{0:T(128)S(1)}, s32[64]{0:T(128)}, u32[]{:S(2)}) copy-start(s32[64]{0:T(128)} %order.5) | copy-start | bytes 772
  39.4 2.2 %collective-permute-start.12 = (bf16[4,288,128]{2,1,0:T(8,128)(2,1)S(1)}, bf16[4,288,128]{2,1,0:T(8,128)(2,1)S(1)}, u32[]{:S(2)}, u32[]{:S(2)}) collective-permute-start(bf16[4,288,128]{2,1,0:T(8,128)(2,1)S(1)} %pad_maximum_fusion.rest_0_), channel_id=1, source_target_pairs={{0,8},{8,0},{1,9},{9,1},{2,10},{10,2},{3,11},{11,3},{4,12},{12,4},... | collective-permute-start | bytes 884744 | tf_op jit(solution)/shard_map/ppermute | solution.py:384
  39.4 2.6 %collective-permute-start.16 = (bf16[4,288,128]{2,1,0:T(8,128)(2,1)S(1)}, bf16[4,288,128]{2,1,0:T(8,128)(2,1)S(1)}, u32[]{:S(2)}, u32[]{:S(2)}) collective-permute-start(bf16[4,288,128]{2,1,0:T(8,128)(2,1)S(1)} %pad_maximum_fusion.1.rest_8_), channel_id=1, source_target_pairs={{0,8},{8,0},{1,9},{9,1},{2,10},{10,2},{3,11},{11,3},{4,12},{12,4},... | collective-permute-start | bytes 884744 | tf_op jit(solution)/shard_map/ppermute | solution.py:384
  41.0 1.6 %collective-permute-start.13 = (bf16[4,288,128]{2,1,0:T(8,128)(2,1)S(1)}, bf16[4,288,128]{2,1,0:T(8,128)(2,1)S(1)}, u32[]{:S(2)}, u32[]{:S(2)}) collective-permute-start(bf16[4,288,128]{2,1,0:T(8,128)(2,1)S(1)} %collective-permute-done.3.rest_2_), channel_id=1, source_target_pairs={{0,8},{8,0},{1,9},{9,1},{2,10},{10,2},{3,11},{11,3},{4,12},{12,4},... | collective-permute-start | bytes 884744 | tf_op jit(solution)/shard_map/ppermute | solution.py:384
  41.1 2.1 %collective-permute-start.14 = (bf16[4,288,128]{2,1,0:T(8,128)(2,1)}, bf16[4,288,128]{2,1,0:T(8,128)(2,1)S(1)}, u32[]{:S(2)}, u32[]{:S(2)}) collective-permute-start(bf16[4,288,128]{2,1,0:T(8,128)(2,1)} %collective-permute-done.4.rest_4_), channel_id=1, source_target_pairs={{0,8},{8,0},{1,9},{9,1},{2,10},{10,2},{3,11},{11,3},{4,12},{12,4},... | collective-permute-start | bytes 884744 | tf_op jit(solution)/shard_map/ppermute | solution.py:384
  41.5 2.3 %collective-permute-start.15 = (bf16[4,288,128]{2,1,0:T(8,128)(2,1)S(1)}, bf16[4,288,128]{2,1,0:T(8,128)(2,1)S(1)}, u32[]{:S(2)}, u32[]{:S(2)}) collective-permute-start(bf16[4,288,128]{2,1,0:T(8,128)(2,1)S(1)} %collective-permute-done.5.rest_6_), channel_id=1, source_target_pairs={{0,8},{8,0},{1,9},{9,1},{2,10},{10,2},{3,11},{11,3},{4,12},{12,4},... | collective-permute-start | bytes 884744 | tf_op jit(solution)/shard_map/ppermute | solution.py:384
  41.6 2.4 %collective-permute-start.17 = (bf16[4,288,128]{2,1,0:T(8,128)(2,1)}, bf16[4,288,128]{2,1,0:T(8,128)(2,1)S(1)}, u32[]{:S(2)}, u32[]{:S(2)}) collective-permute-start(bf16[4,288,128]{2,1,0:T(8,128)(2,1)} %collective-permute-done.9.rest_10_), channel_id=1, source_target_pairs={{0,8},{8,0},{1,9},{9,1},{2,10},{10,2},{3,11},{11,3},{4,12},{12,4},... | collective-permute-start | bytes 884744 | tf_op jit(solution)/shard_map/ppermute | solution.py:384
  42.0 2.9 %copy-start.8 = (bf16[4,288,128]{2,1,0:T(8,128)(2,1)}, bf16[4,288,128]{2,1,0:T(8,128)(2,1)S(1)}, u32[]{:S(2)}) copy-start(bf16[4,288,128]{2,1,0:T(8,128)(2,1)S(1)} %collective-permute-done.16.rest_9_) | copy-start | bytes 884740
  42.0 2.4 %collective-permute-start.18 = (bf16[4,288,128]{2,1,0:T(8,128)(2,1)}, bf16[4,288,128]{2,1,0:T(8,128)(2,1)S(1)}, u32[]{:S(2)}, u32[]{:S(2)}) collective-permute-start(bf16[4,288,128]{2,1,0:T(8,128)(2,1)} %collective-permute-done.10.rest_12_), channel_id=1, source_target_pairs={{0,8},{8,0},{1,9},{9,1},{2,10},{10,2},{3,11},{11,3},{4,12},{12,4},... | collective-permute-start | bytes 884744 | tf_op jit(solution)/shard_map/ppermute | solution.py:384
  42.5 2.3 %copy-start.9 = (bf16[4,288,128]{2,1,0:T(8,128)(2,1)}, bf16[4,288,128]{2,1,0:T(8,128)(2,1)S(1)}, u32[]{:S(2)}) copy-start(bf16[4,288,128]{2,1,0:T(8,128)(2,1)S(1)} %collective-permute-done.13.rest_3_) | copy-start | bytes 884740
  42.5 2.3 %collective-permute-start.19 = (bf16[4,288,128]{2,1,0:T(8,128)(2,1)}, bf16[4,288,128]{2,1,0:T(8,128)(2,1)S(1)}, u32[]{:S(2)}, u32[]{:S(2)}) collective-permute-start(bf16[4,288,128]{2,1,0:T(8,128)(2,1)} %collective-permute-done.11.rest_14_), channel_id=1, source_target_pairs={{0,8},{8,0},{1,9},{9,1},{2,10},{10,2},{3,11},{11,3},{4,12},{12,4},... | collective-permute-start | bytes 884744 | tf_op jit(solution)/shard_map/ppermute | solution.py:384
  42.7 29.7 %copy-start = (bf16[1024,576]{0,1:T(8,128)(2,1)S(1)}, bf16[1024,576]{0,1:T(8,128)(2,1)}, u32[]{:S(2)}) copy-start(bf16[1024,576]{0,1:T(8,128)(2,1)} %copy.25) | copy-start | bytes 3538948
  42.8 29.7 %copy-start.1 = (bf16[1024,512]{0,1:T(8,128)(2,1)S(1)}, bf16[1024,512]{0,1:T(8,128)(2,1)}, u32[]{:S(2)}) copy-start(bf16[1024,512]{0,1:T(8,128)(2,1)} %copy.26) | copy-start | bytes 3145732
  43.2 1.7 %copy-start.10 = (bf16[4,288,128]{2,1,0:T(8,128)(2,1)}, bf16[4,288,128]{2,1,0:T(8,128)(2,1)S(1)}, u32[]{:S(2)}) copy-start(bf16[4,288,128]{2,1,0:T(8,128)(2,1)S(1)} %collective-permute-done.14.rest_5_) | copy-start | bytes 884740
  43.8 1.1 copy-start.11
  44.0 0.9 copy-start.12
  44.4 0.7 copy-start.13
  72.5 8.8 %copy-start.6 = (bf16[4,4,288,128]{3,2,1,0:T(8,128)(2,1)S(1)}, bf16[4,4,288,128]{3,2,1,0:T(8,128)(2,1)}, u32[]{:S(2)}) copy-start(bf16[4,4,288,128]{3,2,1,0:T(8,128)(2,1)} %get-tuple-element.39) | copy-start | bytes 3538948
  81.1 2.9 %collective-permute-start.24 = (bf16[4,4,288,128]{3,2,1,0:T(8,128)(2,1)S(1)}, bf16[4,4,288,128]{3,2,1,0:T(8,128)(2,1)S(1)}, u32[]{:S(2)}, u32[]{:S(2)}) collective-permute-start(bf16[4,4,288,128]{3,2,1,0:T(8,128)(2,1)S(1)} %get-tuple-element.43), channel_id=1, source_target_pairs={{0,8},{8,0},{1,9},{9,1},{2,10},{10,2},{3,11},{11,3},{4,12},{12,4},... | collective-permute-start | bytes 3538952 | tf_op jit(solution)/shard_map/ppermute | solution.py:384
  81.2 8.0 %collective-permute-start.20 = (bf16[4,4,288,128]{3,2,1,0:T(8,128)(2,1)S(1)}, bf16[4,4,288,128]{3,2,1,0:T(8,128)(2,1)S(1)}, u32[]{:S(2)}, u32[]{:S(2)}) collective-permute-start(bf16[4,4,288,128]{3,2,1,0:T(8,128)(2,1)S(1)} %copy-done.6), channel_id=1, source_target_pairs={{0,8},{8,0},{1,9},{9,1},{2,10},{10,2},{3,11},{11,3},{4,12},{12,4},... | collective-permute-start | bytes 3538952 | tf_op jit(solution)/shard_map/ppermute | solution.py:384
  85.9 3.4 %copy-start.4 = (bf16[4,4,288,128]{3,2,1,0:T(8,128)(2,1)S(1)}, bf16[4,4,288,128]{3,2,1,0:T(8,128)(2,1)}, u32[]{:S(2)}) copy-start(bf16[4,4,288,128]{3,2,1,0:T(8,128)(2,1)} %get-tuple-element.38) | copy-start | bytes 3538948
  85.9 16.7 %collective-permute-start.25 = (bf16[4,288,128]{2,1,0:T(8,128)(2,1)S(1)}, bf16[4,288,128]{2,1,0:T(8,128)(2,1)S(1)}, u32[]{:S(2)}, u32[]{:S(2)}) collective-permute-start(bf16[4,288,128]{2,1,0:T(8,128)(2,1)S(1)} %get-tuple-element.44), channel_id=1, source_target_pairs={{0,16},{16,32},{32,48},{48,0},{1,17},{17,33},{33,49},{49,1},{2,18}... | collective-permute-start | bytes 884744 | tf_op jit(solution)/shard_map/ppermute | solution.py:384
  86.5 26.5 %collective-permute-start.26 = (bf16[4,288,128]{2,1,0:T(8,128)(2,1)S(1)}, bf16[4,288,128]{2,1,0:T(8,128)(2,1)S(1)}, u32[]{:S(2)}, u32[]{:S(2)}) collective-permute-start(bf16[4,288,128]{2,1,0:T(8,128)(2,1)S(1)} %get-tuple-element.45), channel_id=1, source_target_pairs={{0,32},{16,48},{32,0},{48,16},{1,33},{17,49},{33,1},{49,17},{2,34}... | collective-permute-start | bytes 884744 | tf_op jit(solution)/shard_map/ppermute | solution.py:384
  87.6 25.4 %collective-permute-start.27 = (bf16[4,288,128]{2,1,0:T(8,128)(2,1)S(1)}, bf16[4,288,128]{2,1,0:T(8,128)(2,1)}, u32[]{:S(2)}, u32[]{:S(2)}) collective-permute-start(bf16[4,288,128]{2,1,0:T(8,128)(2,1)S(1)} %get-tuple-element.46), channel_id=1, source_target_pairs={{0,48},{16,0},{32,16},{48,32},{1,49},{17,1},{33,17},{49,33},{2,50}... | collective-permute-start | bytes 884744 | tf_op jit(solution)/shard_map/ppermute | solution.py:384
  91.2 23.0 %collective-permute-start.21 = (bf16[4,288,128]{2,1,0:T(8,128)(2,1)S(1)}, bf16[4,288,128]{2,1,0:T(8,128)(2,1)}, u32[]{:S(2)}, u32[]{:S(2)}) collective-permute-start(bf16[4,288,128]{2,1,0:T(8,128)(2,1)S(1)} %get-tuple-element.59), channel_id=1, source_target_pairs={{0,64},{64,128},{128,192},{192,0},{1,65},{65,129},{129,193},{193,1... | collective-permute-start | bytes 884744 | tf_op jit(solution)/shard_map/ppermute | solution.py:384
  92.1 22.2 %collective-permute-start.23 = (bf16[4,288,128]{2,1,0:T(8,128)(2,1)S(1)}, bf16[4,288,128]{2,1,0:T(8,128)(2,1)}, u32[]{:S(2)}, u32[]{:S(2)}) collective-permute-start(bf16[4,288,128]{2,1,0:T(8,128)(2,1)S(1)} %get-tuple-element.60), channel_id=1, source_target_pairs={{0,192},{64,0},{128,64},{192,128},{1,193},{65,1},{129,65},{193,129... | collective-permute-start | bytes 884744 | tf_op jit(solution)/shard_map/ppermute | solution.py:384
  102.6 11.7 %collective-permute-start.22 = (bf16[4,288,128]{2,1,0:T(8,128)(2,1)S(1)}, bf16[4,288,128]{2,1,0:T(8,128)(2,1)}, u32[]{:S(2)}, u32[]{:S(2)}) collective-permute-start(bf16[4,288,128]{2,1,0:T(8,128)(2,1)S(1)} %get-tuple-element.61), channel_id=1, source_target_pairs={{0,128},{64,192},{128,0},{192,64},{1,129},{65,193},{129,1},{193,65... | collective-permute-start | bytes 884744 | tf_op jit(solution)/shard_map/ppermute | solution.py:384
  115.8 6.7 %collective-permute-start.28 = (bf16[288,128]{1,0:T(8,128)(2,1)S(1)}, bf16[288,128]{1,0:T(8,128)(2,1)S(1)}, u32[]{:S(2)}, u32[]{:S(2)}) collective-permute-start(bf16[288,128]{1,0:T(8,128)(2,1)S(1)} %get-tuple-element.62), channel_id=1, source_target_pairs={{0,16},{16,32},{32,48},{48,0},{1,17},{17,33},{33,49},{49,1},{2,18}... | collective-permute-start | bytes 221192 | tf_op jit(solution)/shard_map/ppermute | solution.py:384
  115.9 8.2 %collective-permute-start.30 = (bf16[288,128]{1,0:T(8,128)(2,1)S(1)}, bf16[288,128]{1,0:T(8,128)(2,1)S(1)}, u32[]{:S(2)}, u32[]{:S(2)}) collective-permute-start(bf16[288,128]{1,0:T(8,128)(2,1)S(1)} %get-tuple-element.63), channel_id=1, source_target_pairs={{0,48},{16,0},{32,16},{48,32},{1,49},{17,1},{33,17},{49,33},{2,50}... | collective-permute-start | bytes 221192 | tf_op jit(solution)/shard_map/ppermute | solution.py:384
  119.1 5.9 %collective-permute-start.29 = (bf16[288,128]{1,0:T(8,128)(2,1)S(1)}, bf16[288,128]{1,0:T(8,128)(2,1)S(1)}, u32[]{:S(2)}, u32[]{:S(2)}) collective-permute-start(bf16[288,128]{1,0:T(8,128)(2,1)S(1)} %get-tuple-element.64), channel_id=1, source_target_pairs={{0,32},{16,48},{32,0},{48,16},{1,33},{17,49},{33,1},{49,17},{2,34}... | collective-permute-start | bytes 221192 | tf_op jit(solution)/shard_map/ppermute | solution.py:384
  119.2 6.0 %collective-permute-start.31 = (bf16[288,128]{1,0:T(8,128)(2,1)S(1)}, bf16[288,128]{1,0:T(8,128)(2,1)S(1)}, u32[]{:S(2)}, u32[]{:S(2)}) collective-permute-start(bf16[288,128]{1,0:T(8,128)(2,1)S(1)} %get-tuple-element.65), channel_id=1, source_target_pairs={{0,64},{64,128},{128,192},{192,0},{1,65},{65,129},{129,193},{193,1... | collective-permute-start | bytes 221192 | tf_op jit(solution)/shard_map/ppermute | solution.py:384
  120.6 4.6 %collective-permute-start.33 = (bf16[288,128]{1,0:T(8,128)(2,1)S(1)}, bf16[288,128]{1,0:T(8,128)(2,1)S(1)}, u32[]{:S(2)}, u32[]{:S(2)}) collective-permute-start(bf16[288,128]{1,0:T(8,128)(2,1)S(1)} %get-tuple-element.66), channel_id=1, source_target_pairs={{0,192},{64,0},{128,64},{192,128},{1,193},{65,1},{129,65},{193,129... | collective-permute-start | bytes 221192 | tf_op jit(solution)/shard_map/ppermute | solution.py:384
  122.5 5.9 %collective-permute-start.32 = (bf16[288,128]{1,0:T(8,128)(2,1)S(1)}, bf16[288,128]{1,0:T(8,128)(2,1)S(1)}, u32[]{:S(2)}, u32[]{:S(2)}) collective-permute-start(bf16[288,128]{1,0:T(8,128)(2,1)S(1)} %get-tuple-element.67), channel_id=1, source_target_pairs={{0,128},{64,192},{128,0},{192,64},{1,129},{65,193},{129,1},{193,65... | collective-permute-start | bytes 221192 | tf_op jit(solution)/shard_map/ppermute | solution.py:384
  (1 other events, 0.7 us)

commit v4 on v3

v4 whole, which is shorter than its diff:
```python
import functools
import math

import jax
import jax.numpy as jnp
from jax import lax
from jax.experimental import pallas as pl
from jax.experimental.pallas import tpu as pltpu
from jax.sharding import Mesh, PartitionSpec as P

LATENT = 512
ROPE = 64
WIDTH = LATENT + ROPE
HALF = WIDTH // 2
GROUP = 64
BLOCK = 256
PAIR = 2 * GROUP

score_scale = 192.0 ** (-0.5)
log2_scale = score_scale * math.log2(math.e)
neg_fill = -1e30

NT = (((1,), (1,)), ((), ()))


def mm(a, b):
    return jnp.dot(a, b, preferred_element_type=jnp.float32)


def twice(a):
    return jnp.concatenate([a, a], axis=1)


def on_chip(a):
    return pltpu.with_memory_space_constraint(a, pltpu.VMEM)


def visit(items, step, pair_step):
    step(0)

    def body(j, carry):
        pair_step(2 * j + 1, 2 * j + 2)
        return carry

    lax.fori_loop(0, (items - 1) // 2, body, 0)


def key_sums(order, place, q_cols, g_cols, tiles, weigh, *, sides, rows):
    groups = 4 * sides * sides
    blocks = groups * GROUP // BLOCK
    rank = (place[0] * sides + place[1]) * 2 + place[2]
    high_blocks = lax.div(order[2 * rank + 1], BLOCK // GROUP) + 1
    low_blocks = blocks + 1 - high_blocks

    def term(i, half):
        dscores, weights = weigh(i)
        at = half * rows
        from_scores = mm(q_cols[:, at : at + rows], dscores)
        from_values = mm(g_cols[:, at : at + rows], weights)
        return from_scores[:LATENT] + from_values, from_scores[LATENT:]

    def put(b, parts):
        at = pl.multiple_of(b * BLOCK, BLOCK)
        tiles[:LATENT, pl.ds(at, BLOCK)] = parts[0].astype(jnp.bfloat16)
        tiles[LATENT:, pl.ds(at, BLOCK)] = parts[1].astype(jnp.bfloat16)

    def both(b, carry):
        high = term(b, 1)
        low = term(high_blocks + b, 0)
        put(b, [h + l for h, l in zip(high, low)])
        return carry

    def two(j, carry):
        b = low_blocks + 1 + 2 * j
        first = term(b, 1)
        second = term(b + 1, 1)
        put(b, first)
        put(b + 1, second)
        return carry

    def clear(b, carry):
        at = pl.multiple_of(b * BLOCK, BLOCK)
        tiles[:, pl.ds(at, BLOCK)] = jnp.zeros((WIDTH, BLOCK), jnp.bfloat16)
        return carry

    lax.fori_loop(0, low_blocks, both, 0)
    put(low_blocks, term(low_blocks, 1))
    lax.fori_loop(0, lax.div(high_blocks - low_blocks - 1, 2), two, 0)
    lax.fori_loop(high_blocks, blocks, clear, 0)


def emit_tiles(order, place, tiles, keep, send, *, sides):
    groups = 4 * sides * sides
    my_x, my_y, my_c = place[0], place[1], place[2]
    lane = lax.broadcasted_iota(jnp.int32, (HALF, PAIR), 1)

    def pair(p):
        group = order[2 * p]
        odd = lax.rem(group, 2)
        low = lax.div(group, 2)
        high = lax.div(groups - 1 - group, 2)
        first = pl.multiple_of(jnp.where(odd == 1, high, low) * PAIR, PAIR)
        second = pl.multiple_of(jnp.where(odd == 1, low, high) * PAIR, PAIR)
        step_x = lax.rem(lax.div(p, 2 * sides) - my_x + sides, sides)
        step_y = lax.rem(lax.rem(lax.div(p, 2), sides) - my_y + sides, sides)
        for core, ref in ((1 - my_c, send), (my_c, keep)):
            at = pl.ds(pl.multiple_of(core * HALF, HALF), HALF)
            tile = jnp.where(
                lane < GROUP, tiles[at, pl.ds(first, PAIR)], tiles[at, pl.ds(second, PAIR)]
            )
            turned = jnp.concatenate([tile[:, GROUP:], tile[:, :GROUP]], axis=1)
            step1 = jnp.where(core == 0, step_x, step_y)
            step2 = jnp.where(core == 0, step_y, step_x)
            ref[step1, step2, lax.rem(p, 2)] = jnp.where(odd == 1, turned, tile)

    def body(j, carry):
        pair(2 * j)
        pair(2 * j + 1)
        return carry

    lax.fori_loop(0, sides * sides, body, 0)


def rows_kernel(q, g, o, q_rows, g_rows, q_cols, g_cols, deltas, mark):
    mark[...] = jnp.zeros(mark.shape, jnp.float32)
    tokens = q.shape[0] // 2
    heads = q.shape[1] // WIDTH
    for half in range(2):
        for head in range(heads):
            at = (half * heads + head) * tokens
            own = slice(half * tokens, half * tokens + tokens)
            grads = g[own, head * LATENT : (head + 1) * LATENT]
            saved = o[own, head * LATENT : (head + 1) * LATENT]
            q_rows[at : at + tokens, :] = q[own, head * WIDTH : (head + 1) * WIDTH]
            g_rows[at : at + tokens, :] = grads
            delta = jnp.sum(grads.astype(jnp.float32) * saved.astype(jnp.float32), axis=1, keepdims=True)
            deltas[at : at + tokens, :] = jnp.broadcast_to(delta, (tokens, 128))
    for at in range(0, 2 * heads * tokens, 128):
        q_cols[:, at : at + 128] = q_rows[at : at + 128, :].T
        g_cols[:, at : at + 128] = g_rows[at : at + 128, :].T


def run_rows(q, g, o):
    tokens = q.shape[0]
    rows = tokens * q.shape[1] // WIDTH
    bf16 = jnp.bfloat16
    vmem = pl.BlockSpec(memory_space=pltpu.VMEM)
    return pl.pallas_call(
        rows_kernel,
        out_shape=(
            pltpu.VMEM((rows, WIDTH), bf16),
            pltpu.VMEM((rows, LATENT), bf16),
            pltpu.VMEM((WIDTH, rows), bf16),
            pltpu.VMEM((LATENT, rows), bf16),
            pltpu.VMEM((rows, 128), jnp.float32),
            jax.ShapeDtypeStruct((8, 128), jnp.float32),
        ),
        in_specs=[vmem] * 3,
        out_specs=(vmem,) * 6,
        compiler_params=pltpu.CompilerParams(vmem_limit_bytes=32 * 1024 * 1024),
        cost_estimate=pl.CostEstimate(flops=1 << 20, bytes_accessed=24 << 20, transcendentals=0),
        name="latent_rows",
    )(q, g, o)


def grads_kernel(order, place, q_rows, g_rows, q_cols, g_cols, deltas, *rest, sides, rows):
    pieces = 2 * sides
    piece_refs = rest[:pieces]
    keys, dscores, keep, send = rest[pieces : pieces + 4]
    stage, scores, dweights, top, total, tiles, slot_of, sem = rest[pieces + 4 :]
    pairs = stage.shape[0]
    groups = 2 * pairs
    blocks = groups * GROUP // BLOCK
    items = blocks + 1
    my_x, my_y, my_c = place[0], place[1], place[2]
    rank = (my_x * sides + my_y) * 2 + my_c

    copies = []
    for at, ref in enumerate(piece_refs):
        step2 = at % sides
        holder = my_c if at < sides else 1 - my_c
        half = pl.multiple_of(holder * HALF, HALF)
        for step1 in range(sides):
            at_x = lax.rem(my_x + jnp.where(holder == 0, step2, step1), sides)
            at_y = lax.rem(my_y + jnp.where(holder == 0, step1, step2), sides)
            for step_c in range(2):
                pair = (at_x * sides + at_y) * 2 + lax.rem(holder + step_c, 2)
                copy = pltpu.make_async_copy(
                    ref.at[step1, step_c],
                    stage.at[pair, pl.ds(half, HALF)],
                    sem.at[(at * sides + step1) * 2 + step_c],
                )
                copy.start()
                copies.append(copy)

    def note(p, carry):
        slot_of[order[2 * p]] = p
        return carry

    lax.fori_loop(0, pairs, note, 0)
    top[...] = jnp.full(top.shape, neg_fill, jnp.float32)
    total[...] = jnp.zeros(total.shape, jnp.float32)
    for copy in copies:
        copy.wait()

    def place_low(j, carry):
        for i in (2 * j, 2 * j + 1):
            first = stage[slot_of[2 * i]]
            second = stage[slot_of[2 * i + 1]]
            at = pl.multiple_of(i * PAIR, PAIR)
            keys[:, pl.ds(at, PAIR)] = jnp.concatenate([first[:, :GROUP], second[:, :GROUP]], axis=1)
        return carry

    def place_high(j, carry):
        for i in (2 * j, 2 * j + 1):
            first = stage[slot_of[groups - 1 - 2 * i]]
            second = stage[slot_of[groups - 2 - 2 * i]]
            at = pl.multiple_of(i * PAIR, PAIR)
            keys[:, pl.ds(at, PAIR)] = jnp.concatenate([first[:, GROUP:], second[:, GROUP:]], axis=1)
        return carry

    lax.fori_loop(0, pairs // 4, place_low, 0)
    lax.fori_loop(pairs // 4, pairs // 2, place_high, 0)

    low_group = order[2 * rank]
    high_group = order[2 * rank + 1]
    high_blocks = lax.div(high_group, BLOCK // GROUP) + 1

    def score_step(i):
        is_low = (i >= high_blocks).astype(jnp.int32)
        block = i - is_low * high_blocks
        row0 = pl.multiple_of((1 - is_low) * rows, rows)
        key0 = pl.multiple_of(block * BLOCK, BLOCK)
        group = jnp.where(is_low == 1, low_group, high_group)
        key_tile = keys[:, pl.ds(key0, BLOCK)]
        raw = mm(q_rows[pl.ds(row0, rows), :], key_tile) * log2_scale
        dweights[i] = mm(g_rows[pl.ds(row0, rows), :], key_tile[:LATENT])
        token = lax.broadcasted_iota(jnp.int32, (rows, BLOCK), 0) % GROUP
        lane = lax.broadcasted_iota(jnp.int32, (rows, BLOCK), 1)
        visible = lane - token <= group * GROUP - block * BLOCK
        t = jnp.where(visible, raw, neg_fill)
        scores[i] = t
        left, right = t[:, : BLOCK // 2], t[:, BLOCK // 2 :]
        old_top = top[pl.ds(row0, rows), :]
        new_top = jnp.maximum(old_top, jnp.maximum(left, right))
        added = jnp.exp2(left - new_top) + jnp.exp2(right - new_top)
        total[pl.ds(row0, rows), :] = total[pl.ds(row0, rows), :] * jnp.exp2(old_top - new_top) + added
        top[pl.ds(row0, rows), :] = new_top

    def score_pair(i, j):
        score_step(i)
        score_step(j)

    visit(items, score_step, score_pair)

    lane_top = top[...]
    row_top = jnp.max(lane_top, axis=1, keepdims=True)
    row_sum = jnp.sum(total[...] * jnp.exp2(lane_top - row_top), axis=1, keepdims=True)
    top[...] = jnp.broadcast_to(row_top + jnp.log2(row_sum), top.shape)

    def weigh(i):
        row0 = pl.multiple_of((i < high_blocks).astype(jnp.int32) * rows, rows)
        w = jnp.exp2(scores[i] - twice(top[pl.ds(row0, rows), :]))
        ds = w * (dweights[i] - twice(deltas[pl.ds(row0, rows), :])) * score_scale
        ds = ds.astype(jnp.bfloat16)
        dscores[i] = ds
        return ds, w.astype(jnp.bfloat16)

    key_sums(order, place, q_cols, g_cols, tiles, weigh, sides=sides, rows=rows)
    emit_tiles(order, place, tiles, keep, send, sides=sides)


def query_kernel(order, place, dscores, keys, out, acc, *, sides, rows):
    items = dscores.shape[0]
    rank = (place[0] * sides + place[1]) * 2 + place[2]
    high_blocks = lax.div(order[2 * rank + 1], BLOCK // GROUP) + 1
    low_blocks = items - high_blocks
    acc[...] = jnp.zeros(acc.shape, jnp.float32)

    def term(i, key0):
        key0 = pl.multiple_of(key0, BLOCK)
        return lax.dot_general(
            dscores[i], keys[:, pl.ds(key0, BLOCK)], NT, preferred_element_type=jnp.float32
        )

    def high(j, carry):
        acc[rows:, :] += term(2 * j, 2 * j * BLOCK) + term(2 * j + 1, (2 * j + 1) * BLOCK)
        return carry

    def low(j, carry):
        i = high_blocks + 2 * j
        acc[:rows, :] += term(i, 2 * j * BLOCK) + term(i + 1, (2 * j + 1) * BLOCK)
        return carry

    lax.fori_loop(0, lax.div(high_blocks, 2), high, 0)
    lax.fori_loop(0, lax.div(low_blocks, 2), low, 0)
    odd_high = lax.rem(high_blocks, 2)
    row0 = pl.multiple_of(odd_high * rows, rows)
    block = jnp.where(odd_high == 1, high_blocks, low_blocks) - 1
    last = block + (1 - odd_high) * high_blocks
    acc[pl.ds(row0, rows), :] += term(last, block * BLOCK)

    tokens = out.shape[0] // 2
    heads = rows // tokens
    for half in range(2):
        for head in range(heads):
            at = (half * heads + head) * tokens
            out[half * tokens : (half + 1) * tokens, head * WIDTH : (head + 1) * WIDTH] = acc[
                at : at + tokens, :
            ].astype(jnp.bfloat16)


def run_grads(order, place, local, pieces, sides):
    rows = local[0].shape[0] // 2
    pairs = 2 * sides * sides
    items = pairs * PAIR // BLOCK + 1
    vmem = pl.BlockSpec(memory_space=pltpu.VMEM)
    smem = pl.BlockSpec(memory_space=pltpu.SMEM)
    hbm = pl.BlockSpec(memory_space=pl.ANY)
    bf16, f32 = jnp.bfloat16, jnp.float32
    part = jax.ShapeDtypeStruct((sides, sides, 2, HALF, PAIR), bf16)
    return pl.pallas_call(
        functools.partial(grads_kernel, sides=sides, rows=rows),
        out_shape=(
            pltpu.VMEM((WIDTH, pairs * PAIR), bf16),
            pltpu.VMEM((items, rows, BLOCK), bf16),
            part,
            part,
        ),
        in_specs=[smem, smem] + [vmem] * 5 + [hbm] * len(pieces),
        out_specs=(vmem,) * 4,
        scratch_shapes=[
            pltpu.VMEM((pairs, WIDTH, PAIR), bf16),
            pltpu.VMEM((items, rows, BLOCK), f32),
            pltpu.VMEM((items, rows, BLOCK), f32),
            pltpu.VMEM((2 * rows, 128), f32),
            pltpu.VMEM((2 * rows, 128), f32),
            pltpu.VMEM((WIDTH, pairs * PAIR), bf16),
            pltpu.SMEM((2 * pairs,), jnp.int32),
            pltpu.SemaphoreType.DMA((2 * pairs,)),
        ],
        compiler_params=pltpu.CompilerParams(vmem_limit_bytes=42 * 1024 * 1024),
        cost_estimate=pl.CostEstimate(
            flops=items * rows * BLOCK * 2 * 2176, bytes_accessed=24 << 20, transcendentals=0
        ),
        name="latent_grads",
    )(order, place, *[on_chip(a) for a in local], *pieces)


def run_queries(order, place, dscores, keys, sides, out_shape):
    items, rows = dscores.shape[:2]
    vmem = pl.BlockSpec(memory_space=pltpu.VMEM)
    smem = pl.BlockSpec(memory_space=pltpu.SMEM)
    return pl.pallas_call(
        functools.partial(query_kernel, sides=sides, rows=rows),
        out_shape=jax.ShapeDtypeStruct(out_shape, jnp.bfloat16),
        in_specs=[smem, smem, vmem, vmem],
        out_specs=vmem,
        scratch_shapes=[pltpu.VMEM((2 * rows, WIDTH), jnp.float32)],
        compiler_params=pltpu.CompilerParams(vmem_limit_bytes=24 * 1024 * 1024),
        cost_estimate=pl.CostEstimate(
            flops=items * rows * BLOCK * 2 * WIDTH, bytes_accessed=10 << 20, transcendentals=0
        ),
        name="latent_queries",
    )(order, place, on_chip(dscores), on_chip(keys))


def hop(a, sides, stage, step):
    moves = []
    for x in range(sides):
        for y in range(sides):
            for c in range(2):
                along_y = stage == c
                from_x = x if along_y else (x + step) % sides
                from_y = (y + step) % sides if along_y else y
                moves.append(((from_x * sides + from_y) * 2 + c, (x * sides + y) * 2 + c))
    return lax.ppermute(a, ("x", "y", "c"), moves)


def swap(a):
    return lax.ppermute(a, "c", [(0, 1), (1, 0)])


def shards(q_latent, kv_latent, out_grad, saved_out, group_order, *, sides, depth):
    my_c = lax.axis_index("c")
    place = jnp.stack([lax.axis_index("x"), lax.axis_index("y"), my_c]).astype(jnp.int32)

    own = kv_latent.T
    first, second = own[:HALF], own[HALF:]
    mine = jnp.where(my_c == 0, first, second)
    both = jnp.stack([mine, swap(jnp.where(my_c == 0, second, first))])
    line = jnp.stack([both] + [hop(both, sides, 0, d) for d in range(1, sides)])
    far = [hop(line, sides, 1, d) for d in range(1, sides)]
    *local, mark = run_rows(q_latent, out_grad, saved_out)
    far, mark = lax.optimization_barrier((far, mark))
    pieces = [line] + far
    pieces = pieces + [swap(piece) for piece in pieces]

    keys, dscores, keep, send = run_grads(group_order, place, local, pieces, sides)
    total = keep.astype(jnp.float32) + swap(send).astype(jnp.float32)
    low = [total[d].astype(jnp.bfloat16) for d in range(1, sides)]
    low, dscores = lax.optimization_barrier((low, dscores))
    q_grad = run_queries(group_order, place, dscores, keys, sides, q_latent.shape)
    total = total[0]
    for d in range(1, sides):
        total = total + hop(low[d - 1], sides, 1, -d).astype(jnp.float32)
    total, q_grad = lax.optimization_barrier((total, q_grad))
    low = [total[d].astype(jnp.bfloat16) for d in range(1, sides)]
    total = total[0]
    for d in range(1, sides):
        total = total + hop(low[d - 1], sides, 0, -d).astype(jnp.float32)

    each = PAIR // depth
    by_owner = total.reshape(2, HALF, depth, each).transpose(0, 2, 3, 1)
    by_owner = by_owner.reshape(2 * depth, each, HALF).astype(jnp.bfloat16)
    parts = lax.all_to_all(by_owner, ("c", "z"), 0, 0, tiled=True)
    parts = jnp.sum(parts.astype(jnp.float32).reshape(2, depth, each, HALF), axis=1)
    return q_grad, jnp.concatenate([parts[0], parts[1]], axis=1)


def solution(mesh):
    ctx, depth = mesh.shape["ctx"], mesh.shape["head"]
    sides = math.isqrt(ctx // 2)
    finer = Mesh(mesh.devices.reshape(sides, sides, 2, depth), ("x", "y", "c", "z"))
    ctx_axes = ("x", "y", "c")
    placed = (P(ctx_axes, "z"), P(ctx_axes, None), P(ctx_axes, "z"), P(ctx_axes, "z"), P())
    return jax.shard_map(
        functools.partial(shards, sides=sides, depth=depth),
        mesh=finer,
        in_specs=placed,
        out_specs=(P(ctx_axes, "z"), P(("x", "y", "c", "z"), None)),
        check_vma=False,
    )
```

time: 147 us -> 121 us (0.82)
  local copies, waits for them, and re-layouts: 20.1 us -> 2.81 us
  waiting for transfers between devices: 19 us -> 35.9 us
  starting transfers between devices: 37.7 us -> 21 us
  Pallas kernels: 42.2 us -> 36.8 us
  other arithmetic: 9.34 us -> 5.4 us
  blocking collectives: 16.3 us -> 18 us
    ppermute x34 -> x18, waiting for transfers between devices: 19 us -> 35.9 us  [the longest x12 30.1 us: hop(): return lax.ppermute(a, ('x', 'y', 'c'), moves)]
    ppermute x34 -> x18, starting transfers between devices: 37.7 us -> 21 us  [the longest x12 19.9 us: hop(): return lax.ppermute(a, ('x', 'y', 'c'), moves)]
    reshape x5 -> x0, local copies, waits for them, and re-layouts: 12.4 us -> none  [the longest x2 6.08 us: head_rows(): a = a.reshape(2, tokens // 2, heads, width).transpose(0, 2, 1, 3)]
    pallas_call x2, Pallas kernels: 35.2 us -> 29.4 us  [the longest x1 27.5 us: run_grads(): pl.pallas_call(functools.partial(grads_kernel, sides=sides, rows=rows), o...]
    add x2 -> x1, other arithmetic: 2.7 us -> 0.23 us  [shards(): total = total + hop(low[d - 1], sides, 1, -d).astype(jnp.float32)]
    transpose x4 -> x0, local copies, waits for them, and re-layouts: 2.18 us -> none  [the longest x2 1.37 us: head_rows(): a = a.reshape(2, tokens // 2, heads, width).transpose(0, 2, 1, 3)]
    mul x1 -> x0, other arithmetic: 1.8 us -> none  [shards(): out_grad.astype(jnp.float32) * saved_out.astype(jnp.float32)]
    all_to_all x1, blocking collectives: 16.3 us -> 18 us  [shards(): parts = lax.all_to_all(by_owner, ('c', 'z'), 0, 0, tiled=True)]
  transfers between devices with their start and end apart: 34 -> 18, of which waited for: 12 -> 12; matrix products, arithmetic and copies ran while one was open for 17% -> 0% of each run, Pallas kernels for 5% -> 8%
where the time goes in v4:
time: 121 us
  Pallas kernels  36.8 us (30%)
  waiting for transfers between devices  35.9 us (30%)
  starting transfers between devices  21 us (17%)
  blocking collectives  18 us (15%)
  other arithmetic  5.4 us (4%)
  local copies, waits for them, and re-layouts  2.81 us (2%)
    ppermute x12, waiting for transfers between devices, hop(): return lax.ppermute(a, ('x', 'y', 'c'), moves)  30.1 us
    pallas_call x1, Pallas kernels, run_grads(): pl.pallas_call(functools.partial(grads_kernel, sides=sides, rows=rows), o...  27.5 us
    ppermute x12, starting transfers between devices, hop(): return lax.ppermute(a, ('x', 'y', 'c'), moves)  19.9 us
    all_to_all x1, blocking collectives, shards(): parts = lax.all_to_all(by_owner, ('c', 'z'), 0, 0, tiled=True)  18 us
    pallas_call x1, Pallas kernels, run_queries(): pl.pallas_call(functools.partial(query_kernel, sides=sides, rows=rows), o...  7.49 us
    ppermute x6, waiting for transfers between devices, swap(): return lax.ppermute(a, 'c', [(0, 1), (1, 0)])  5.77 us
    another operation x2, other arithmetic  2.65 us
    unnamed x18, local copies, waits for them, and re-layouts  2.48 us
  transfers between devices with their start and end apart: 18, of which 12 were waited for; matrix products, arithmetic and copies ran while one was open for 0% of the time, Pallas kernels for 8%

profile of v4, /device:TPU:32, one launch (start us, length us, event | category | flops | bytes accessed | tf_op | source)
XLA Modules:
  0.0 120.8 jit_solution(10844306463882304588)
XLA Ops:
  0.6 1.0 select_bitcast_fusion
  1.7 0.1 collective-permute-start
  1.8 1.3 %collective-permute-done = bf16[288,128]{1,0:T(8,128)(2,1)S(1)} collective-permute-done((bf16[288,128]{1,0:T(8,128)(2,1)S(1)}, bf16[288,128]{1,0:T(8,128)(2,1)S(1)}, u32[]{:S(2)}, u32[]{:S(2)}) %collective-permute-start) | collective-permute-done | bytes 73760 | tf_op jit(solution)/shard_map/ppermute | solution.py:381
  3.1 3.3 %collective-permute-start.2 = (bf16[2,288,128]{2,1,0:T(8,128)(2,1)S(1)}, bf16[2,288,128]{2,1,0:T(8,128)(2,1)S(1)}, u32[]{:S(2)}, u32[]{:S(2)}) collective-permute-start(bf16[2,288,128]{2,1,0:T(8,128)(2,1)S(1)} %get-tuple-element.47), channel_id=1, source_target_pairs={{32,0},{136,8},{48,16},{152,24},{0,32},{168,40},{16,48},{184,56},{... | collective-permute-start | bytes 442376 | tf_op jit(solution)/shard_map/ppermute | solution.py:377
  6.3 1.1 collective-permute-start.1
  7.4 1.0 collective-permute-start.3
  8.4 1.4 %collective-permute-done.2 = bf16[2,288,128]{2,1,0:T(8,128)(2,1)S(1)} collective-permute-done((bf16[2,288,128]{2,1,0:T(8,128)(2,1)S(1)}, bf16[2,288,128]{2,1,0:T(8,128)(2,1)S(1)}, u32[]{:S(2)}, u32[]{:S(2)}) %collective-permute-start.2) | collective-permute-done | bytes 147488 | tf_op jit(solution)/shard_map/ppermute | solution.py:377
  9.8 1.9 %collective-permute-done.1 = bf16[2,288,128]{2,1,0:T(8,128)(2,1)S(1)} collective-permute-done((bf16[2,288,128]{2,1,0:T(8,128)(2,1)S(1)}, bf16[2,288,128]{2,1,0:T(8,128)(2,1)S(1)}, u32[]{:S(2)}, u32[]{:S(2)}) %collective-permute-start.1) | collective-permute-done | bytes 147488 | tf_op jit(solution)/shard_map/ppermute | solution.py:377
  11.7 2.0 %collective-permute-done.3 = bf16[2,288,128]{2,1,0:T(8,128)(2,1)S(1)} collective-permute-done((bf16[2,288,128]{2,1,0:T(8,128)(2,1)S(1)}, bf16[2,288,128]{2,1,0:T(8,128)(2,1)S(1)}, u32[]{:S(2)}, u32[]{:S(2)}) %collective-permute-start.3) | collective-permute-done | bytes 147488 | tf_op jit(solution)/shard_map/ppermute | solution.py:377
  13.7 0.1 pad_maximum_fusion.rest_0_
  13.8 0.0 copy-start.5
  13.8 1.6 %collective-permute-start.6 = (bf16[4,2,288,128]{3,2,1,0:T(8,128)(2,1)S(1)}, bf16[4,2,288,128]{3,2,1,0:T(8,128)(2,1)S(1)}, u32[]{:S(2)}, u32[]{:S(2)}) collective-permute-start(bf16[4,2,288,128]{3,2,1,0:T(8,128)(2,1)S(1)} %pad_maximum_fusion.rest_0_), channel_id=1, source_target_pairs={{192,0},{56,8},{208,16},{8,24},{224,32},{24,40},{240,48},{40,56},{... | collective-permute-start | bytes 1769480 | tf_op jit(solution)/shard_map/ppermute | solution.py:377
  15.4 2.7 %collective-permute-start.5 = (bf16[4,2,288,128]{3,2,1,0:T(8,128)(2,1)S(1)}, bf16[4,2,288,128]{3,2,1,0:T(8,128)(2,1)S(1)}, u32[]{:S(2)}, u32[]{:S(2)}) collective-permute-start(bf16[4,2,288,128]{3,2,1,0:T(8,128)(2,1)S(1)} %pad_maximum_fusion.rest_0_), channel_id=1, source_target_pairs={{128,0},{40,8},{144,16},{56,24},{160,32},{8,40},{176,48},{24,56},{... | collective-permute-start | bytes 1769480 | tf_op jit(solution)/shard_map/ppermute | solution.py:377
  18.1 1.4 %collective-permute-start.4 = (bf16[4,2,288,128]{3,2,1,0:T(8,128)(2,1)S(1)}, bf16[4,2,288,128]{3,2,1,0:T(8,128)(2,1)S(1)}, u32[]{:S(2)}, u32[]{:S(2)}) collective-permute-start(bf16[4,2,288,128]{3,2,1,0:T(8,128)(2,1)S(1)} %pad_maximum_fusion.rest_0_), channel_id=1, source_target_pairs={{64,0},{24,8},{80,16},{40,24},{96,32},{56,40},{112,48},{8,56},{128... | collective-permute-start | bytes 1769480 | tf_op jit(solution)/shard_map/ppermute | solution.py:377
  19.6 5.4 %collective-permute-done.6.rest_3_ = bf16[4,2,288,128]{3,2,1,0:T(8,128)(2,1)S(1)} collective-permute-done((bf16[4,2,288,128]{3,2,1,0:T(8,128)(2,1)S(1)}, bf16[4,2,288,128]{3,2,1,0:T(8,128)(2,1)S(1)}, u32[]{:S(2)}, u32[]{:S(2)}) %collective-permute-start.6) | collective-permute-done | bytes 589856 | tf_op jit(solution)/shard_map/ppermute | solution.py:377
  25.0 7.3 %collective-permute-done.5.rest_2_ = bf16[4,2,288,128]{3,2,1,0:T(8,128)(2,1)S(1)} collective-permute-done((bf16[4,2,288,128]{3,2,1,0:T(8,128)(2,1)S(1)}, bf16[4,2,288,128]{3,2,1,0:T(8,128)(2,1)S(1)}, u32[]{:S(2)}, u32[]{:S(2)}) %collective-permute-start.5) | collective-permute-done | bytes 589856 | tf_op jit(solution)/shard_map/ppermute | solution.py:377
  32.3 0.1 collective-permute-start.8
  32.4 0.5 collective-permute-start.9
  32.9 0.1 collective-permute-start.10
  33.0 1.2 %copy-done.1 = bf16[128,4096]{1,0:T(8,128)(2,1)S(1)} copy-done((bf16[128,4096]{1,0:T(8,128)(2,1)S(1)}, bf16[128,4096]{1,0:T(8,128)(2,1)}, u32[]{:S(2)}) %copy-start.1) | copy-done | bytes 1048600
  34.2 1.2 %copy-done.2 = bf16[128,4096]{1,0:T(8,128)(2,1)S(1)} copy-done((bf16[128,4096]{1,0:T(8,128)(2,1)S(1)}, bf16[128,4096]{1,0:T(8,128)(2,1)}, u32[]{:S(2)}) %copy-start.2) | copy-done | bytes 1048600
  35.5 1.8 %latent_rows.1 = (bf16[1024,576]{1,0:T(8,128)(2,1)S(1)}, bf16[1024,512]{1,0:T(8,128)(2,1)S(1)}, bf16[576,1024]{1,0:T(8,128)(2,1)S(1)}, bf16[512,1024]{1,0:T(8,12...) custom-call(bf16[128,4608]{1,0:T(8,128)(2,1)S(1)} %copy-done, bf16[128,4096]{1,0:T(8,128)(2,1)S(1)} %copy-done.1, ...), custom_call_target="tpu_custom_call" | custom-call | flops 1048576 | bytes 25165824 | tf_op jit(solution)/shard_map/latent_rows/pallas_call | solution.py:148
  37.3 0.6 pad_add_fusion.place
  37.9 0.0 collective-permute-done.7.rest_4_
  37.9 27.5 %latent_grads.1 = (bf16[576,4096]{1,0:T(8,128)(2,1)S(1)}, bf16[17,512,256]{2,1,0:T(8,128)(2,1)S(1)}, bf16[4,4,2,288,128]{4,3,2,1,0:T(8,128)(2,1)}, bf16[4,4,2,288,128]{4,3,2,1,0:T(8,128)(2,1)}) custom-call(s32[64]{0:T(128)} %order.3, s32[3]{0:T(128)} %pad_add_fusion.place, bf16[1024,576]{1,0:T(8,128)(2,1)S(1)} %get-tuple-element.20.q_rows, ...), custom_call_target="tpu_custom_call" | custom-call | flops 9697230848 | bytes 25165824 | tf_op jit(solution)/shard_map/latent_grads/pallas_call | solution.py:322
  65.5 0.3 collective-permute-start.11
  65.8 4.5 %collective-permute-done.11 = bf16[4,4,2,288,128]{4,3,2,1,0:T(8,128)(2,1)S(1)} collective-permute-done((bf16[4,4,2,288,128]{4,3,2,1,0:T(8,128)(2,1)}, bf16[4,4,2,288,128]{4,3,2,1,0:T(8,128)(2,1)S(1)}, u32[]{:S(2)}, u32[]{:S(2)}) %collective-permute-start.11) | collective-permute-done | bytes 2359328 | tf_op jit(solution)/shard_map/ppermute | solution.py:381
  70.3 2.6 %fusion.7 = (bf16[4,4,2,288,128]{4,3,2,1,0:T(8,128)(2,1)S(1)}, f32[4,4,2,288,128]{4,3,2,1,0:T(8,128)S(1)}) fusion(bf16[4,4,2,288,128]{4,3,2,1,0:T(8,128)(2,1)S(1)} %collective-permute-done.11, bf16[4,4,2,288,128]{4,3,2,1,0:T(8,128)(2,1)} %get-tuple-element.28), kind=kLoop, calls=%fused_computation.25 | loop fusion | flops 4718592 | bytes 11796480 | tf_op jit(solution)/shard_map/convert.6
  72.9 0.0 copy-start.3
  72.9 0.0 copy-start.4
  72.9 0.1 slice_bitcast_fusion.1
  73.0 2.0 %collective-permute-start.12 = (bf16[4,2,288,128]{3,2,1,0:T(8,128)(2,1)S(1)}, bf16[4,2,288,128]{3,2,1,0:T(8,128)(2,1)S(1)}, u32[]{:S(2)}, u32[]{:S(2)}) collective-permute-start(bf16[4,2,288,128]{3,2,1,0:T(8,128)(2,1)S(1)} %get-tuple-element.31), channel_id=1, source_target_pairs={{192,0},{56,8},{208,16},{8,24},{224,32},{24,40},{240,48},{40,56},{... | collective-permute-start | bytes 1769480 | tf_op jit(solution)/shard_map/ppermute | solution.py:377
  75.1 1.8 %collective-permute-start.13 = (bf16[4,2,288,128]{3,2,1,0:T(8,128)(2,1)S(1)}, bf16[4,2,288,128]{3,2,1,0:T(8,128)(2,1)S(1)}, u32[]{:S(2)}, u32[]{:S(2)}) collective-permute-start(bf16[4,2,288,128]{3,2,1,0:T(8,128)(2,1)S(1)} %get-tuple-element.32), channel_id=1, source_target_pairs={{128,0},{40,8},{144,16},{56,24},{160,32},{8,40},{176,48},{24,56},{... | collective-permute-start | bytes 1769480 | tf_op jit(solution)/shard_map/ppermute | solution.py:377
  76.9 1.7 %collective-permute-start.14 = (bf16[4,2,288,128]{3,2,1,0:T(8,128)(2,1)S(1)}, bf16[4,2,288,128]{3,2,1,0:T(8,128)(2,1)S(1)}, u32[]{:S(2)}, u32[]{:S(2)}) collective-permute-start(bf16[4,2,288,128]{3,2,1,0:T(8,128)(2,1)S(1)} %get-tuple-element.33), channel_id=1, source_target_pairs={{64,0},{24,8},{80,16},{40,24},{96,32},{56,40},{112,48},{8,56},{128... | collective-permute-start | bytes 1769480 | tf_op jit(solution)/shard_map/ppermute | solution.py:377
  78.6 7.5 %latent_queries.1 = bf16[128,4608]{1,0:T(8,128)(2,1)} custom-call(s32[64]{0:T(128)S(1)} %copy-done.4, s32[3]{0:T(128)S(1)} %copy-done.3, bf16[17,512,256]{2,1,0:T(8,128)(2,1)S(1)} %get-tuple-element.34.dscores, bf16[576,4096]{1,0:T(8,128)(2,1)S(1)} %get-tuple-element.35.keys), custom_call_target="tpu_custom_call" | custom-call | flops 2566914048 | bytes 10485760 | tf_op jit(solution)/shard_map/latent_queries/pallas_call | solution.py:354
  86.1 5.0 %collective-permute-done.13 = bf16[4,2,288,128]{3,2,1,0:T(8,128)(2,1)S(1)} collective-permute-done((bf16[4,2,288,128]{3,2,1,0:T(8,128)(2,1)S(1)}, bf16[4,2,288,128]{3,2,1,0:T(8,128)(2,1)S(1)}, u32[]{:S(2)}, u32[]{:S(2)}) %collective-permute-start.13) | collective-permute-done | bytes 589856 | tf_op jit(solution)/shard_map/ppermute | solution.py:377
  91.1 0.4 collective-permute-done.14
  91.4 0.2 fusion.2
  91.7 0.1 convert.12
  91.8 0.1 collective-permute-start.15
  91.9 3.2 %collective-permute-start.17 = (bf16[2,288,128]{2,1,0:T(8,128)(2,1)S(1)}, bf16[2,288,128]{2,1,0:T(8,128)(2,1)S(1)}, u32[]{:S(2)}, u32[]{:S(2)}) collective-permute-start(bf16[2,288,128]{2,1,0:T(8,128)(2,1)S(1)} %get-tuple-element.44), channel_id=1, source_target_pairs={{16,0},{72,8},{32,16},{88,24},{48,32},{104,40},{0,48},{120,56},{80... | collective-permute-start | bytes 442376 | tf_op jit(solution)/shard_map/ppermute | solution.py:377
  95.1 3.1 %collective-permute-done.15 = bf16[2,288,128]{2,1,0:T(8,128)(2,1)S(1)} collective-permute-done((bf16[2,288,128]{2,1,0:T(8,128)(2,1)S(1)}, bf16[2,288,128]{2,1,0:T(8,128)(2,1)S(1)}, u32[]{:S(2)}, u32[]{:S(2)}) %collective-permute-start.15) | collective-permute-done | bytes 147488 | tf_op jit(solution)/shard_map/ppermute | solution.py:377
  98.2 1.2 collective-permute-done.17
  99.4 2.4 %collective-permute-done.16 = bf16[2,288,128]{2,1,0:T(8,128)(2,1)S(1)} collective-permute-done((bf16[2,288,128]{2,1,0:T(8,128)(2,1)S(1)}, bf16[2,288,128]{2,1,0:T(8,128)(2,1)S(1)}, u32[]{:S(2)}, u32[]{:S(2)}) %collective-permute-start.16) | collective-permute-done | bytes 147488 | tf_op jit(solution)/shard_map/ppermute | solution.py:377
  101.8 0.1 fusion.5
  101.8 0.2 copy.7
  102.0 18.0 %all_to_all.5 = bf16[16,16,288]{2,1,0:T(8,128)(2,1)S(1)} all-to-all(bf16[16,16,288]{2,1,0:T(8,128)(2,1)S(1)} %bitcast.52), channel_id=1, replica_groups=mesh['x'=4,'y'=4,'c'=2,'z'=8] {'c','z'}, dimensions={0} | all-to-all | bytes 294912 | tf_op jit(solution)/shard_map/all_to_all | solution.py:416
  120.1 0.7 pad_maximum_fusion.2
  (24 shorter events, 0.1 us)
Async XLA Ops:
  0.6 32.4 %copy-start = (bf16[128,4608]{1,0:T(8,128)(2,1)S(1)}, bf16[128,4608]{1,0:T(8,128)(2,1)}, u32[]{:S(2)}) copy-start(bf16[128,4608]{1,0:T(8,128)(2,1)} %q.1) | copy-start | bytes 3538948
  1.7 1.4 %collective-permute-start = (bf16[288,128]{1,0:T(8,128)(2,1)S(1)}, bf16[288,128]{1,0:T(8,128)(2,1)S(1)}, u32[]{:S(2)}, u32[]{:S(2)}) collective-permute-start(bf16[288,128]{1,0:T(8,128)(2,1)S(1)} %get-tuple-element.49), channel_id=1, source_target_pairs={{0,8},{8,0},{1,9},{9,1},{2,10},{10,2},{3,11},{11,3},{4,12},{12,4},... | collective-permute-start | bytes 221192 | tf_op jit(solution)/shard_map/ppermute | solution.py:381
  3.1 6.7 %collective-permute-start.2 = (bf16[2,288,128]{2,1,0:T(8,128)(2,1)S(1)}, bf16[2,288,128]{2,1,0:T(8,128)(2,1)S(1)}, u32[]{:S(2)}, u32[]{:S(2)}) collective-permute-start(bf16[2,288,128]{2,1,0:T(8,128)(2,1)S(1)} %get-tuple-element.47), channel_id=1, source_target_pairs={{32,0},{136,8},{48,16},{152,24},{0,32},{168,40},{16,48},{184,56},{... | collective-permute-start | bytes 442376 | tf_op jit(solution)/shard_map/ppermute | solution.py:377
  6.3 5.4 %collective-permute-start.1 = (bf16[2,288,128]{2,1,0:T(8,128)(2,1)S(1)}, bf16[2,288,128]{2,1,0:T(8,128)(2,1)S(1)}, u32[]{:S(2)}, u32[]{:S(2)}) collective-permute-start(bf16[2,288,128]{2,1,0:T(8,128)(2,1)S(1)} %get-tuple-element.47), channel_id=1, source_target_pairs={{16,0},{72,8},{32,16},{88,24},{48,32},{104,40},{0,48},{120,56},{80... | collective-permute-start | bytes 442376 | tf_op jit(solution)/shard_map/ppermute | solution.py:377
  7.4 6.4 %collective-permute-start.3 = (bf16[2,288,128]{2,1,0:T(8,128)(2,1)S(1)}, bf16[2,288,128]{2,1,0:T(8,128)(2,1)S(1)}, u32[]{:S(2)}, u32[]{:S(2)}) collective-permute-start(bf16[2,288,128]{2,1,0:T(8,128)(2,1)S(1)} %get-tuple-element.47), channel_id=1, source_target_pairs={{48,0},{200,8},{0,16},{216,24},{16,32},{232,40},{32,48},{248,56},{... | collective-permute-start | bytes 442376 | tf_op jit(solution)/shard_map/ppermute | solution.py:377
  13.8 24.1 %copy-start.5 = (bf16[4,2,288,128]{3,2,1,0:T(8,128)(2,1)}, bf16[4,2,288,128]{3,2,1,0:T(8,128)(2,1)S(1)}, u32[]{:S(2)}) copy-start(bf16[4,2,288,128]{3,2,1,0:T(8,128)(2,1)S(1)} %pad_maximum_fusion.rest_0_) | copy-start | bytes 1769476
  13.8 11.2 %collective-permute-start.6 = (bf16[4,2,288,128]{3,2,1,0:T(8,128)(2,1)S(1)}, bf16[4,2,288,128]{3,2,1,0:T(8,128)(2,1)S(1)}, u32[]{:S(2)}, u32[]{:S(2)}) collective-permute-start(bf16[4,2,288,128]{3,2,1,0:T(8,128)(2,1)S(1)} %pad_maximum_fusion.rest_0_), channel_id=1, source_target_pairs={{192,0},{56,8},{208,16},{8,24},{224,32},{24,40},{240,48},{40,56},{... | collective-permute-start | bytes 1769480 | tf_op jit(solution)/shard_map/ppermute | solution.py:377
  15.4 16.9 %collective-permute-start.5 = (bf16[4,2,288,128]{3,2,1,0:T(8,128)(2,1)S(1)}, bf16[4,2,288,128]{3,2,1,0:T(8,128)(2,1)S(1)}, u32[]{:S(2)}, u32[]{:S(2)}) collective-permute-start(bf16[4,2,288,128]{3,2,1,0:T(8,128)(2,1)S(1)} %pad_maximum_fusion.rest_0_), channel_id=1, source_target_pairs={{128,0},{40,8},{144,16},{56,24},{160,32},{8,40},{176,48},{24,56},{... | collective-permute-start | bytes 1769480 | tf_op jit(solution)/shard_map/ppermute | solution.py:377
  18.1 14.2 %collective-permute-start.4 = (bf16[4,2,288,128]{3,2,1,0:T(8,128)(2,1)S(1)}, bf16[4,2,288,128]{3,2,1,0:T(8,128)(2,1)S(1)}, u32[]{:S(2)}, u32[]{:S(2)}) collective-permute-start(bf16[4,2,288,128]{3,2,1,0:T(8,128)(2,1)S(1)} %pad_maximum_fusion.rest_0_), channel_id=1, source_target_pairs={{64,0},{24,8},{80,16},{40,24},{96,32},{56,40},{112,48},{8,56},{128... | collective-permute-start | bytes 1769480 | tf_op jit(solution)/shard_map/ppermute | solution.py:377
  19.6 18.3 %collective-permute-start.7 = (bf16[4,2,288,128]{3,2,1,0:T(8,128)(2,1)S(1)}, bf16[4,2,288,128]{3,2,1,0:T(8,128)(2,1)}, u32[]{:S(2)}, u32[]{:S(2)}) collective-permute-start(bf16[4,2,288,128]{3,2,1,0:T(8,128)(2,1)S(1)} %pad_maximum_fusion.rest_0_), channel_id=1, source_target_pairs={{0,8},{8,0},{1,9},{9,1},{2,10},{10,2},{3,11},{11,3},{4,12},{12,4},... | collective-permute-start | bytes 1769480 | tf_op jit(solution)/shard_map/ppermute | solution.py:381
  25.0 12.9 %copy-start.6 = (bf16[4,2,288,128]{3,2,1,0:T(8,128)(2,1)}, bf16[4,2,288,128]{3,2,1,0:T(8,128)(2,1)S(1)}, u32[]{:S(2)}) copy-start(bf16[4,2,288,128]{3,2,1,0:T(8,128)(2,1)S(1)} %collective-permute-done.6.rest_3_) | copy-start | bytes 1769476
  32.3 5.6 %copy-start.7 = (bf16[4,2,288,128]{3,2,1,0:T(8,128)(2,1)}, bf16[4,2,288,128]{3,2,1,0:T(8,128)(2,1)S(1)}, u32[]{:S(2)}) copy-start(bf16[4,2,288,128]{3,2,1,0:T(8,128)(2,1)S(1)} %collective-permute-done.5.rest_2_) | copy-start | bytes 1769476
  32.3 5.6 %copy-start.8 = (bf16[4,2,288,128]{3,2,1,0:T(8,128)(2,1)}, bf16[4,2,288,128]{3,2,1,0:T(8,128)(2,1)S(1)}, u32[]{:S(2)}) copy-start(bf16[4,2,288,128]{3,2,1,0:T(8,128)(2,1)S(1)} %collective-permute-done.4.rest_1_) | copy-start | bytes 1769476
  32.3 5.6 %collective-permute-start.8 = (bf16[4,2,288,128]{3,2,1,0:T(8,128)(2,1)S(1)}, bf16[4,2,288,128]{3,2,1,0:T(8,128)(2,1)}, u32[]{:S(2)}, u32[]{:S(2)}) collective-permute-start(bf16[4,2,288,128]{3,2,1,0:T(8,128)(2,1)S(1)} %collective-permute-done.4.rest_1_), channel_id=1, source_target_pairs={{0,8},{8,0},{1,9},{9,1},{2,10},{10,2},{3,11},{11,3},{4,12},{12,4},... | collective-permute-start | bytes 1769480 | tf_op jit(solution)/shard_map/ppermute | solution.py:381
  32.4 5.5 %collective-permute-start.9 = (bf16[4,2,288,128]{3,2,1,0:T(8,128)(2,1)S(1)}, bf16[4,2,288,128]{3,2,1,0:T(8,128)(2,1)}, u32[]{:S(2)}, u32[]{:S(2)}) collective-permute-start(bf16[4,2,288,128]{3,2,1,0:T(8,128)(2,1)S(1)} %collective-permute-done.5.rest_2_), channel_id=1, source_target_pairs={{0,8},{8,0},{1,9},{9,1},{2,10},{10,2},{3,11},{11,3},{4,12},{12,4},... | collective-permute-start | bytes 1769480 | tf_op jit(solution)/shard_map/ppermute | solution.py:381
  32.9 5.0 %collective-permute-start.10 = (bf16[4,2,288,128]{3,2,1,0:T(8,128)(2,1)S(1)}, bf16[4,2,288,128]{3,2,1,0:T(8,128)(2,1)}, u32[]{:S(2)}, u32[]{:S(2)}) collective-permute-start(bf16[4,2,288,128]{3,2,1,0:T(8,128)(2,1)S(1)} %collective-permute-done.6.rest_3_), channel_id=1, source_target_pairs={{0,8},{8,0},{1,9},{9,1},{2,10},{10,2},{3,11},{11,3},{4,12},{12,4},... | collective-permute-start | bytes 1769480 | tf_op jit(solution)/shard_map/ppermute | solution.py:381
  33.0 1.2 %copy-start.1 = (bf16[128,4096]{1,0:T(8,128)(2,1)S(1)}, bf16[128,4096]{1,0:T(8,128)(2,1)}, u32[]{:S(2)}) copy-start(bf16[128,4096]{1,0:T(8,128)(2,1)} %g.1) | copy-start | bytes 3145732
  34.2 1.2 %copy-start.2 = (bf16[128,4096]{1,0:T(8,128)(2,1)S(1)}, bf16[128,4096]{1,0:T(8,128)(2,1)}, u32[]{:S(2)}) copy-start(bf16[128,4096]{1,0:T(8,128)(2,1)} %o.1) | copy-start | bytes 3145732
  65.5 4.8 %collective-permute-start.11 = (bf16[4,4,2,288,128]{4,3,2,1,0:T(8,128)(2,1)}, bf16[4,4,2,288,128]{4,3,2,1,0:T(8,128)(2,1)S(1)}, u32[]{:S(2)}, u32[]{:S(2)}) collective-permute-start(bf16[4,4,2,288,128]{4,3,2,1,0:T(8,128)(2,1)} %get-tuple-element.29), channel_id=1, source_target_pairs={{0,8},{8,0},{1,9},{9,1},{2,10},{10,2},{3,11},{11,3},{4,12},{12,4},... | collective-permute-start | bytes 7077896 | tf_op jit(solution)/shard_map/ppermute | solution.py:381
  72.9 5.7 %copy-start.3 = (s32[3]{0:T(128)S(1)}, s32[3]{0:T(128)}, u32[]{:S(2)}) copy-start(s32[3]{0:T(128)} %pad_add_fusion.place) | copy-start | bytes 40
  72.9 5.7 %copy-start.4 = (s32[64]{0:T(128)S(1)}, s32[64]{0:T(128)}, u32[]{:S(2)}) copy-start(s32[64]{0:T(128)} %order.3) | copy-start | bytes 772
  73.0 13.0 %collective-permute-start.12 = (bf16[4,2,288,128]{3,2,1,0:T(8,128)(2,1)S(1)}, bf16[4,2,288,128]{3,2,1,0:T(8,128)(2,1)S(1)}, u32[]{:S(2)}, u32[]{:S(2)}) collective-permute-start(bf16[4,2,288,128]{3,2,1,0:T(8,128)(2,1)S(1)} %get-tuple-element.31), channel_id=1, source_target_pairs={{192,0},{56,8},{208,16},{8,24},{224,32},{24,40},{240,48},{40,56},{... | collective-permute-start | bytes 1769480 | tf_op jit(solution)/shard_map/ppermute | solution.py:377
  75.1 16.0 %collective-permute-start.13 = (bf16[4,2,288,128]{3,2,1,0:T(8,128)(2,1)S(1)}, bf16[4,2,288,128]{3,2,1,0:T(8,128)(2,1)S(1)}, u32[]{:S(2)}, u32[]{:S(2)}) collective-permute-start(bf16[4,2,288,128]{3,2,1,0:T(8,128)(2,1)S(1)} %get-tuple-element.32), channel_id=1, source_target_pairs={{128,0},{40,8},{144,16},{56,24},{160,32},{8,40},{176,48},{24,56},{... | collective-permute-start | bytes 1769480 | tf_op jit(solution)/shard_map/ppermute | solution.py:377
  76.9 14.6 %collective-permute-start.14 = (bf16[4,2,288,128]{3,2,1,0:T(8,128)(2,1)S(1)}, bf16[4,2,288,128]{3,2,1,0:T(8,128)(2,1)S(1)}, u32[]{:S(2)}, u32[]{:S(2)}) collective-permute-start(bf16[4,2,288,128]{3,2,1,0:T(8,128)(2,1)S(1)} %get-tuple-element.33), channel_id=1, source_target_pairs={{64,0},{24,8},{80,16},{40,24},{96,32},{56,40},{112,48},{8,56},{128... | collective-permute-start | bytes 1769480 | tf_op jit(solution)/shard_map/ppermute | solution.py:377
  91.8 6.4 %collective-permute-start.15 = (bf16[2,288,128]{2,1,0:T(8,128)(2,1)S(1)}, bf16[2,288,128]{2,1,0:T(8,128)(2,1)S(1)}, u32[]{:S(2)}, u32[]{:S(2)}) collective-permute-start(bf16[2,288,128]{2,1,0:T(8,128)(2,1)S(1)} %get-tuple-element.43), channel_id=1, source_target_pairs={{48,0},{200,8},{0,16},{216,24},{16,32},{232,40},{32,48},{248,56},{... | collective-permute-start | bytes 442376 | tf_op jit(solution)/shard_map/ppermute | solution.py:377
  91.9 7.5 %collective-permute-start.17 = (bf16[2,288,128]{2,1,0:T(8,128)(2,1)S(1)}, bf16[2,288,128]{2,1,0:T(8,128)(2,1)S(1)}, u32[]{:S(2)}, u32[]{:S(2)}) collective-permute-start(bf16[2,288,128]{2,1,0:T(8,128)(2,1)S(1)} %get-tuple-element.44), channel_id=1, source_target_pairs={{16,0},{72,8},{32,16},{88,24},{48,32},{104,40},{0,48},{120,56},{80... | collective-permute-start | bytes 442376 | tf_op jit(solution)/shard_map/ppermute | solution.py:377
  95.1 6.6 %collective-permute-start.16 = (bf16[2,288,128]{2,1,0:T(8,128)(2,1)S(1)}, bf16[2,288,128]{2,1,0:T(8,128)(2,1)S(1)}, u32[]{:S(2)}, u32[]{:S(2)}) collective-permute-start(bf16[2,288,128]{2,1,0:T(8,128)(2,1)S(1)} %get-tuple-element.45), channel_id=1, source_target_pairs={{32,0},{136,8},{48,16},{152,24},{0,32},{168,40},{16,48},{184,56},{... | collective-permute-start | bytes 442376 | tf_op jit(solution)/shard_map/ppermute | solution.py:377

commit v5 on v4

v5 whole, which is shorter than its diff:
```python
import functools
import math

import jax
import jax.numpy as jnp
from jax import lax
from jax.experimental import pallas as pl
from jax.experimental.pallas import tpu as pltpu
from jax.sharding import Mesh, PartitionSpec as P

LATENT = 512
ROPE = 64
WIDTH = LATENT + ROPE
HALF = WIDTH // 2
GROUP = 64
BLOCK = 256
PAIR = 2 * GROUP

score_scale = 192.0 ** (-0.5)
log2_scale = score_scale * math.log2(math.e)
neg_fill = -1e30

NT = (((1,), (1,)), ((), ()))


def mm(a, b):
    return jnp.dot(a, b, preferred_element_type=jnp.float32)


def twice(a):
    return jnp.concatenate([a, a], axis=1)


def on_chip(a):
    return pltpu.with_memory_space_constraint(a, pltpu.VMEM)


def here():
    return lax.axis_index("x"), lax.axis_index("y"), lax.axis_index("c")


def own_kernel(order, keys, mine, theirs, *, sides):
    my_x, my_y, my_c = here()
    odd = lax.rem(order[2 * ((my_x * sides + my_y) * 2 + my_c)], 2)
    tile = keys[...]
    turned = jnp.concatenate([tile[:, GROUP:], tile[:, :GROUP]], axis=1)
    tile = jnp.where(odd == 1, turned, tile)
    mine[...] = jnp.where(my_c == 0, tile[:HALF], tile[HALF:])
    theirs[...] = jnp.where(my_c == 0, tile[HALF:], tile[:HALF])


def run_own(order, keys, sides):
    half = jax.ShapeDtypeStruct((HALF, PAIR), jnp.bfloat16)
    vmem = pl.BlockSpec(memory_space=pltpu.VMEM)
    return pl.pallas_call(
        functools.partial(own_kernel, sides=sides),
        out_shape=(half, half),
        in_specs=[pl.BlockSpec(memory_space=pltpu.SMEM), vmem],
        out_specs=(vmem, vmem),
        name="latent_own",
    )(order, keys)


def owner_kernel(order, first, *rest, sides):
    parts, out = rest[:-1], rest[-1]
    my_x, my_y, _ = here()
    for core in range(2):
        total = first[core]
        for part in parts:
            total = total + part[core].astype(jnp.float32)
        odd = lax.rem(order[2 * ((my_x * sides + my_y) * 2 + core)], 2)
        turned = jnp.concatenate([total[:, GROUP:], total[:, :GROUP]], axis=1)
        total = jnp.where(odd == 1, turned, total)
        out[core * PAIR : (core + 1) * PAIR, :] = total.astype(jnp.bfloat16).T


def run_owner(order, first, parts, sides):
    vmem = pl.BlockSpec(memory_space=pltpu.VMEM)
    return pl.pallas_call(
        functools.partial(owner_kernel, sides=sides),
        out_shape=jax.ShapeDtypeStruct((2 * PAIR, HALF), jnp.bfloat16),
        in_specs=[pl.BlockSpec(memory_space=pltpu.SMEM)] + [vmem] * (1 + len(parts)),
        out_specs=vmem,
        name="latent_owner",
    )(order, *[on_chip(a) for a in (first, *parts)])


def key_sums(order, q_cols, g_cols, slot_of, keep, send, weigh, *, sides, rows):
    groups = 4 * sides * sides
    per_block = BLOCK // GROUP
    blocks = groups // per_block
    my_x, my_y, my_c = here()
    rank = (my_x * sides + my_y) * 2 + my_c
    high_blocks = lax.div(order[2 * rank + 1], per_block) + 1
    low_blocks = blocks + 1 - high_blocks

    def term(i, half):
        dscores, weights = weigh(i)
        at = half * rows
        return mm(q_cols[:, at : at + rows], dscores) + mm(g_cols[:, at : at + rows], weights)

    def put(b, tile):
        tile = tile.astype(jnp.bfloat16)
        for j in range(per_block):
            p = slot_of[b * per_block + j]
            step_x = lax.rem(lax.div(p, 2 * sides) - my_x + sides, sides)
            step_y = lax.rem(lax.rem(lax.div(p, 2), sides) - my_y + sides, sides)
            step1 = jnp.where(my_c == 0, step_x, step_y)
            step2 = jnp.where(my_c == 0, step_y, step_x)
            core = lax.rem(p, 2)
            lanes = pl.ds(j % 2 * GROUP, GROUP)
            keep[step1, step2, core, :, lanes] = tile[:HALF, j * GROUP : (j + 1) * GROUP]
            send[step2, step1, core, :, lanes] = tile[HALF:, j * GROUP : (j + 1) * GROUP]

    def both(b, carry):
        high = term(b, 1)
        put(b, high + term(high_blocks + b, 0))
        return carry

    def two(j, carry):
        b = low_blocks + 1 + 2 * j
        first = term(b, 1)
        second = term(b + 1, 1)
        put(b, first)
        put(b + 1, second)
        return carry

    def clear(b, carry):
        put(b, jnp.zeros((WIDTH, BLOCK), jnp.float32))
        return carry

    lax.fori_loop(0, low_blocks, both, 0)
    put(low_blocks, term(low_blocks, 1))
    lax.fori_loop(0, lax.div(high_blocks - low_blocks - 1, 2), two, 0)
    lax.fori_loop(high_blocks, blocks, clear, 0)


def spread_rows(core, q, g, o, q_rows, g_rows, q_cols, g_cols, deltas):
    tokens = q.shape[0] // 2
    heads = q.shape[1] // WIDTH
    for half in range(2):
        for head in range(heads):
            at = (half * heads + head) * tokens
            own = slice(half * tokens, half * tokens + tokens)
            grads = g[own, head * LATENT : (head + 1) * LATENT]
            saved = o[own, head * LATENT : (head + 1) * LATENT]
            q_rows[at : at + tokens, :] = q[own, head * WIDTH : (head + 1) * WIDTH]
            g_rows[at : at + tokens, :] = grads
            delta = jnp.sum(grads.astype(jnp.float32) * saved.astype(jnp.float32), axis=1, keepdims=True)
            deltas[at : at + tokens, :] = jnp.broadcast_to(delta, (tokens, 128))
    first = pl.multiple_of(core * HALF, HALF)
    second = pl.multiple_of((1 - core) * HALF, HALF)
    g_cols[pl.ds(second, HALF), :] = jnp.zeros((HALF, g_cols.shape[1]), jnp.bfloat16)
    for at in range(0, 2 * heads * tokens, 128):
        q_turned = q_rows[at : at + 128, :].T
        g_turned = g_rows[at : at + 128, :].T
        q_cols[pl.ds(first, HALF), at : at + 128] = q_turned[:HALF]
        q_cols[pl.ds(second, HALF), at : at + 128] = q_turned[HALF:]
        g_cols[pl.ds(first, HALF), at : at + 128] = g_turned[:HALF]
        g_cols[pl.ds(second, LATENT - HALF), at : at + 128] = g_turned[HALF:]


def grads_kernel(order, q_in, g_in, o_in, *rest, sides, rows):
    pieces = 2 * sides
    piece_refs = rest[:pieces]
    keys, dscores, keep, send = rest[pieces : pieces + 4]
    (
            scores, dweights, top, total, q, g, o, q_rows, g_rows, q_cols, g_cols,
        deltas, slot_of, own_sem,
    ) = rest[pieces + 4 :]
    pairs = keys.shape[1] // PAIR
    groups = 2 * pairs
    blocks = groups * GROUP // BLOCK
    items = blocks + 1
    my_x, my_y, my_c = here()
    rank = (my_x * sides + my_y) * 2 + my_c

    own = [
        pltpu.make_async_copy(src, dst, own_sem.at[at])
        for at, (src, dst) in enumerate([(q_in, q), (g_in, g), (o_in, o)])
    ]
    for copy in own:
        copy.start()
    def note(p, carry):
        slot_of[order[2 * p]] = p
        slot_of[order[2 * p + 1]] = p
        return carry

    lax.fori_loop(0, pairs, note, 0)
    top[...] = jnp.full(top.shape, neg_fill, jnp.float32)
    total[...] = jnp.zeros(total.shape, jnp.float32)

    for at, ref in enumerate(piece_refs):
        step2 = at % sides
        holder = my_c if at < sides else 1 - my_c
        half = pl.ds(pl.multiple_of(holder * HALF, HALF), HALF)
        for step1 in range(sides):
            at_x = lax.rem(my_x + jnp.where(holder == 0, step2, step1), sides)
            at_y = lax.rem(my_y + jnp.where(holder == 0, step1, step2), sides)
            for step_c in range(2):
                pair = (at_x * sides + at_y) * 2 + lax.rem(holder + step_c, 2)
                tile = ref[step1, step_c]
                turn = lax.rem(order[2 * pair], 2)
                even = lax.div(order[2 * pair + turn], 2) * PAIR
                odd = lax.div(order[2 * pair + 1 - turn], 2) * PAIR
                evens = keys.at[half, pl.ds(pl.multiple_of(even, PAIR), PAIR)]
                odds = keys.at[half, pl.ds(pl.multiple_of(odd, PAIR), PAIR)]
                evens[:, :GROUP] = tile[:, :GROUP]
                odds[:, GROUP:] = tile[:, GROUP:]
    for copy in own:
        copy.wait()
    spread_rows(my_c, q, g, o, q_rows, g_rows, q_cols, g_cols, deltas)

    low_group = order[2 * rank]
    high_group = order[2 * rank + 1]
    high_blocks = lax.div(high_group, BLOCK // GROUP) + 1

    def score_step(i, diagonal=False):
        is_low = (i >= high_blocks).astype(jnp.int32)
        block = i - is_low * high_blocks
        row0 = pl.multiple_of((1 - is_low) * rows, rows)
        key0 = pl.multiple_of(block * BLOCK, BLOCK)
        key_tile = keys[:, pl.ds(key0, BLOCK)]
        t = mm(q_rows[pl.ds(row0, rows), :], key_tile) * log2_scale
        dweights[i] = mm(g_rows[pl.ds(row0, rows), :], key_tile[:LATENT])
        if diagonal:
            group = jnp.where(is_low == 1, low_group, high_group)
            token = lax.broadcasted_iota(jnp.int32, (rows, BLOCK), 0) % GROUP
            lane = lax.broadcasted_iota(jnp.int32, (rows, BLOCK), 1)
            t = jnp.where(lane - token <= group * GROUP - block * BLOCK, t, neg_fill)
        scores[i] = t
        left, right = t[:, : BLOCK // 2], t[:, BLOCK // 2 :]
        old_top = top[pl.ds(row0, rows), :]
        new_top = jnp.maximum(old_top, jnp.maximum(left, right))
        added = jnp.exp2(left - new_top) + jnp.exp2(right - new_top)
        total[pl.ds(row0, rows), :] = total[pl.ds(row0, rows), :] * jnp.exp2(old_top - new_top) + added
        top[pl.ds(row0, rows), :] = new_top

    def whole(k):
        score_step(k + (k >= high_blocks - 1).astype(jnp.int32))

    def whole_pair(j, carry):
        whole(2 * j + 1)
        whole(2 * j + 2)
        return carry

    score_step(high_blocks - 1, diagonal=True)
    score_step(jnp.int32(items - 1), diagonal=True)
    whole(jnp.int32(0))
    lax.fori_loop(0, (items - 3) // 2, whole_pair, 0)

    lane_top = top[...]
    row_top = jnp.max(lane_top, axis=1, keepdims=True)
    row_sum = jnp.sum(total[...] * jnp.exp2(lane_top - row_top), axis=1, keepdims=True)
    top[...] = jnp.broadcast_to(row_top + jnp.log2(row_sum), top.shape)

    def weigh(i):
        row0 = pl.multiple_of((i < high_blocks).astype(jnp.int32) * rows, rows)
        w = jnp.exp2(scores[i] - twice(top[pl.ds(row0, rows), :]))
        ds = w * (dweights[i] - twice(deltas[pl.ds(row0, rows), :])) * score_scale
        ds = ds.astype(jnp.bfloat16)
        dscores[i] = ds
        return ds, w.astype(jnp.bfloat16)

    key_sums(
        order, q_cols, g_cols, slot_of, keep, send, weigh, sides=sides, rows=rows
    )


def query_kernel(order, dscores, keys, out, acc, *, sides, rows):
    items = dscores.shape[0]
    my_x, my_y, my_c = here()
    rank = (my_x * sides + my_y) * 2 + my_c
    high_blocks = lax.div(order[2 * rank + 1], BLOCK // GROUP) + 1
    low_blocks = items - high_blocks
    acc[...] = jnp.zeros(acc.shape, jnp.float32)

    def term(i, key0):
        key0 = pl.multiple_of(key0, BLOCK)
        return lax.dot_general(
            dscores[i], keys[:, pl.ds(key0, BLOCK)], NT, preferred_element_type=jnp.float32
        )

    def high(j, carry):
        acc[rows:, :] += term(2 * j, 2 * j * BLOCK) + term(2 * j + 1, (2 * j + 1) * BLOCK)
        return carry

    def low(j, carry):
        i = high_blocks + 2 * j
        acc[:rows, :] += term(i, 2 * j * BLOCK) + term(i + 1, (2 * j + 1) * BLOCK)
        return carry

    lax.fori_loop(0, lax.div(high_blocks, 2), high, 0)
    lax.fori_loop(0, lax.div(low_blocks, 2), low, 0)
    odd_high = lax.rem(high_blocks, 2)
    row0 = pl.multiple_of(odd_high * rows, rows)
    block = jnp.where(odd_high == 1, high_blocks, low_blocks) - 1
    last = block + (1 - odd_high) * high_blocks
    acc[pl.ds(row0, rows), :] += term(last, block * BLOCK)

    tokens = out.shape[0] // 2
    heads = rows // tokens
    for half in range(2):
        for head in range(heads):
            at = (half * heads + head) * tokens
            out[half * tokens : (half + 1) * tokens, head * WIDTH : (head + 1) * WIDTH] = acc[
                at : at + tokens, :
            ].astype(jnp.bfloat16)


def run_grads(order, q, g, o, pieces, sides):
    rows = q.shape[0] * q.shape[1] // WIDTH // 2
    pairs = 2 * sides * sides
    items = pairs * PAIR // BLOCK + 1
    vmem = pl.BlockSpec(memory_space=pltpu.VMEM)
    smem = pl.BlockSpec(memory_space=pltpu.SMEM)
    hbm = pl.BlockSpec(memory_space=pl.ANY)
    bf16, f32 = jnp.bfloat16, jnp.float32
    part = pltpu.VMEM((sides, sides, 2, HALF, PAIR), bf16)
    return pl.pallas_call(
        functools.partial(grads_kernel, sides=sides, rows=rows),
        out_shape=(
            pltpu.VMEM((WIDTH, pairs * PAIR), bf16),
            pltpu.VMEM((items, rows, BLOCK), bf16),
            part,
            part,
        ),
        in_specs=[smem] + [hbm] * 3 + [vmem] * len(pieces),
        out_specs=(vmem,) * 4,
        scratch_shapes=[
            pltpu.VMEM((items, rows, BLOCK), f32),
            pltpu.VMEM((items, rows, BLOCK), f32),
            pltpu.VMEM((2 * rows, 128), f32),
            pltpu.VMEM((2 * rows, 128), f32),
            pltpu.VMEM(q.shape, bf16),
            pltpu.VMEM(g.shape, bf16),
            pltpu.VMEM(o.shape, bf16),
            pltpu.VMEM((2 * rows, WIDTH), bf16),
            pltpu.VMEM((2 * rows, LATENT), bf16),
            pltpu.VMEM((WIDTH, 2 * rows), bf16),
            pltpu.VMEM((WIDTH, 2 * rows), bf16),
            pltpu.VMEM((2 * rows, 128), f32),
            pltpu.SMEM((2 * pairs,), jnp.int32),
            pltpu.SemaphoreType.DMA((3,)),
        ],
        compiler_params=pltpu.CompilerParams(vmem_limit_bytes=38 * 1024 * 1024),
        cost_estimate=pl.CostEstimate(
            flops=items * rows * BLOCK * 2 * 2176, bytes_accessed=24 << 20, transcendentals=0
        ),
        name="latent_grads",
    )(order, q, g, o, *[on_chip(a) for a in pieces])


def run_queries(order, dscores, keys, sides, out_shape):
    items, rows = dscores.shape[:2]
    vmem = pl.BlockSpec(memory_space=pltpu.VMEM)
    smem = pl.BlockSpec(memory_space=pltpu.SMEM)
    return pl.pallas_call(
        functools.partial(query_kernel, sides=sides, rows=rows),
        out_shape=jax.ShapeDtypeStruct(out_shape, jnp.bfloat16),
        in_specs=[smem, vmem, vmem],
        out_specs=vmem,
        scratch_shapes=[pltpu.VMEM((2 * rows, WIDTH), jnp.float32)],
        compiler_params=pltpu.CompilerParams(vmem_limit_bytes=24 * 1024 * 1024),
        cost_estimate=pl.CostEstimate(
            flops=items * rows * BLOCK * 2 * WIDTH, bytes_accessed=10 << 20, transcendentals=0
        ),
        name="latent_queries",
    )(order, on_chip(dscores), on_chip(keys))


def hop(a, sides, stage, step):
    moves = []
    for x in range(sides):
        for y in range(sides):
            for c in range(2):
                along_y = stage == c
                from_x = x if along_y else (x + step) % sides
                from_y = (y + step) % sides if along_y else y
                moves.append(((from_x * sides + from_y) * 2 + c, (x * sides + y) * 2 + c))
    return lax.ppermute(a, ("x", "y", "c"), moves)


def swap(a):
    return lax.ppermute(a, "c", [(0, 1), (1, 0)])


def shards(q_latent, kv_latent, out_grad, saved_out, group_order, *, sides, depth):
    mine, theirs = run_own(group_order, kv_latent.T, sides)
    both = jnp.stack([mine, swap(theirs)])
    line = jnp.stack([both] + [hop(both, sides, 0, d) for d in range(1, sides)])
    far = [hop(line, sides, 1, d) for d in range(1, sides)]
    pieces = [line] + far
    pieces = pieces + [swap(piece) for piece in pieces]

    keys, dscores, keep, send = run_grads(
        group_order, q_latent, out_grad, saved_out, pieces, sides
    )
    total = keep.astype(jnp.float32) + swap(send).astype(jnp.float32)
    low = [total[d].astype(jnp.bfloat16) for d in range(1, sides)]
    low, dscores = lax.optimization_barrier((low, dscores))
    q_grad = run_queries(group_order, dscores, keys, sides, q_latent.shape)
    total = total[0]
    for d in range(1, sides):
        total = total + hop(low[d - 1], sides, 1, -d).astype(jnp.float32)
    total, q_grad = lax.optimization_barrier((total, q_grad))
    low = [total[d].astype(jnp.bfloat16) for d in range(1, sides)]
    parts = [hop(low[d - 1], sides, 0, -d) for d in range(1, sides)]
    each = PAIR // depth
    by_owner = run_owner(group_order, total[0], parts, sides).reshape(2 * depth, each, HALF)
    parts = lax.all_to_all(by_owner, ("c", "z"), 0, 0, tiled=True)
    parts = jnp.sum(parts.astype(jnp.float32).reshape(2, depth, each, HALF), axis=1)
    return q_grad, jnp.concatenate([parts[0], parts[1]], axis=1)


def solution(mesh):
    ctx, depth = mesh.shape["ctx"], mesh.shape["head"]
    sides = math.isqrt(ctx // 2)
    finer = Mesh(mesh.devices.reshape(sides, sides, 2, depth), ("x", "y", "c", "z"))
    ctx_axes = ("x", "y", "c")
    placed = (P(ctx_axes, "z"), P(ctx_axes, None), P(ctx_axes, "z"), P(ctx_axes, "z"), P())
    return jax.shard_map(
        functools.partial(shards, sides=sides, depth=depth),
        mesh=finer,
        in_specs=placed,
        out_specs=(P(ctx_axes, "z"), P(("x", "y", "c", "z"), None)),
        check_vma=False,
    )
```

time: 121 us -> 112 us (0.926)
  Pallas kernels: 36.8 us -> 31.5 us
  waiting for transfers between devices: 35.9 us -> 39.2 us
  local copies, waits for them, and re-layouts: 2.81 us -> 0.18 us
  other arithmetic: 5.4 us -> 2.93 us
  starting transfers between devices: 21 us -> 18.6 us
    pallas_call x1, Pallas kernels: 27.5 us -> 20.8 us  [run_grads(): pl.pallas_call(functools.partial(grads_kernel, sides=sides, rows=rows), o...]
    another operation x4 -> x2, other arithmetic: 4.27 us -> 0.99 us
    unnamed x18 -> x2, local copies, waits for them, and re-layouts: 2.48 us -> 0.01 us
    ppermute x6, waiting for transfers between devices: 5.77 us -> 8.21 us  [swap(): return lax.ppermute(a, 'c', [(0, 1), (1, 0)])]
    ppermute x12, starting transfers between devices: 19.9 us -> 17.9 us  [hop(): return lax.ppermute(a, ('x', 'y', 'c'), moves)]
    pallas_call x1 -> x2, Pallas kernels: 1.82 us -> 3.24 us  [the longest x1 1.69 us: run_own(): pl.pallas_call(functools.partial(own_kernel, sides=sides), out_shape=(hal...]
  transfers between devices with their start and end apart: 18 -> 18, of which waited for: 12 -> 14; matrix products, arithmetic and copies ran while one was open for 0% -> 0% of each run, Pallas kernels for 8% -> 7%
where the time goes in v5:
time: 112 us; the launch traced here: 111 us
  waiting for transfers between devices  39.2 us (35%)
  Pallas kernels  31.5 us (28%)
  starting transfers between devices  18.6 us (17%)
  blocking collectives  18.2 us (16%)
  other arithmetic  2.93 us (3%)
    ppermute x12, waiting for transfers between devices, hop(): return lax.ppermute(a, ('x', 'y', 'c'), moves)  31 us
    pallas_call x1, Pallas kernels, run_grads(): pl.pallas_call(functools.partial(grads_kernel, sides=sides, rows=rows), o...  20.8 us
    all_to_all x1, blocking collectives, shards(): parts = lax.all_to_all(by_owner, ('c', 'z'), 0, 0, tiled=True)  18.2 us
    ppermute x12, starting transfers between devices, hop(): return lax.ppermute(a, ('x', 'y', 'c'), moves)  17.9 us
    ppermute x6, waiting for transfers between devices, swap(): return lax.ppermute(a, 'c', [(0, 1), (1, 0)])  8.21 us
    pallas_call x1, Pallas kernels, run_queries(): pl.pallas_call(functools.partial(query_kernel, sides=sides, rows=rows), o...  7.48 us
  transfers between devices with their start and end apart: 18, of which 14 were waited for; matrix products, arithmetic and copies ran while one was open for 0% of the time, Pallas kernels for 7%

profile of v5, /device:TPU:32, one launch (start us, length us, event | category | flops | bytes accessed | tf_op | source)
XLA Modules:
  0.0 111.4 jit_solution(17157746785443661448)
XLA Ops:
  0.6 1.7 %latent_own.1 = (bf16[288,128]{1,0:T(8,128)(2,1)}, bf16[288,128]{1,0:T(8,128)(2,1)}) custom-call(s32[64]{0:T(128)} %order.7, bf16[576,128]{1,0:T(8,128)(2,1)} %bitcast.42), custom_call_target="tpu_custom_call" | custom-call | tf_op jit(solution)/shard_map/latent_own/pallas_call | solution.py:55
  2.3 0.0 collective-permute-start
  2.3 1.5 %collective-permute-done = bf16[288,128]{1,0:T(8,128)(2,1)S(1)} collective-permute-done((bf16[288,128]{1,0:T(8,128)(2,1)}, bf16[288,128]{1,0:T(8,128)(2,1)S(1)}, u32[]{:S(2)}, u32[]{:S(2)}) %collective-permute-start) | collective-permute-done | bytes 73760 | tf_op jit(solution)/shard_map/ppermute | solution.py:385
  3.8 0.9 fusion.3
  4.7 3.3 %collective-permute-start.2 = (bf16[2,288,128]{2,1,0:T(8,128)(2,1)S(1)}, bf16[2,288,128]{2,1,0:T(8,128)(2,1)S(1)}, u32[]{:S(2)}, u32[]{:S(2)}) collective-permute-start(bf16[2,288,128]{2,1,0:T(8,128)(2,1)S(1)} %get-tuple-element.35), channel_id=1, source_target_pairs={{32,0},{136,8},{48,16},{152,24},{0,32},{168,40},{16,48},{184,56},{... | collective-permute-start | bytes 442376 | tf_op jit(solution)/shard_map/ppermute | solution.py:381
  8.0 1.1 collective-permute-start.1
  9.0 1.0 collective-permute-start.3
  10.0 1.4 %collective-permute-done.2 = bf16[2,288,128]{2,1,0:T(8,128)(2,1)S(1)} collective-permute-done((bf16[2,288,128]{2,1,0:T(8,128)(2,1)S(1)}, bf16[2,288,128]{2,1,0:T(8,128)(2,1)S(1)}, u32[]{:S(2)}, u32[]{:S(2)}) %collective-permute-start.2) | collective-permute-done | bytes 147488 | tf_op jit(solution)/shard_map/ppermute | solution.py:381
  11.4 1.9 %collective-permute-done.1 = bf16[2,288,128]{2,1,0:T(8,128)(2,1)S(1)} collective-permute-done((bf16[2,288,128]{2,1,0:T(8,128)(2,1)S(1)}, bf16[2,288,128]{2,1,0:T(8,128)(2,1)S(1)}, u32[]{:S(2)}, u32[]{:S(2)}) %collective-permute-start.1) | collective-permute-done | bytes 147488 | tf_op jit(solution)/shard_map/ppermute | solution.py:381
  13.4 2.0 %collective-permute-done.3 = bf16[2,288,128]{2,1,0:T(8,128)(2,1)S(1)} collective-permute-done((bf16[2,288,128]{2,1,0:T(8,128)(2,1)S(1)}, bf16[2,288,128]{2,1,0:T(8,128)(2,1)S(1)}, u32[]{:S(2)}, u32[]{:S(2)}) %collective-permute-start.3) | collective-permute-done | bytes 147488 | tf_op jit(solution)/shard_map/ppermute | solution.py:381
  15.4 0.1 pad_maximum_fusion.rest_0_
  15.5 1.6 %collective-permute-start.6 = (bf16[4,2,288,128]{3,2,1,0:T(8,128)(2,1)S(1)}, bf16[4,2,288,128]{3,2,1,0:T(8,128)(2,1)S(1)}, u32[]{:S(2)}, u32[]{:S(2)}) collective-permute-start(bf16[4,2,288,128]{3,2,1,0:T(8,128)(2,1)S(1)} %pad_maximum_fusion.rest_0_), channel_id=1, source_target_pairs={{192,0},{56,8},{208,16},{8,24},{224,32},{24,40},{240,48},{40,56},{... | collective-permute-start | bytes 1769480 | tf_op jit(solution)/shard_map/ppermute | solution.py:381
  17.0 2.7 %collective-permute-start.5 = (bf16[4,2,288,128]{3,2,1,0:T(8,128)(2,1)S(1)}, bf16[4,2,288,128]{3,2,1,0:T(8,128)(2,1)S(1)}, u32[]{:S(2)}, u32[]{:S(2)}) collective-permute-start(bf16[4,2,288,128]{3,2,1,0:T(8,128)(2,1)S(1)} %pad_maximum_fusion.rest_0_), channel_id=1, source_target_pairs={{128,0},{40,8},{144,16},{56,24},{160,32},{8,40},{176,48},{24,56},{... | collective-permute-start | bytes 1769480 | tf_op jit(solution)/shard_map/ppermute | solution.py:381
  19.8 1.4 %collective-permute-start.4 = (bf16[4,2,288,128]{3,2,1,0:T(8,128)(2,1)S(1)}, bf16[4,2,288,128]{3,2,1,0:T(8,128)(2,1)S(1)}, u32[]{:S(2)}, u32[]{:S(2)}) collective-permute-start(bf16[4,2,288,128]{3,2,1,0:T(8,128)(2,1)S(1)} %pad_maximum_fusion.rest_0_), channel_id=1, source_target_pairs={{64,0},{24,8},{80,16},{40,24},{96,32},{56,40},{112,48},{8,56},{128... | collective-permute-start | bytes 1769480 | tf_op jit(solution)/shard_map/ppermute | solution.py:381
  21.2 0.0 collective-permute-start.7
  21.2 5.4 %collective-permute-done.6.rest_3_ = bf16[4,2,288,128]{3,2,1,0:T(8,128)(2,1)S(1)} collective-permute-done((bf16[4,2,288,128]{3,2,1,0:T(8,128)(2,1)S(1)}, bf16[4,2,288,128]{3,2,1,0:T(8,128)(2,1)S(1)}, u32[]{:S(2)}, u32[]{:S(2)}) %collective-permute-start.6) | collective-permute-done | bytes 589856 | tf_op jit(solution)/shard_map/ppermute | solution.py:381
  26.6 0.0 collective-permute-start.10
  26.6 7.3 %collective-permute-done.5.rest_2_ = bf16[4,2,288,128]{3,2,1,0:T(8,128)(2,1)S(1)} collective-permute-done((bf16[4,2,288,128]{3,2,1,0:T(8,128)(2,1)S(1)}, bf16[4,2,288,128]{3,2,1,0:T(8,128)(2,1)S(1)}, u32[]{:S(2)}, u32[]{:S(2)}) %collective-permute-start.5) | collective-permute-done | bytes 589856 | tf_op jit(solution)/shard_map/ppermute | solution.py:381
  33.9 0.0 collective-permute-start.9
  34.0 0.0 collective-permute-done.4.rest_1_
  34.0 0.5 collective-permute-start.8
  34.5 0.0 collective-permute-done.7.rest_4_
  34.5 0.0 collective-permute-done.10.rest_7_
  34.5 1.5 %collective-permute-done.9.rest_6_ = bf16[4,2,288,128]{3,2,1,0:T(8,128)(2,1)S(1)} collective-permute-done((bf16[4,2,288,128]{3,2,1,0:T(8,128)(2,1)S(1)}, bf16[4,2,288,128]{3,2,1,0:T(8,128)(2,1)S(1)}, u32[]{:S(2)}, u32[]{:S(2)}) %collective-permute-start.9) | collective-permute-done | bytes 589856 | tf_op jit(solution)/shard_map/ppermute | solution.py:385
  36.0 0.8 collective-permute-done.8.rest_5_
  36.8 20.8 %latent_grads.1 = (bf16[576,4096]{1,0:T(8,128)(2,1)S(1)}, bf16[17,512,256]{2,1,0:T(8,128)(2,1)S(1)}, bf16[4,4,2,288,128]{4,3,2,1,0:T(8,128)(2,1)S(1)}, bf16[4,4,2,288,128]{4,3,2,1,0:T(8,128)(2,1)S(1)}) custom-call(s32[64]{0:T(128)} %order.7, bf16[128,4608]{1,0:T(8,128)(2,1)} %q_in.1, bf16[128,4096]{1,0:T(8,128)(2,1)} %g_in.1, bf16[128,4096]{1,0:T(8,128)(2,1)} %o_in.1, ...), custom_call_target="tpu_custom_call" | custom-call | flops 9697230848 | bytes 25165824 | tf_op jit(solution)/shard_map/latent_grads/pallas_call | solution.py:320
  57.6 0.2 collective-permute-start.11
  57.8 4.4 %collective-permute-done.11 = bf16[4,4,2,288,128]{4,3,2,1,0:T(8,128)(2,1)S(1)} collective-permute-done((bf16[4,4,2,288,128]{4,3,2,1,0:T(8,128)(2,1)S(1)}, bf16[4,4,2,288,128]{4,3,2,1,0:T(8,128)(2,1)S(1)}, u32[]{:S(2)}, u32[]{:S(2)}) %collective-permute-start.11) | collective-permute-done | bytes 2359328 | tf_op jit(solution)/shard_map/ppermute | solution.py:385
  62.2 0.9 fusion.4
  63.1 0.0 copy-start
  63.2 0.1 slice_bitcast_fusion.1
  63.3 1.1 %collective-permute-start.12 = (bf16[4,2,288,128]{3,2,1,0:T(8,128)(2,1)S(1)}, bf16[4,2,288,128]{3,2,1,0:T(8,128)(2,1)S(1)}, u32[]{:S(2)}, u32[]{:S(2)}) collective-permute-start(bf16[4,2,288,128]{3,2,1,0:T(8,128)(2,1)S(1)} %get-tuple-element.19), channel_id=1, source_target_pairs={{192,0},{56,8},{208,16},{8,24},{224,32},{24,40},{240,48},{40,56},{... | collective-permute-start | bytes 1769480 | tf_op jit(solution)/shard_map/ppermute | solution.py:381
  64.4 1.9 %collective-permute-start.13 = (bf16[4,2,288,128]{3,2,1,0:T(8,128)(2,1)S(1)}, bf16[4,2,288,128]{3,2,1,0:T(8,128)(2,1)S(1)}, u32[]{:S(2)}, u32[]{:S(2)}) collective-permute-start(bf16[4,2,288,128]{3,2,1,0:T(8,128)(2,1)S(1)} %get-tuple-element.20), channel_id=1, source_target_pairs={{128,0},{40,8},{144,16},{56,24},{160,32},{8,40},{176,48},{24,56},{... | collective-permute-start | bytes 1769480 | tf_op jit(solution)/shard_map/ppermute | solution.py:381
  66.3 1.6 %collective-permute-start.14 = (bf16[4,2,288,128]{3,2,1,0:T(8,128)(2,1)S(1)}, bf16[4,2,288,128]{3,2,1,0:T(8,128)(2,1)S(1)}, u32[]{:S(2)}, u32[]{:S(2)}) collective-permute-start(bf16[4,2,288,128]{3,2,1,0:T(8,128)(2,1)S(1)} %get-tuple-element.21), channel_id=1, source_target_pairs={{64,0},{24,8},{80,16},{40,24},{96,32},{56,40},{112,48},{8,56},{128... | collective-permute-start | bytes 1769480 | tf_op jit(solution)/shard_map/ppermute | solution.py:381
  67.9 7.5 %latent_queries.1 = bf16[128,4608]{1,0:T(8,128)(2,1)} custom-call(s32[64]{0:T(128)S(1)} %copy-done, bf16[17,512,256]{2,1,0:T(8,128)(2,1)S(1)} %get-tuple-element.22.dscores, bf16[576,4096]{1,0:T(8,128)(2,1)S(1)} %get-tuple-element.23.keys), custom_call_target="tpu_custom_call" | custom-call | flops 2566914048 | bytes 10485760 | tf_op jit(solution)/shard_map/latent_queries/pallas_call | solution.py:358
  75.4 5.4 %collective-permute-done.12 = bf16[4,2,288,128]{3,2,1,0:T(8,128)(2,1)S(1)} collective-permute-done((bf16[4,2,288,128]{3,2,1,0:T(8,128)(2,1)S(1)}, bf16[4,2,288,128]{3,2,1,0:T(8,128)(2,1)S(1)}, u32[]{:S(2)}, u32[]{:S(2)}) %collective-permute-start.12) | collective-permute-done | bytes 589856 | tf_op jit(solution)/shard_map/ppermute | solution.py:381
  80.8 0.9 collective-permute-done.14
  81.7 0.2 fusion.2
  81.9 0.1 convert.12
  82.0 0.6 collective-permute-start.17
  82.7 1.4 %collective-permute-start.16 = (bf16[2,288,128]{2,1,0:T(8,128)(2,1)S(1)}, bf16[2,288,128]{2,1,0:T(8,128)(2,1)S(1)}, u32[]{:S(2)}, u32[]{:S(2)}) collective-permute-start(bf16[2,288,128]{2,1,0:T(8,128)(2,1)S(1)} %get-tuple-element.32), channel_id=1, source_target_pairs={{32,0},{136,8},{48,16},{152,24},{0,32},{168,40},{16,48},{184,56},{... | collective-permute-start | bytes 442376 | tf_op jit(solution)/shard_map/ppermute | solution.py:381
  84.0 0.2 collective-permute-start.15
  84.3 3.0 %collective-permute-done.17.rest_2_ = bf16[2,288,128]{2,1,0:T(8,128)(2,1)S(1)} collective-permute-done((bf16[2,288,128]{2,1,0:T(8,128)(2,1)S(1)}, bf16[2,288,128]{2,1,0:T(8,128)(2,1)S(1)}, u32[]{:S(2)}, u32[]{:S(2)}) %collective-permute-start.17) | collective-permute-done | bytes 147488 | tf_op jit(solution)/shard_map/ppermute | solution.py:381
  87.3 2.1 %collective-permute-done.16.rest_1_ = bf16[2,288,128]{2,1,0:T(8,128)(2,1)S(1)} collective-permute-done((bf16[2,288,128]{2,1,0:T(8,128)(2,1)S(1)}, bf16[2,288,128]{2,1,0:T(8,128)(2,1)S(1)}, u32[]{:S(2)}, u32[]{:S(2)}) %collective-permute-start.16) | collective-permute-done | bytes 147488 | tf_op jit(solution)/shard_map/ppermute | solution.py:381
  89.4 1.5 %collective-permute-done.15.rest_0_ = bf16[2,288,128]{2,1,0:T(8,128)(2,1)S(1)} collective-permute-done((bf16[2,288,128]{2,1,0:T(8,128)(2,1)S(1)}, bf16[2,288,128]{2,1,0:T(8,128)(2,1)S(1)}, u32[]{:S(2)}, u32[]{:S(2)}) %collective-permute-start.15) | collective-permute-done | bytes 147488 | tf_op jit(solution)/shard_map/ppermute | solution.py:381
  90.9 1.6 %latent_owner.1 = bf16[256,288]{1,0:T(8,128)(2,1)} custom-call(s32[64]{0:T(128)} %order.7, f32[2,288,128]{2,1,0:T(8,128)S(1)} %slice_bitcast_fusion.4.first, bf16[2,288,128]{2,1,0:T(8,128)(2,1)S(1)} %collective-permute-done.15.rest_0_, bf16[2,288,128]{2,1,0:T(8,128)(2,1)S(1)} %collective-permute-done.16.rest_1_, ...), custom_call_target="tpu_custom_call" | custom-call | tf_op jit(solution)/shard_map/latent_owner/pallas_call | solution.py:79
  92.4 18.2 %all_to_all.5 = bf16[16,16,288]{2,1,0:T(8,128)(2,1)S(1)} all-to-all(bf16[16,16,288]{2,1,0:T(8,128)(2,1)} %bitcast.38), channel_id=1, replica_groups=mesh['x'=4,'y'=4,'c'=2,'z'=8] {'c','z'}, dimensions={0} | all-to-all | bytes 294912 | tf_op jit(solution)/shard_map/all_to_all | solution.py:411
  110.7 0.7 pad_maximum_fusion.2
  (6 shorter events, 0.1 us)
Async XLA Ops:
  2.3 1.5 %collective-permute-start = (bf16[288,128]{1,0:T(8,128)(2,1)}, bf16[288,128]{1,0:T(8,128)(2,1)S(1)}, u32[]{:S(2)}, u32[]{:S(2)}) collective-permute-start(bf16[288,128]{1,0:T(8,128)(2,1)} %get-tuple-element.15), channel_id=1, source_target_pairs={{0,8},{8,0},{1,9},{9,1},{2,10},{10,2},{3,11},{11,3},{4,12},{12,4},... | collective-permute-start | bytes 221192 | tf_op jit(solution)/shard_map/ppermute | solution.py:385
  4.7 6.7 %collective-permute-start.2 = (bf16[2,288,128]{2,1,0:T(8,128)(2,1)S(1)}, bf16[2,288,128]{2,1,0:T(8,128)(2,1)S(1)}, u32[]{:S(2)}, u32[]{:S(2)}) collective-permute-start(bf16[2,288,128]{2,1,0:T(8,128)(2,1)S(1)} %get-tuple-element.35), channel_id=1, source_target_pairs={{32,0},{136,8},{48,16},{152,24},{0,32},{168,40},{16,48},{184,56},{... | collective-permute-start | bytes 442376 | tf_op jit(solution)/shard_map/ppermute | solution.py:381
  8.0 5.4 %collective-permute-start.1 = (bf16[2,288,128]{2,1,0:T(8,128)(2,1)S(1)}, bf16[2,288,128]{2,1,0:T(8,128)(2,1)S(1)}, u32[]{:S(2)}, u32[]{:S(2)}) collective-permute-start(bf16[2,288,128]{2,1,0:T(8,128)(2,1)S(1)} %get-tuple-element.35), channel_id=1, source_target_pairs={{16,0},{72,8},{32,16},{88,24},{48,32},{104,40},{0,48},{120,56},{80... | collective-permute-start | bytes 442376 | tf_op jit(solution)/shard_map/ppermute | solution.py:381
  9.0 6.4 %collective-permute-start.3 = (bf16[2,288,128]{2,1,0:T(8,128)(2,1)S(1)}, bf16[2,288,128]{2,1,0:T(8,128)(2,1)S(1)}, u32[]{:S(2)}, u32[]{:S(2)}) collective-permute-start(bf16[2,288,128]{2,1,0:T(8,128)(2,1)S(1)} %get-tuple-element.35), channel_id=1, source_target_pairs={{48,0},{200,8},{0,16},{216,24},{16,32},{232,40},{32,48},{248,56},{... | collective-permute-start | bytes 442376 | tf_op jit(solution)/shard_map/ppermute | solution.py:381
  15.5 11.2 %collective-permute-start.6 = (bf16[4,2,288,128]{3,2,1,0:T(8,128)(2,1)S(1)}, bf16[4,2,288,128]{3,2,1,0:T(8,128)(2,1)S(1)}, u32[]{:S(2)}, u32[]{:S(2)}) collective-permute-start(bf16[4,2,288,128]{3,2,1,0:T(8,128)(2,1)S(1)} %pad_maximum_fusion.rest_0_), channel_id=1, source_target_pairs={{192,0},{56,8},{208,16},{8,24},{224,32},{24,40},{240,48},{40,56},{... | collective-permute-start | bytes 1769480 | tf_op jit(solution)/shard_map/ppermute | solution.py:381
  17.0 16.9 %collective-permute-start.5 = (bf16[4,2,288,128]{3,2,1,0:T(8,128)(2,1)S(1)}, bf16[4,2,288,128]{3,2,1,0:T(8,128)(2,1)S(1)}, u32[]{:S(2)}, u32[]{:S(2)}) collective-permute-start(bf16[4,2,288,128]{3,2,1,0:T(8,128)(2,1)S(1)} %pad_maximum_fusion.rest_0_), channel_id=1, source_target_pairs={{128,0},{40,8},{144,16},{56,24},{160,32},{8,40},{176,48},{24,56},{... | collective-permute-start | bytes 1769480 | tf_op jit(solution)/shard_map/ppermute | solution.py:381
  19.8 14.2 %collective-permute-start.4 = (bf16[4,2,288,128]{3,2,1,0:T(8,128)(2,1)S(1)}, bf16[4,2,288,128]{3,2,1,0:T(8,128)(2,1)S(1)}, u32[]{:S(2)}, u32[]{:S(2)}) collective-permute-start(bf16[4,2,288,128]{3,2,1,0:T(8,128)(2,1)S(1)} %pad_maximum_fusion.rest_0_), channel_id=1, source_target_pairs={{64,0},{24,8},{80,16},{40,24},{96,32},{56,40},{112,48},{8,56},{128... | collective-permute-start | bytes 1769480 | tf_op jit(solution)/shard_map/ppermute | solution.py:381
  21.2 13.3 %collective-permute-start.7 = (bf16[4,2,288,128]{3,2,1,0:T(8,128)(2,1)S(1)}, bf16[4,2,288,128]{3,2,1,0:T(8,128)(2,1)S(1)}, u32[]{:S(2)}, u32[]{:S(2)}) collective-permute-start(bf16[4,2,288,128]{3,2,1,0:T(8,128)(2,1)S(1)} %pad_maximum_fusion.rest_0_), channel_id=1, source_target_pairs={{0,8},{8,0},{1,9},{9,1},{2,10},{10,2},{3,11},{11,3},{4,12},{12,4},... | collective-permute-start | bytes 1769480 | tf_op jit(solution)/shard_map/ppermute | solution.py:385
  26.6 7.8 %collective-permute-start.10 = (bf16[4,2,288,128]{3,2,1,0:T(8,128)(2,1)S(1)}, bf16[4,2,288,128]{3,2,1,0:T(8,128)(2,1)S(1)}, u32[]{:S(2)}, u32[]{:S(2)}) collective-permute-start(bf16[4,2,288,128]{3,2,1,0:T(8,128)(2,1)S(1)} %collective-permute-done.6.rest_3_), channel_id=1, source_target_pairs={{0,8},{8,0},{1,9},{9,1},{2,10},{10,2},{3,11},{11,3},{4,12},{12,4},... | collective-permute-start | bytes 1769480 | tf_op jit(solution)/shard_map/ppermute | solution.py:385
  33.9 2.0 %collective-permute-start.9 = (bf16[4,2,288,128]{3,2,1,0:T(8,128)(2,1)S(1)}, bf16[4,2,288,128]{3,2,1,0:T(8,128)(2,1)S(1)}, u32[]{:S(2)}, u32[]{:S(2)}) collective-permute-start(bf16[4,2,288,128]{3,2,1,0:T(8,128)(2,1)S(1)} %collective-permute-done.5.rest_2_), channel_id=1, source_target_pairs={{0,8},{8,0},{1,9},{9,1},{2,10},{10,2},{3,11},{11,3},{4,12},{12,4},... | collective-permute-start | bytes 1769480 | tf_op jit(solution)/shard_map/ppermute | solution.py:385
  34.0 2.8 %collective-permute-start.8 = (bf16[4,2,288,128]{3,2,1,0:T(8,128)(2,1)S(1)}, bf16[4,2,288,128]{3,2,1,0:T(8,128)(2,1)S(1)}, u32[]{:S(2)}, u32[]{:S(2)}) collective-permute-start(bf16[4,2,288,128]{3,2,1,0:T(8,128)(2,1)S(1)} %collective-permute-done.4.rest_1_), channel_id=1, source_target_pairs={{0,8},{8,0},{1,9},{9,1},{2,10},{10,2},{3,11},{11,3},{4,12},{12,4},... | collective-permute-start | bytes 1769480 | tf_op jit(solution)/shard_map/ppermute | solution.py:385
  57.6 4.6 %collective-permute-start.11 = (bf16[4,4,2,288,128]{4,3,2,1,0:T(8,128)(2,1)S(1)}, bf16[4,4,2,288,128]{4,3,2,1,0:T(8,128)(2,1)S(1)}, u32[]{:S(2)}, u32[]{:S(2)}) collective-permute-start(bf16[4,4,2,288,128]{4,3,2,1,0:T(8,128)(2,1)S(1)} %get-tuple-element.17), channel_id=1, source_target_pairs={{0,8},{8,0},{1,9},{9,1},{2,10},{10,2},{3,11},{11,3},{4,12},{12,4},... | collective-permute-start | bytes 7077896 | tf_op jit(solution)/shard_map/ppermute | solution.py:385
  63.1 4.8 %copy-start = (s32[64]{0:T(128)S(1)}, s32[64]{0:T(128)}, u32[]{:S(2)}) copy-start(s32[64]{0:T(128)} %order.7) | copy-start | bytes 772
  63.3 17.5 %collective-permute-start.12 = (bf16[4,2,288,128]{3,2,1,0:T(8,128)(2,1)S(1)}, bf16[4,2,288,128]{3,2,1,0:T(8,128)(2,1)S(1)}, u32[]{:S(2)}, u32[]{:S(2)}) collective-permute-start(bf16[4,2,288,128]{3,2,1,0:T(8,128)(2,1)S(1)} %get-tuple-element.19), channel_id=1, source_target_pairs={{192,0},{56,8},{208,16},{8,24},{224,32},{24,40},{240,48},{40,56},{... | collective-permute-start | bytes 1769480 | tf_op jit(solution)/shard_map/ppermute | solution.py:381
  64.4 16.4 %collective-permute-start.13 = (bf16[4,2,288,128]{3,2,1,0:T(8,128)(2,1)S(1)}, bf16[4,2,288,128]{3,2,1,0:T(8,128)(2,1)S(1)}, u32[]{:S(2)}, u32[]{:S(2)}) collective-permute-start(bf16[4,2,288,128]{3,2,1,0:T(8,128)(2,1)S(1)} %get-tuple-element.20), channel_id=1, source_target_pairs={{128,0},{40,8},{144,16},{56,24},{160,32},{8,40},{176,48},{24,56},{... | collective-permute-start | bytes 1769480 | tf_op jit(solution)/shard_map/ppermute | solution.py:381
  66.3 15.4 %collective-permute-start.14 = (bf16[4,2,288,128]{3,2,1,0:T(8,128)(2,1)S(1)}, bf16[4,2,288,128]{3,2,1,0:T(8,128)(2,1)S(1)}, u32[]{:S(2)}, u32[]{:S(2)}) collective-permute-start(bf16[4,2,288,128]{3,2,1,0:T(8,128)(2,1)S(1)} %get-tuple-element.21), channel_id=1, source_target_pairs={{64,0},{24,8},{80,16},{40,24},{96,32},{56,40},{112,48},{8,56},{128... | collective-permute-start | bytes 1769480 | tf_op jit(solution)/shard_map/ppermute | solution.py:381
  82.0 5.2 %collective-permute-start.17 = (bf16[2,288,128]{2,1,0:T(8,128)(2,1)S(1)}, bf16[2,288,128]{2,1,0:T(8,128)(2,1)S(1)}, u32[]{:S(2)}, u32[]{:S(2)}) collective-permute-start(bf16[2,288,128]{2,1,0:T(8,128)(2,1)S(1)} %get-tuple-element.31), channel_id=1, source_target_pairs={{16,0},{72,8},{32,16},{88,24},{48,32},{104,40},{0,48},{120,56},{80... | collective-permute-start | bytes 442376 | tf_op jit(solution)/shard_map/ppermute | solution.py:381
  82.7 6.7 %collective-permute-start.16 = (bf16[2,288,128]{2,1,0:T(8,128)(2,1)S(1)}, bf16[2,288,128]{2,1,0:T(8,128)(2,1)S(1)}, u32[]{:S(2)}, u32[]{:S(2)}) collective-permute-start(bf16[2,288,128]{2,1,0:T(8,128)(2,1)S(1)} %get-tuple-element.32), channel_id=1, source_target_pairs={{32,0},{136,8},{48,16},{152,24},{0,32},{168,40},{16,48},{184,56},{... | collective-permute-start | bytes 442376 | tf_op jit(solution)/shard_map/ppermute | solution.py:381
  84.0 6.9 %collective-permute-start.15 = (bf16[2,288,128]{2,1,0:T(8,128)(2,1)S(1)}, bf16[2,288,128]{2,1,0:T(8,128)(2,1)S(1)}, u32[]{:S(2)}, u32[]{:S(2)}) collective-permute-start(bf16[2,288,128]{2,1,0:T(8,128)(2,1)S(1)} %get-tuple-element.33), channel_id=1, source_target_pairs={{48,0},{200,8},{0,16},{216,24},{16,32},{232,40},{32,48},{248,56},{... | collective-permute-start | bytes 442376 | tf_op jit(solution)/shard_map/ppermute | solution.py:381

commit v6 on v5

--- a/solution.py
+++ b/solution.py
@@ -39,24 +39,21 @@
     return lax.axis_index("x"), lax.axis_index("y"), lax.axis_index("c")
 
 
-def own_kernel(order, keys, mine, theirs, *, sides):
+def own_kernel(order, keys, out, *, sides):
     my_x, my_y, my_c = here()
     odd = lax.rem(order[2 * ((my_x * sides + my_y) * 2 + my_c)], 2)
     tile = keys[...]
     turned = jnp.concatenate([tile[:, GROUP:], tile[:, :GROUP]], axis=1)
-    tile = jnp.where(odd == 1, turned, tile)
-    mine[...] = jnp.where(my_c == 0, tile[:HALF], tile[HALF:])
-    theirs[...] = jnp.where(my_c == 0, tile[HALF:], tile[:HALF])
+    out[...] = jnp.where(odd == 1, turned, tile)
 
 
 def run_own(order, keys, sides):
-    half = jax.ShapeDtypeStruct((HALF, PAIR), jnp.bfloat16)
     vmem = pl.BlockSpec(memory_space=pltpu.VMEM)
     return pl.pallas_call(
         functools.partial(own_kernel, sides=sides),
-        out_shape=(half, half),
+        out_shape=jax.ShapeDtypeStruct(keys.shape, keys.dtype),
         in_specs=[pl.BlockSpec(memory_space=pltpu.SMEM), vmem],
-        out_specs=(vmem, vmem),
+        out_specs=vmem,
         name="latent_own",
     )(order, keys)
 
@@ -165,8 +162,8 @@
     piece_refs = rest[:pieces]
     keys, dscores, keep, send = rest[pieces : pieces + 4]
     (
-            scores, dweights, top, total, q, g, o, q_rows, g_rows, q_cols, g_cols,
-        deltas, slot_of, own_sem,
+        scores, dweights, top, total, q, g, o, q_rows, g_rows, q_cols, g_cols, deltas, slot_of,
+        own_sem,
     ) = rest[pieces + 4 :]
     pairs = keys.shape[1] // PAIR
     groups = 2 * pairs
@@ -193,20 +190,18 @@
     for at, ref in enumerate(piece_refs):
         step2 = at % sides
         holder = my_c if at < sides else 1 - my_c
-        half = pl.ds(pl.multiple_of(holder * HALF, HALF), HALF)
         for step1 in range(sides):
             at_x = lax.rem(my_x + jnp.where(holder == 0, step2, step1), sides)
             at_y = lax.rem(my_y + jnp.where(holder == 0, step1, step2), sides)
-            for step_c in range(2):
-                pair = (at_x * sides + at_y) * 2 + lax.rem(holder + step_c, 2)
-                tile = ref[step1, step_c]
-                turn = lax.rem(order[2 * pair], 2)
-                even = lax.div(order[2 * pair + turn], 2) * PAIR
-                odd = lax.div(order[2 * pair + 1 - turn], 2) * PAIR
-                evens = keys.at[half, pl.ds(pl.multiple_of(even, PAIR), PAIR)]
-                odds = keys.at[half, pl.ds(pl.multiple_of(odd, PAIR), PAIR)]
-                evens[:, :GROUP] = tile[:, :GROUP]
-                odds[:, GROUP:] = tile[:, GROUP:]
+            pair = (at_x * sides + at_y) * 2 + holder
+            tile = ref[step1]
+            turn = lax.rem(order[2 * pair], 2)
+            even = lax.div(order[2 * pair + turn], 2) * PAIR
+            odd = lax.div(order[2 * pair + 1 - turn], 2) * PAIR
+            evens = keys.at[:, pl.ds(pl.multiple_of(even, PAIR), PAIR)]
+            odds = keys.at[:, pl.ds(pl.multiple_of(odd, PAIR), PAIR)]
+            evens[:, :GROUP] = tile[:, :GROUP]
+            odds[:, GROUP:] = tile[:, GROUP:]
     for copy in own:
         copy.wait()
     spread_rows(my_c, q, g, o, q_rows, g_rows, q_cols, g_cols, deltas)
@@ -386,9 +381,8 @@
 
 
 def shards(q_latent, kv_latent, out_grad, saved_out, group_order, *, sides, depth):
-    mine, theirs = run_own(group_order, kv_latent.T, sides)
-    both = jnp.stack([mine, swap(theirs)])
-    line = jnp.stack([both] + [hop(both, sides, 0, d) for d in range(1, sides)])
+    own = run_own(group_order, kv_latent.T, sides)
+    line = jnp.stack([own] + [hop(own, sides, 0, d) for d in range(1, sides)])
     far = [hop(line, sides, 1, d) for d in range(1, sides)]
     pieces = [line] + far
     pieces = pieces + [swap(piece) for piece in pieces]
@@ -396,11 +390,13 @@
     keys, dscores, keep, send = run_grads(
         group_order, q_latent, out_grad, saved_out, pieces, sides
     )
-    total = keep.astype(jnp.float32) + swap(send).astype(jnp.float32)
-    low = [total[d].astype(jnp.bfloat16) for d in range(1, sides)]
+    both = {}
+    for d in sorted(range(sides), key=lambda d: -min(d, sides - d)):
+        both[d] = keep[d].astype(jnp.float32) + swap(send[d]).astype(jnp.float32)
+    low = [both[d].astype(jnp.bfloat16) for d in range(1, sides)]
     low, dscores = lax.optimization_barrier((low, dscores))
     q_grad = run_queries(group_order, dscores, keys, sides, q_latent.shape)
-    total = total[0]
+    total = both[0]
     for d in range(1, sides):
         total = total + hop(low[d - 1], sides, 1, -d).astype(jnp.float32)
     total, q_grad = lax.optimization_barrier((total, q_grad))

time: 112 us -> 110 us (0.982)
  waiting for transfers between devices: 39.2 us -> 34.7 us
  starting transfers between devices: 18.6 us -> 21.6 us
    ppermute x6 -> x8, waiting for transfers between devices: 8.21 us -> 5 us  [swap(): return lax.ppermute(a, 'c', [(0, 1), (1, 0)])]
    ppermute x12, starting transfers between devices: 17.9 us -> 20 us  [hop(): return lax.ppermute(a, ('x', 'y', 'c'), moves)]
    ppermute x12, waiting for transfers between devices: 31 us -> 29.7 us  [hop(): return lax.ppermute(a, ('x', 'y', 'c'), moves)]
  transfers between devices with their start and end apart: 18 -> 20, of which waited for: 14 -> 15; matrix products, arithmetic and copies ran while one was open for 0% -> 0% of each run, Pallas kernels for 7% -> 7%
where the time goes in v6:
time: 110 us
  waiting for transfers between devices  34.7 us (32%)
  Pallas kernels  31.4 us (29%)
  starting transfers between devices  21.6 us (20%)
  blocking collectives  18.2 us (17%)
  other arithmetic  2.62 us (2%)
    ppermute x12, waiting for transfers between devices, hop(): return lax.ppermute(a, ('x', 'y', 'c'), moves)  29.7 us
    pallas_call x1, Pallas kernels, run_grads(): pl.pallas_call(functools.partial(grads_kernel, sides=sides, rows=rows), o...  20.7 us
    ppermute x12, starting transfers between devices, hop(): return lax.ppermute(a, ('x', 'y', 'c'), moves)  20 us
    all_to_all x1, blocking collectives, shards(): parts = lax.all_to_all(by_owner, ('c', 'z'), 0, 0, tiled=True)  18.2 us
    pallas_call x1, Pallas kernels, run_queries(): pl.pallas_call(functools.partial(query_kernel, sides=sides, rows=rows), o...  7.48 us
    ppermute x8, waiting for transfers between devices, swap(): return lax.ppermute(a, 'c', [(0, 1), (1, 0)])  5 us
  transfers between devices with their start and end apart: 20, of which 15 were waited for; matrix products, arithmetic and copies ran while one was open for 0% of the time, Pallas kernels for 7%

profile of v6, /device:TPU:32, one launch (start us, length us, event | category | flops | bytes accessed | tf_op | source)
XLA Modules:
  0.0 109.5 jit_solution(13076357194817588752)
XLA Ops:
  0.6 1.7 %latent_own.1 = bf16[576,128]{1,0:T(8,128)(2,1)} custom-call(s32[64]{0:T(128)} %order.7, bf16[576,128]{1,0:T(8,128)(2,1)} %bitcast.46), custom_call_target="tpu_custom_call" | custom-call | tf_op jit(solution)/shard_map/latent_own/pallas_call | solution.py:52
  2.3 1.6 %collective-permute-start.2 = (bf16[576,128]{1,0:T(8,128)(2,1)}, bf16[576,128]{1,0:T(8,128)(2,1)S(1)}, u32[]{:S(2)}, u32[]{:S(2)}) collective-permute-start(bf16[576,128]{1,0:T(8,128)(2,1)} %latent_own.1), channel_id=1, source_target_pairs={{48,0},{200,8},{0,16},{216,24},{16,32},{232,40},{32,48},{248,56},{... | collective-permute-start | bytes 442376 | tf_op jit(solution)/shard_map/ppermute | solution.py:376
  3.9 2.9 %collective-permute-start.1 = (bf16[576,128]{1,0:T(8,128)(2,1)}, bf16[576,128]{1,0:T(8,128)(2,1)S(1)}, u32[]{:S(2)}, u32[]{:S(2)}) collective-permute-start(bf16[576,128]{1,0:T(8,128)(2,1)} %latent_own.1), channel_id=1, source_target_pairs={{32,0},{136,8},{48,16},{152,24},{0,32},{168,40},{16,48},{184,56},{... | collective-permute-start | bytes 442376 | tf_op jit(solution)/shard_map/ppermute | solution.py:376
  6.8 1.3 %collective-permute-start = (bf16[576,128]{1,0:T(8,128)(2,1)}, bf16[576,128]{1,0:T(8,128)(2,1)S(1)}, u32[]{:S(2)}, u32[]{:S(2)}) collective-permute-start(bf16[576,128]{1,0:T(8,128)(2,1)} %latent_own.1), channel_id=1, source_target_pairs={{16,0},{72,8},{32,16},{88,24},{48,32},{104,40},{0,48},{120,56},{80... | collective-permute-start | bytes 442376 | tf_op jit(solution)/shard_map/ppermute | solution.py:376
  8.1 0.7 collective-permute-done.2
  8.9 2.8 %collective-permute-done.1 = bf16[576,128]{1,0:T(8,128)(2,1)S(1)} collective-permute-done((bf16[576,128]{1,0:T(8,128)(2,1)}, bf16[576,128]{1,0:T(8,128)(2,1)S(1)}, u32[]{:S(2)}, u32[]{:S(2)}) %collective-permute-start.1) | collective-permute-done | bytes 147488 | tf_op jit(solution)/shard_map/ppermute | solution.py:376
  11.7 0.4 collective-permute-done
  12.1 1.0 pad_maximum_fusion.rest_0_
  13.1 1.6 %collective-permute-start.5 = (bf16[4,576,128]{2,1,0:T(8,128)(2,1)S(1)}, bf16[4,576,128]{2,1,0:T(8,128)(2,1)S(1)}, u32[]{:S(2)}, u32[]{:S(2)}) collective-permute-start(bf16[4,576,128]{2,1,0:T(8,128)(2,1)S(1)} %pad_maximum_fusion.rest_0_), channel_id=1, source_target_pairs={{192,0},{56,8},{208,16},{8,24},{224,32},{24,40},{240,48},{40,56},{... | collective-permute-start | bytes 1769480 | tf_op jit(solution)/shard_map/ppermute | solution.py:376
  14.7 2.7 %collective-permute-start.4 = (bf16[4,576,128]{2,1,0:T(8,128)(2,1)S(1)}, bf16[4,576,128]{2,1,0:T(8,128)(2,1)S(1)}, u32[]{:S(2)}, u32[]{:S(2)}) collective-permute-start(bf16[4,576,128]{2,1,0:T(8,128)(2,1)S(1)} %pad_maximum_fusion.rest_0_), channel_id=1, source_target_pairs={{128,0},{40,8},{144,16},{56,24},{160,32},{8,40},{176,48},{24,56},{... | collective-permute-start | bytes 1769480 | tf_op jit(solution)/shard_map/ppermute | solution.py:376
  17.4 1.4 %collective-permute-start.3 = (bf16[4,576,128]{2,1,0:T(8,128)(2,1)S(1)}, bf16[4,576,128]{2,1,0:T(8,128)(2,1)S(1)}, u32[]{:S(2)}, u32[]{:S(2)}) collective-permute-start(bf16[4,576,128]{2,1,0:T(8,128)(2,1)S(1)} %pad_maximum_fusion.rest_0_), channel_id=1, source_target_pairs={{64,0},{24,8},{80,16},{40,24},{96,32},{56,40},{112,48},{8,56},{128... | collective-permute-start | bytes 1769480 | tf_op jit(solution)/shard_map/ppermute | solution.py:376
  18.9 0.0 collective-permute-start.6
  18.9 5.4 %collective-permute-done.5.rest_3_ = bf16[4,576,128]{2,1,0:T(8,128)(2,1)S(1)} collective-permute-done((bf16[4,576,128]{2,1,0:T(8,128)(2,1)S(1)}, bf16[4,576,128]{2,1,0:T(8,128)(2,1)S(1)}, u32[]{:S(2)}, u32[]{:S(2)}) %collective-permute-start.5) | collective-permute-done | bytes 589856 | tf_op jit(solution)/shard_map/ppermute | solution.py:376
  24.3 0.0 collective-permute-start.9
  24.3 7.3 %collective-permute-done.4.rest_2_ = bf16[4,576,128]{2,1,0:T(8,128)(2,1)S(1)} collective-permute-done((bf16[4,576,128]{2,1,0:T(8,128)(2,1)S(1)}, bf16[4,576,128]{2,1,0:T(8,128)(2,1)S(1)}, u32[]{:S(2)}, u32[]{:S(2)}) %collective-permute-start.4) | collective-permute-done | bytes 589856 | tf_op jit(solution)/shard_map/ppermute | solution.py:376
  31.6 0.0 collective-permute-start.8
  31.6 0.0 collective-permute-done.3.rest_1_
  31.6 0.5 collective-permute-start.7
  32.1 0.0 collective-permute-done.9.rest_7_
  32.1 1.5 %collective-permute-done.8.rest_6_ = bf16[4,576,128]{2,1,0:T(8,128)(2,1)S(1)} collective-permute-done((bf16[4,576,128]{2,1,0:T(8,128)(2,1)S(1)}, bf16[4,576,128]{2,1,0:T(8,128)(2,1)S(1)}, u32[]{:S(2)}, u32[]{:S(2)}) %collective-permute-start.8) | collective-permute-done | bytes 589856 | tf_op jit(solution)/shard_map/ppermute | solution.py:380
  33.6 0.8 collective-permute-done.7.rest_5_
  34.5 20.7 %latent_grads.1 = (bf16[576,4096]{1,0:T(8,128)(2,1)S(1)}, bf16[17,512,256]{2,1,0:T(8,128)(2,1)S(1)}, bf16[4,4,2,288,128]{4,3,2,1,0:T(8,128)(2,1)S(1)}, bf16[4,4,2,288,128]{4,3,2,1,0:T(8,128)(2,1)S(1)}) custom-call(s32[64]{0:T(128)} %order.7, bf16[128,4608]{1,0:T(8,128)(2,1)} %q_in.1, bf16[128,4096]{1,0:T(8,128)(2,1)} %g_in.1, bf16[128,4096]{1,0:T(8,128)(2,1)} %o_in.1, ...), custom_call_target="tpu_custom_call" | custom-call | flops 9697230848 | bytes 25165824 | tf_op jit(solution)/shard_map/latent_grads/pallas_call | solution.py:315
  55.1 0.2 slice_bitcast_fusion.3
  55.3 0.1 collective-permute-start.13
  55.5 0.5 collective-permute-start.12
  55.9 0.1 collective-permute-start.11
  56.0 0.4 collective-permute-start.10
  56.5 1.0 collective-permute-done.13
  57.4 0.8 collective-permute-done.12
  58.3 0.8 collective-permute-done.11
  59.1 0.5 fusion
  59.6 0.9 collective-permute-start.14
  60.5 2.4 %collective-permute-start.15 = (bf16[4,2,288,128]{3,2,1,0:T(8,128)(2,1)S(1)}, bf16[4,2,288,128]{3,2,1,0:T(8,128)(2,1)S(1)}, u32[]{:S(2)}, u32[]{:S(2)}) collective-permute-start(bf16[4,2,288,128]{3,2,1,0:T(8,128)(2,1)S(1)} %get-tuple-element.16), channel_id=1, source_target_pairs={{128,0},{40,8},{144,16},{56,24},{160,32},{8,40},{176,48},{24,56},{... | collective-permute-start | bytes 1769480 | tf_op jit(solution)/shard_map/ppermute | solution.py:376
  62.9 1.3 %collective-permute-start.16 = (bf16[4,2,288,128]{3,2,1,0:T(8,128)(2,1)S(1)}, bf16[4,2,288,128]{3,2,1,0:T(8,128)(2,1)S(1)}, u32[]{:S(2)}, u32[]{:S(2)}) collective-permute-start(bf16[4,2,288,128]{3,2,1,0:T(8,128)(2,1)S(1)} %get-tuple-element.17), channel_id=1, source_target_pairs={{64,0},{24,8},{80,16},{40,24},{96,32},{56,40},{112,48},{8,56},{128... | collective-permute-start | bytes 1769480 | tf_op jit(solution)/shard_map/ppermute | solution.py:376
  64.2 7.5 %latent_queries.1 = bf16[128,4608]{1,0:T(8,128)(2,1)} custom-call(s32[64]{0:T(128)S(1)} %copy-done, bf16[17,512,256]{2,1,0:T(8,128)(2,1)S(1)} %get-tuple-element.18.dscores, bf16[576,4096]{1,0:T(8,128)(2,1)S(1)} %get-tuple-element.19.keys), custom_call_target="tpu_custom_call" | custom-call | flops 2566914048 | bytes 10485760 | tf_op jit(solution)/shard_map/latent_queries/pallas_call | solution.py:353
  71.7 5.4 %collective-permute-done.15 = bf16[4,2,288,128]{3,2,1,0:T(8,128)(2,1)S(1)} collective-permute-done((bf16[4,2,288,128]{3,2,1,0:T(8,128)(2,1)S(1)}, bf16[4,2,288,128]{3,2,1,0:T(8,128)(2,1)S(1)}, u32[]{:S(2)}, u32[]{:S(2)}) %collective-permute-start.15) | collective-permute-done | bytes 589856 | tf_op jit(solution)/shard_map/ppermute | solution.py:376
  77.1 0.9 collective-permute-done.16
  78.0 0.3 fusion.5
  78.4 0.1 convert.10
  78.5 2.3 %collective-permute-start.19 = (bf16[2,288,128]{2,1,0:T(8,128)(2,1)S(1)}, bf16[2,288,128]{2,1,0:T(8,128)(2,1)S(1)}, u32[]{:S(2)}, u32[]{:S(2)}) collective-permute-start(bf16[2,288,128]{2,1,0:T(8,128)(2,1)S(1)} %get-tuple-element.29), channel_id=1, source_target_pairs={{16,0},{72,8},{32,16},{88,24},{48,32},{104,40},{0,48},{120,56},{80... | collective-permute-start | bytes 442376 | tf_op jit(solution)/shard_map/ppermute | solution.py:376
  80.8 0.8 collective-permute-start.18
  81.6 0.7 collective-permute-start.17
  82.3 2.8 %collective-permute-done.19.rest_2_ = bf16[2,288,128]{2,1,0:T(8,128)(2,1)S(1)} collective-permute-done((bf16[2,288,128]{2,1,0:T(8,128)(2,1)S(1)}, bf16[2,288,128]{2,1,0:T(8,128)(2,1)S(1)}, u32[]{:S(2)}, u32[]{:S(2)}) %collective-permute-start.19) | collective-permute-done | bytes 147488 | tf_op jit(solution)/shard_map/ppermute | solution.py:376
  85.1 2.5 %collective-permute-done.18.rest_1_ = bf16[2,288,128]{2,1,0:T(8,128)(2,1)S(1)} collective-permute-done((bf16[2,288,128]{2,1,0:T(8,128)(2,1)S(1)}, bf16[2,288,128]{2,1,0:T(8,128)(2,1)S(1)}, u32[]{:S(2)}, u32[]{:S(2)}) %collective-permute-start.18) | collective-permute-done | bytes 147488 | tf_op jit(solution)/shard_map/ppermute | solution.py:376
  87.6 1.5 %collective-permute-done.17.rest_0_ = bf16[2,288,128]{2,1,0:T(8,128)(2,1)S(1)} collective-permute-done((bf16[2,288,128]{2,1,0:T(8,128)(2,1)S(1)}, bf16[2,288,128]{2,1,0:T(8,128)(2,1)S(1)}, u32[]{:S(2)}, u32[]{:S(2)}) %collective-permute-start.17) | collective-permute-done | bytes 147488 | tf_op jit(solution)/shard_map/ppermute | solution.py:376
  89.1 1.6 %latent_owner.1 = bf16[256,288]{1,0:T(8,128)(2,1)} custom-call(s32[64]{0:T(128)} %order.7, f32[2,288,128]{2,1,0:T(8,128)S(1)} %slice_bitcast_fusion.4.first, bf16[2,288,128]{2,1,0:T(8,128)(2,1)S(1)} %collective-permute-done.17.rest_0_, bf16[2,288,128]{2,1,0:T(8,128)(2,1)S(1)} %collective-permute-done.18.rest_1_, ...), custom_call_target="tpu_custom_call" | custom-call | tf_op jit(solution)/shard_map/latent_owner/pallas_call | solution.py:76
  90.6 18.2 %all_to_all.5 = bf16[16,16,288]{2,1,0:T(8,128)(2,1)S(1)} all-to-all(bf16[16,16,288]{2,1,0:T(8,128)(2,1)} %bitcast.41), channel_id=1, replica_groups=mesh['x'=4,'y'=4,'c'=2,'z'=8] {'c','z'}, dimensions={0} | all-to-all | bytes 294912 | tf_op jit(solution)/shard_map/all_to_all | solution.py:407
  108.8 0.7 pad_maximum_fusion.1
  (9 shorter events, 0.1 us)
Async XLA Ops:
  2.3 6.6 %collective-permute-start.2 = (bf16[576,128]{1,0:T(8,128)(2,1)}, bf16[576,128]{1,0:T(8,128)(2,1)S(1)}, u32[]{:S(2)}, u32[]{:S(2)}) collective-permute-start(bf16[576,128]{1,0:T(8,128)(2,1)} %latent_own.1), channel_id=1, source_target_pairs={{48,0},{200,8},{0,16},{216,24},{16,32},{232,40},{32,48},{248,56},{... | collective-permute-start | bytes 442376 | tf_op jit(solution)/shard_map/ppermute | solution.py:376
  3.9 7.8 %collective-permute-start.1 = (bf16[576,128]{1,0:T(8,128)(2,1)}, bf16[576,128]{1,0:T(8,128)(2,1)S(1)}, u32[]{:S(2)}, u32[]{:S(2)}) collective-permute-start(bf16[576,128]{1,0:T(8,128)(2,1)} %latent_own.1), channel_id=1, source_target_pairs={{32,0},{136,8},{48,16},{152,24},{0,32},{168,40},{16,48},{184,56},{... | collective-permute-start | bytes 442376 | tf_op jit(solution)/shard_map/ppermute | solution.py:376
  6.8 5.4 %collective-permute-start = (bf16[576,128]{1,0:T(8,128)(2,1)}, bf16[576,128]{1,0:T(8,128)(2,1)S(1)}, u32[]{:S(2)}, u32[]{:S(2)}) collective-permute-start(bf16[576,128]{1,0:T(8,128)(2,1)} %latent_own.1), channel_id=1, source_target_pairs={{16,0},{72,8},{32,16},{88,24},{48,32},{104,40},{0,48},{120,56},{80... | collective-permute-start | bytes 442376 | tf_op jit(solution)/shard_map/ppermute | solution.py:376
  13.1 11.2 %collective-permute-start.5 = (bf16[4,576,128]{2,1,0:T(8,128)(2,1)S(1)}, bf16[4,576,128]{2,1,0:T(8,128)(2,1)S(1)}, u32[]{:S(2)}, u32[]{:S(2)}) collective-permute-start(bf16[4,576,128]{2,1,0:T(8,128)(2,1)S(1)} %pad_maximum_fusion.rest_0_), channel_id=1, source_target_pairs={{192,0},{56,8},{208,16},{8,24},{224,32},{24,40},{240,48},{40,56},{... | collective-permute-start | bytes 1769480 | tf_op jit(solution)/shard_map/ppermute | solution.py:376
  14.7 16.9 %collective-permute-start.4 = (bf16[4,576,128]{2,1,0:T(8,128)(2,1)S(1)}, bf16[4,576,128]{2,1,0:T(8,128)(2,1)S(1)}, u32[]{:S(2)}, u32[]{:S(2)}) collective-permute-start(bf16[4,576,128]{2,1,0:T(8,128)(2,1)S(1)} %pad_maximum_fusion.rest_0_), channel_id=1, source_target_pairs={{128,0},{40,8},{144,16},{56,24},{160,32},{8,40},{176,48},{24,56},{... | collective-permute-start | bytes 1769480 | tf_op jit(solution)/shard_map/ppermute | solution.py:376
  17.4 14.2 %collective-permute-start.3 = (bf16[4,576,128]{2,1,0:T(8,128)(2,1)S(1)}, bf16[4,576,128]{2,1,0:T(8,128)(2,1)S(1)}, u32[]{:S(2)}, u32[]{:S(2)}) collective-permute-start(bf16[4,576,128]{2,1,0:T(8,128)(2,1)S(1)} %pad_maximum_fusion.rest_0_), channel_id=1, source_target_pairs={{64,0},{24,8},{80,16},{40,24},{96,32},{56,40},{112,48},{8,56},{128... | collective-permute-start | bytes 1769480 | tf_op jit(solution)/shard_map/ppermute | solution.py:376
  18.9 13.3 %collective-permute-start.6 = (bf16[4,576,128]{2,1,0:T(8,128)(2,1)S(1)}, bf16[4,576,128]{2,1,0:T(8,128)(2,1)S(1)}, u32[]{:S(2)}, u32[]{:S(2)}) collective-permute-start(bf16[4,576,128]{2,1,0:T(8,128)(2,1)S(1)} %pad_maximum_fusion.rest_0_), channel_id=1, source_target_pairs={{0,8},{8,0},{1,9},{9,1},{2,10},{10,2},{3,11},{11,3},{4,12},{12,4},... | collective-permute-start | bytes 1769480 | tf_op jit(solution)/shard_map/ppermute | solution.py:380
  24.3 7.8 %collective-permute-start.9 = (bf16[4,576,128]{2,1,0:T(8,128)(2,1)S(1)}, bf16[4,576,128]{2,1,0:T(8,128)(2,1)S(1)}, u32[]{:S(2)}, u32[]{:S(2)}) collective-permute-start(bf16[4,576,128]{2,1,0:T(8,128)(2,1)S(1)} %collective-permute-done.5.rest_3_), channel_id=1, source_target_pairs={{0,8},{8,0},{1,9},{9,1},{2,10},{10,2},{3,11},{11,3},{4,12},{12,4},... | collective-permute-start | bytes 1769480 | tf_op jit(solution)/shard_map/ppermute | solution.py:380
  31.6 2.0 %collective-permute-start.8 = (bf16[4,576,128]{2,1,0:T(8,128)(2,1)S(1)}, bf16[4,576,128]{2,1,0:T(8,128)(2,1)S(1)}, u32[]{:S(2)}, u32[]{:S(2)}) collective-permute-start(bf16[4,576,128]{2,1,0:T(8,128)(2,1)S(1)} %collective-permute-done.4.rest_2_), channel_id=1, source_target_pairs={{0,8},{8,0},{1,9},{9,1},{2,10},{10,2},{3,11},{11,3},{4,12},{12,4},... | collective-permute-start | bytes 1769480 | tf_op jit(solution)/shard_map/ppermute | solution.py:380
  31.6 2.8 %collective-permute-start.7 = (bf16[4,576,128]{2,1,0:T(8,128)(2,1)S(1)}, bf16[4,576,128]{2,1,0:T(8,128)(2,1)S(1)}, u32[]{:S(2)}, u32[]{:S(2)}) collective-permute-start(bf16[4,576,128]{2,1,0:T(8,128)(2,1)S(1)} %collective-permute-done.3.rest_1_), channel_id=1, source_target_pairs={{0,8},{8,0},{1,9},{9,1},{2,10},{10,2},{3,11},{11,3},{4,12},{12,4},... | collective-permute-start | bytes 1769480 | tf_op jit(solution)/shard_map/ppermute | solution.py:380
  55.3 2.1 %collective-permute-start.13 = (bf16[4,2,288,128]{3,2,1,0:T(8,128)(2,1)S(1)}, bf16[4,2,288,128]{3,2,1,0:T(8,128)(2,1)S(1)}, u32[]{:S(2)}, u32[]{:S(2)}) collective-permute-start(bf16[4,2,288,128]{3,2,1,0:T(8,128)(2,1)S(1)} %get-tuple-element.23), channel_id=1, source_target_pairs={{0,8},{8,0},{1,9},{9,1},{2,10},{10,2},{3,11},{11,3},{4,12},{12,4},... | collective-permute-start | bytes 1769480 | tf_op jit(solution)/shard_map/ppermute | solution.py:380
  55.5 2.8 %collective-permute-start.12 = (bf16[4,2,288,128]{3,2,1,0:T(8,128)(2,1)S(1)}, bf16[4,2,288,128]{3,2,1,0:T(8,128)(2,1)S(1)}, u32[]{:S(2)}, u32[]{:S(2)}) collective-permute-start(bf16[4,2,288,128]{3,2,1,0:T(8,128)(2,1)S(1)} %get-tuple-element.24), channel_id=1, source_target_pairs={{0,8},{8,0},{1,9},{9,1},{2,10},{10,2},{3,11},{11,3},{4,12},{12,4},... | collective-permute-start | bytes 1769480 | tf_op jit(solution)/shard_map/ppermute | solution.py:380
  55.9 3.2 %collective-permute-start.11 = (bf16[4,2,288,128]{3,2,1,0:T(8,128)(2,1)S(1)}, bf16[4,2,288,128]{3,2,1,0:T(8,128)(2,1)S(1)}, u32[]{:S(2)}, u32[]{:S(2)}) collective-permute-start(bf16[4,2,288,128]{3,2,1,0:T(8,128)(2,1)S(1)} %get-tuple-element.25), channel_id=1, source_target_pairs={{0,8},{8,0},{1,9},{9,1},{2,10},{10,2},{3,11},{11,3},{4,12},{12,4},... | collective-permute-start | bytes 1769480 | tf_op jit(solution)/shard_map/ppermute | solution.py:380
  56.0 15.7 %collective-permute-start.10 = (bf16[4,2,288,128]{3,2,1,0:T(8,128)(2,1)S(1)}, bf16[4,2,288,128]{3,2,1,0:T(8,128)(2,1)S(1)}, u32[]{:S(2)}, u32[]{:S(2)}) collective-permute-start(bf16[4,2,288,128]{3,2,1,0:T(8,128)(2,1)S(1)} %get-tuple-element.22), channel_id=1, source_target_pairs={{0,8},{8,0},{1,9},{9,1},{2,10},{10,2},{3,11},{11,3},{4,12},{12,4},... | collective-permute-start | bytes 1769480 | tf_op jit(solution)/shard_map/ppermute | solution.py:380
  59.1 5.1 %copy-start = (s32[64]{0:T(128)S(1)}, s32[64]{0:T(128)}, u32[]{:S(2)}) copy-start(s32[64]{0:T(128)} %order.7) | copy-start | bytes 772
  59.6 12.1 %collective-permute-start.14 = (bf16[4,2,288,128]{3,2,1,0:T(8,128)(2,1)S(1)}, bf16[4,2,288,128]{3,2,1,0:T(8,128)(2,1)S(1)}, u32[]{:S(2)}, u32[]{:S(2)}) collective-permute-start(bf16[4,2,288,128]{3,2,1,0:T(8,128)(2,1)S(1)} %get-tuple-element.15), channel_id=1, source_target_pairs={{192,0},{56,8},{208,16},{8,24},{224,32},{24,40},{240,48},{40,56},{... | collective-permute-start | bytes 1769480 | tf_op jit(solution)/shard_map/ppermute | solution.py:376
  60.5 16.6 %collective-permute-start.15 = (bf16[4,2,288,128]{3,2,1,0:T(8,128)(2,1)S(1)}, bf16[4,2,288,128]{3,2,1,0:T(8,128)(2,1)S(1)}, u32[]{:S(2)}, u32[]{:S(2)}) collective-permute-start(bf16[4,2,288,128]{3,2,1,0:T(8,128)(2,1)S(1)} %get-tuple-element.16), channel_id=1, source_target_pairs={{128,0},{40,8},{144,16},{56,24},{160,32},{8,40},{176,48},{24,56},{... | collective-permute-start | bytes 1769480 | tf_op jit(solution)/shard_map/ppermute | solution.py:376
  62.9 15.1 %collective-permute-start.16 = (bf16[4,2,288,128]{3,2,1,0:T(8,128)(2,1)S(1)}, bf16[4,2,288,128]{3,2,1,0:T(8,128)(2,1)S(1)}, u32[]{:S(2)}, u32[]{:S(2)}) collective-permute-start(bf16[4,2,288,128]{3,2,1,0:T(8,128)(2,1)S(1)} %get-tuple-element.17), channel_id=1, source_target_pairs={{64,0},{24,8},{80,16},{40,24},{96,32},{56,40},{112,48},{8,56},{128... | collective-permute-start | bytes 1769480 | tf_op jit(solution)/shard_map/ppermute | solution.py:376
  78.5 6.6 %collective-permute-start.19 = (bf16[2,288,128]{2,1,0:T(8,128)(2,1)S(1)}, bf16[2,288,128]{2,1,0:T(8,128)(2,1)S(1)}, u32[]{:S(2)}, u32[]{:S(2)}) collective-permute-start(bf16[2,288,128]{2,1,0:T(8,128)(2,1)S(1)} %get-tuple-element.29), channel_id=1, source_target_pairs={{16,0},{72,8},{32,16},{88,24},{48,32},{104,40},{0,48},{120,56},{80... | collective-permute-start | bytes 442376 | tf_op jit(solution)/shard_map/ppermute | solution.py:376
  80.8 6.8 %collective-permute-start.18 = (bf16[2,288,128]{2,1,0:T(8,128)(2,1)S(1)}, bf16[2,288,128]{2,1,0:T(8,128)(2,1)S(1)}, u32[]{:S(2)}, u32[]{:S(2)}) collective-permute-start(bf16[2,288,128]{2,1,0:T(8,128)(2,1)S(1)} %get-tuple-element.30), channel_id=1, source_target_pairs={{32,0},{136,8},{48,16},{152,24},{0,32},{168,40},{16,48},{184,56},{... | collective-permute-start | bytes 442376 | tf_op jit(solution)/shard_map/ppermute | solution.py:376
  81.6 7.5 %collective-permute-start.17 = (bf16[2,288,128]{2,1,0:T(8,128)(2,1)S(1)}, bf16[2,288,128]{2,1,0:T(8,128)(2,1)S(1)}, u32[]{:S(2)}, u32[]{:S(2)}) collective-permute-start(bf16[2,288,128]{2,1,0:T(8,128)(2,1)S(1)} %get-tuple-element.31), channel_id=1, source_target_pairs={{48,0},{200,8},{0,16},{216,24},{16,32},{232,40},{32,48},{248,56},{... | collective-permute-start | bytes 442376 | tf_op jit(solution)/shard_map/ppermute | solution.py:376

commit v7 on v6

--- a/solution.py
+++ b/solution.py
@@ -390,10 +390,19 @@
     keys, dscores, keep, send = run_grads(
         group_order, q_latent, out_grad, saved_out, pieces, sides
     )
-    both = {}
-    for d in sorted(range(sides), key=lambda d: -min(d, sides - d)):
-        both[d] = keep[d].astype(jnp.float32) + swap(send[d]).astype(jnp.float32)
-    low = [both[d].astype(jnp.bfloat16) for d in range(1, sides)]
+    far_step = sides // 2
+    others = [d for d in range(sides) if d != far_step]
+
+    def add(d, sent):
+        return keep[d].astype(jnp.float32) + swap(sent).astype(jnp.float32)
+
+    both = {far_step: add(far_step, send[far_step])}
+    low_far, sent = lax.optimization_barrier(
+        (both[far_step].astype(jnp.bfloat16), [send[d] for d in others])
+    )
+    for d, part in zip(others, sent):
+        both[d] = add(d, part)
+    low = [low_far if d == far_step else both[d].astype(jnp.bfloat16) for d in range(1, sides)]
     low, dscores = lax.optimization_barrier((low, dscores))
     q_grad = run_queries(group_order, dscores, keys, sides, q_latent.shape)
     total = both[0]

time: 110 us -> 111 us (level)
  waiting for transfers between devices: 34.7 us -> 36.3 us
    ppermute x8, waiting for transfers between devices: 5 us -> 6.49 us  [swap(): return lax.ppermute(a, 'c', [(0, 1), (1, 0)])]
where the time goes in v7:
time: 111 us
  waiting for transfers between devices  36.3 us (33%)
  Pallas kernels  31.5 us (28%)
  starting transfers between devices  21.3 us (19%)
  blocking collectives  18.2 us (16%)
  other arithmetic  2.62 us (2%)
    ppermute x12, waiting for transfers between devices, hop(): return lax.ppermute(a, ('x', 'y', 'c'), moves)  29.8 us
    pallas_call x1, Pallas kernels, run_grads(): pl.pallas_call(functools.partial(grads_kernel, sides=sides, rows=rows), o...  20.8 us
    ppermute x12, starting transfers between devices, hop(): return lax.ppermute(a, ('x', 'y', 'c'), moves)  19.9 us
    all_to_all x1, blocking collectives, shards(): parts = lax.all_to_all(by_owner, ('c', 'z'), 0, 0, tiled=True)  18.2 us
    pallas_call x1, Pallas kernels, run_queries(): pl.pallas_call(functools.partial(query_kernel, sides=sides, rows=rows), o...  7.48 us
    ppermute x8, waiting for transfers between devices, swap(): return lax.ppermute(a, 'c', [(0, 1), (1, 0)])  6.49 us
  transfers between devices with their start and end apart: 20, of which 15 were waited for; matrix products, arithmetic and copies ran while one was open for 0% of the time, Pallas kernels for 7%

profile of v7, /device:TPU:32, one launch (start us, length us, event | category | flops | bytes accessed | tf_op | source)
XLA Modules:
  0.0 110.9 jit_solution(13931798448183462589)
XLA Ops:
  0.6 1.7 %latent_own.1 = bf16[576,128]{1,0:T(8,128)(2,1)} custom-call(s32[64]{0:T(128)} %order.7, bf16[576,128]{1,0:T(8,128)(2,1)} %bitcast.46), custom_call_target="tpu_custom_call" | custom-call | tf_op jit(solution)/shard_map/latent_own/pallas_call | solution.py:52
  2.3 1.6 %collective-permute-start.2 = (bf16[576,128]{1,0:T(8,128)(2,1)}, bf16[576,128]{1,0:T(8,128)(2,1)S(1)}, u32[]{:S(2)}, u32[]{:S(2)}) collective-permute-start(bf16[576,128]{1,0:T(8,128)(2,1)} %latent_own.1), channel_id=1, source_target_pairs={{48,0},{200,8},{0,16},{216,24},{16,32},{232,40},{32,48},{248,56},{... | collective-permute-start | bytes 442376 | tf_op jit(solution)/shard_map/ppermute | solution.py:376
  3.9 2.9 %collective-permute-start.1 = (bf16[576,128]{1,0:T(8,128)(2,1)}, bf16[576,128]{1,0:T(8,128)(2,1)S(1)}, u32[]{:S(2)}, u32[]{:S(2)}) collective-permute-start(bf16[576,128]{1,0:T(8,128)(2,1)} %latent_own.1), channel_id=1, source_target_pairs={{32,0},{136,8},{48,16},{152,24},{0,32},{168,40},{16,48},{184,56},{... | collective-permute-start | bytes 442376 | tf_op jit(solution)/shard_map/ppermute | solution.py:376
  6.8 1.3 %collective-permute-start = (bf16[576,128]{1,0:T(8,128)(2,1)}, bf16[576,128]{1,0:T(8,128)(2,1)S(1)}, u32[]{:S(2)}, u32[]{:S(2)}) collective-permute-start(bf16[576,128]{1,0:T(8,128)(2,1)} %latent_own.1), channel_id=1, source_target_pairs={{16,0},{72,8},{32,16},{88,24},{48,32},{104,40},{0,48},{120,56},{80... | collective-permute-start | bytes 442376 | tf_op jit(solution)/shard_map/ppermute | solution.py:376
  8.1 0.7 collective-permute-done.2
  8.9 2.8 %collective-permute-done.1 = bf16[576,128]{1,0:T(8,128)(2,1)S(1)} collective-permute-done((bf16[576,128]{1,0:T(8,128)(2,1)}, bf16[576,128]{1,0:T(8,128)(2,1)S(1)}, u32[]{:S(2)}, u32[]{:S(2)}) %collective-permute-start.1) | collective-permute-done | bytes 147488 | tf_op jit(solution)/shard_map/ppermute | solution.py:376
  11.7 0.4 collective-permute-done
  12.1 1.0 pad_maximum_fusion.rest_0_
  13.1 1.6 %collective-permute-start.5 = (bf16[4,576,128]{2,1,0:T(8,128)(2,1)S(1)}, bf16[4,576,128]{2,1,0:T(8,128)(2,1)S(1)}, u32[]{:S(2)}, u32[]{:S(2)}) collective-permute-start(bf16[4,576,128]{2,1,0:T(8,128)(2,1)S(1)} %pad_maximum_fusion.rest_0_), channel_id=1, source_target_pairs={{192,0},{56,8},{208,16},{8,24},{224,32},{24,40},{240,48},{40,56},{... | collective-permute-start | bytes 1769480 | tf_op jit(solution)/shard_map/ppermute | solution.py:376
  14.7 2.7 %collective-permute-start.4 = (bf16[4,576,128]{2,1,0:T(8,128)(2,1)S(1)}, bf16[4,576,128]{2,1,0:T(8,128)(2,1)S(1)}, u32[]{:S(2)}, u32[]{:S(2)}) collective-permute-start(bf16[4,576,128]{2,1,0:T(8,128)(2,1)S(1)} %pad_maximum_fusion.rest_0_), channel_id=1, source_target_pairs={{128,0},{40,8},{144,16},{56,24},{160,32},{8,40},{176,48},{24,56},{... | collective-permute-start | bytes 1769480 | tf_op jit(solution)/shard_map/ppermute | solution.py:376
  17.4 1.4 %collective-permute-start.3 = (bf16[4,576,128]{2,1,0:T(8,128)(2,1)S(1)}, bf16[4,576,128]{2,1,0:T(8,128)(2,1)S(1)}, u32[]{:S(2)}, u32[]{:S(2)}) collective-permute-start(bf16[4,576,128]{2,1,0:T(8,128)(2,1)S(1)} %pad_maximum_fusion.rest_0_), channel_id=1, source_target_pairs={{64,0},{24,8},{80,16},{40,24},{96,32},{56,40},{112,48},{8,56},{128... | collective-permute-start | bytes 1769480 | tf_op jit(solution)/shard_map/ppermute | solution.py:376
  18.9 0.0 collective-permute-start.6
  18.9 5.4 %collective-permute-done.5.rest_3_ = bf16[4,576,128]{2,1,0:T(8,128)(2,1)S(1)} collective-permute-done((bf16[4,576,128]{2,1,0:T(8,128)(2,1)S(1)}, bf16[4,576,128]{2,1,0:T(8,128)(2,1)S(1)}, u32[]{:S(2)}, u32[]{:S(2)}) %collective-permute-start.5) | collective-permute-done | bytes 589856 | tf_op jit(solution)/shard_map/ppermute | solution.py:376
  24.3 7.3 %collective-permute-done.4.rest_2_ = bf16[4,576,128]{2,1,0:T(8,128)(2,1)S(1)} collective-permute-done((bf16[4,576,128]{2,1,0:T(8,128)(2,1)S(1)}, bf16[4,576,128]{2,1,0:T(8,128)(2,1)S(1)}, u32[]{:S(2)}, u32[]{:S(2)}) %collective-permute-start.4) | collective-permute-done | bytes 589856 | tf_op jit(solution)/shard_map/ppermute | solution.py:376
  31.6 0.5 collective-permute-start.7
  32.1 0.0 collective-permute-done.9.rest_7_
  32.1 1.5 %collective-permute-done.8.rest_6_ = bf16[4,576,128]{2,1,0:T(8,128)(2,1)S(1)} collective-permute-done((bf16[4,576,128]{2,1,0:T(8,128)(2,1)S(1)}, bf16[4,576,128]{2,1,0:T(8,128)(2,1)S(1)}, u32[]{:S(2)}, u32[]{:S(2)}) %collective-permute-start.8) | collective-permute-done | bytes 589856 | tf_op jit(solution)/shard_map/ppermute | solution.py:380
  33.6 0.8 collective-permute-done.7.rest_5_
  34.5 20.8 %latent_grads.1 = (bf16[576,4096]{1,0:T(8,128)(2,1)S(1)}, bf16[17,512,256]{2,1,0:T(8,128)(2,1)S(1)}, bf16[4,4,2,288,128]{4,3,2,1,0:T(8,128)(2,1)S(1)}, bf16[4,4,2,288,128]{4,3,2,1,0:T(8,128)(2,1)S(1)}) custom-call(s32[64]{0:T(128)} %order.7, bf16[128,4608]{1,0:T(8,128)(2,1)} %q_in.1, bf16[128,4096]{1,0:T(8,128)(2,1)} %g_in.1, bf16[128,4096]{1,0:T(8,128)(2,1)} %o_in.1, ...), custom_call_target="tpu_custom_call" | custom-call | flops 9697230848 | bytes 25165824 | tf_op jit(solution)/shard_map/latent_grads/pallas_call | solution.py:315
  55.2 0.2 slice_bitcast_fusion
  55.5 0.1 collective-permute-start.10
  55.6 2.0 %collective-permute-done.10 = bf16[4,2,288,128]{3,2,1,0:T(8,128)(2,1)S(1)} collective-permute-done((bf16[4,2,288,128]{3,2,1,0:T(8,128)(2,1)S(1)}, bf16[4,2,288,128]{3,2,1,0:T(8,128)(2,1)S(1)}, u32[]{:S(2)}, u32[]{:S(2)}) %collective-permute-start.10) | collective-permute-done | bytes 589856 | tf_op jit(solution)/shard_map/ppermute | solution.py:380
  57.5 0.2 fusion.2
  57.7 0.0 copy-start
  57.7 0.2 collective-permute-start.12
  57.9 0.4 collective-permute-start.13
  58.3 0.1 collective-permute-start.11
  58.5 1.4 %collective-permute-done.12 = bf16[4,2,288,128]{3,2,1,0:T(8,128)(2,1)S(1)} collective-permute-done((bf16[4,2,288,128]{3,2,1,0:T(8,128)(2,1)S(1)}, bf16[4,2,288,128]{3,2,1,0:T(8,128)(2,1)S(1)}, u32[]{:S(2)}, u32[]{:S(2)}) %collective-permute-start.12) | collective-permute-done | bytes 589856 | tf_op jit(solution)/shard_map/ppermute | solution.py:380
  59.8 0.8 collective-permute-done.13
  60.7 0.3 fusion
  61.0 1.0 collective-permute-start.14
  62.0 2.0 %collective-permute-start.15 = (bf16[4,2,288,128]{3,2,1,0:T(8,128)(2,1)S(1)}, bf16[4,2,288,128]{3,2,1,0:T(8,128)(2,1)S(1)}, u32[]{:S(2)}, u32[]{:S(2)}) collective-permute-start(bf16[4,2,288,128]{3,2,1,0:T(8,128)(2,1)S(1)} %fusion.2), channel_id=1, source_target_pairs={{128,0},{40,8},{144,16},{56,24},{160,32},{8,40},{176,48},{24,56},{... | collective-permute-start | bytes 1769480 | tf_op jit(solution)/shard_map/ppermute | solution.py:376
  64.0 1.5 %collective-permute-start.16 = (bf16[4,2,288,128]{3,2,1,0:T(8,128)(2,1)S(1)}, bf16[4,2,288,128]{3,2,1,0:T(8,128)(2,1)S(1)}, u32[]{:S(2)}, u32[]{:S(2)}) collective-permute-start(bf16[4,2,288,128]{3,2,1,0:T(8,128)(2,1)S(1)} %get-tuple-element.25), channel_id=1, source_target_pairs={{64,0},{24,8},{80,16},{40,24},{96,32},{56,40},{112,48},{8,56},{128... | collective-permute-start | bytes 1769480 | tf_op jit(solution)/shard_map/ppermute | solution.py:376
  65.5 7.5 %latent_queries.1 = bf16[128,4608]{1,0:T(8,128)(2,1)} custom-call(s32[64]{0:T(128)S(1)} %copy-done, bf16[17,512,256]{2,1,0:T(8,128)(2,1)S(1)} %get-tuple-element.26.dscores, bf16[576,4096]{1,0:T(8,128)(2,1)S(1)} %get-tuple-element.27.keys), custom_call_target="tpu_custom_call" | custom-call | flops 2566914048 | bytes 10485760 | tf_op jit(solution)/shard_map/latent_queries/pallas_call | solution.py:353
  73.0 0.0 collective-permute-done.11
  73.0 5.5 %collective-permute-done.14 = bf16[4,2,288,128]{3,2,1,0:T(8,128)(2,1)S(1)} collective-permute-done((bf16[4,2,288,128]{3,2,1,0:T(8,128)(2,1)S(1)}, bf16[4,2,288,128]{3,2,1,0:T(8,128)(2,1)S(1)}, u32[]{:S(2)}, u32[]{:S(2)}) %collective-permute-start.14) | collective-permute-done | bytes 589856 | tf_op jit(solution)/shard_map/ppermute | solution.py:376
  78.5 0.9 collective-permute-done.16
  79.4 0.3 fusion.5
  79.7 0.1 convert.10
  79.8 2.4 %collective-permute-start.19 = (bf16[2,288,128]{2,1,0:T(8,128)(2,1)S(1)}, bf16[2,288,128]{2,1,0:T(8,128)(2,1)S(1)}, u32[]{:S(2)}, u32[]{:S(2)}) collective-permute-start(bf16[2,288,128]{2,1,0:T(8,128)(2,1)S(1)} %get-tuple-element.36), channel_id=1, source_target_pairs={{16,0},{72,8},{32,16},{88,24},{48,32},{104,40},{0,48},{120,56},{80... | collective-permute-start | bytes 442376 | tf_op jit(solution)/shard_map/ppermute | solution.py:376
  82.2 0.8 collective-permute-start.18
  83.0 0.7 collective-permute-start.17
  83.7 2.8 %collective-permute-done.19.rest_2_ = bf16[2,288,128]{2,1,0:T(8,128)(2,1)S(1)} collective-permute-done((bf16[2,288,128]{2,1,0:T(8,128)(2,1)S(1)}, bf16[2,288,128]{2,1,0:T(8,128)(2,1)S(1)}, u32[]{:S(2)}, u32[]{:S(2)}) %collective-permute-start.19) | collective-permute-done | bytes 147488 | tf_op jit(solution)/shard_map/ppermute | solution.py:376
  86.5 2.5 %collective-permute-done.18.rest_1_ = bf16[2,288,128]{2,1,0:T(8,128)(2,1)S(1)} collective-permute-done((bf16[2,288,128]{2,1,0:T(8,128)(2,1)S(1)}, bf16[2,288,128]{2,1,0:T(8,128)(2,1)S(1)}, u32[]{:S(2)}, u32[]{:S(2)}) %collective-permute-start.18) | collective-permute-done | bytes 147488 | tf_op jit(solution)/shard_map/ppermute | solution.py:376
  89.0 1.5 %collective-permute-done.17.rest_0_ = bf16[2,288,128]{2,1,0:T(8,128)(2,1)S(1)} collective-permute-done((bf16[2,288,128]{2,1,0:T(8,128)(2,1)S(1)}, bf16[2,288,128]{2,1,0:T(8,128)(2,1)S(1)}, u32[]{:S(2)}, u32[]{:S(2)}) %collective-permute-start.17) | collective-permute-done | bytes 147488 | tf_op jit(solution)/shard_map/ppermute | solution.py:376
  90.4 1.6 %latent_owner.1 = bf16[256,288]{1,0:T(8,128)(2,1)} custom-call(s32[64]{0:T(128)} %order.7, f32[2,288,128]{2,1,0:T(8,128)S(1)} %slice_bitcast_fusion.4.first, bf16[2,288,128]{2,1,0:T(8,128)(2,1)S(1)} %collective-permute-done.17.rest_0_, bf16[2,288,128]{2,1,0:T(8,128)(2,1)S(1)} %collective-permute-done.18.rest_1_, ...), custom_call_target="tpu_custom_call" | custom-call | tf_op jit(solution)/shard_map/latent_owner/pallas_call | solution.py:76
  92.0 18.2 %all_to_all.5 = bf16[16,16,288]{2,1,0:T(8,128)(2,1)S(1)} all-to-all(bf16[16,16,288]{2,1,0:T(8,128)(2,1)} %bitcast.41), channel_id=1, replica_groups=mesh['x'=4,'y'=4,'c'=2,'z'=8] {'c','z'}, dimensions={0} | all-to-all | bytes 294912 | tf_op jit(solution)/shard_map/all_to_all | solution.py:416
  110.2 0.7 pad_maximum_fusion.1
  (10 shorter events, 0.1 us)
Async XLA Ops:
  2.3 6.6 %collective-permute-start.2 = (bf16[576,128]{1,0:T(8,128)(2,1)}, bf16[576,128]{1,0:T(8,128)(2,1)S(1)}, u32[]{:S(2)}, u32[]{:S(2)}) collective-permute-start(bf16[576,128]{1,0:T(8,128)(2,1)} %latent_own.1), channel_id=1, source_target_pairs={{48,0},{200,8},{0,16},{216,24},{16,32},{232,40},{32,48},{248,56},{... | collective-permute-start | bytes 442376 | tf_op jit(solution)/shard_map/ppermute | solution.py:376
  3.9 7.8 %collective-permute-start.1 = (bf16[576,128]{1,0:T(8,128)(2,1)}, bf16[576,128]{1,0:T(8,128)(2,1)S(1)}, u32[]{:S(2)}, u32[]{:S(2)}) collective-permute-start(bf16[576,128]{1,0:T(8,128)(2,1)} %latent_own.1), channel_id=1, source_target_pairs={{32,0},{136,8},{48,16},{152,24},{0,32},{168,40},{16,48},{184,56},{... | collective-permute-start | bytes 442376 | tf_op jit(solution)/shard_map/ppermute | solution.py:376
  6.8 5.4 %collective-permute-start = (bf16[576,128]{1,0:T(8,128)(2,1)}, bf16[576,128]{1,0:T(8,128)(2,1)S(1)}, u32[]{:S(2)}, u32[]{:S(2)}) collective-permute-start(bf16[576,128]{1,0:T(8,128)(2,1)} %latent_own.1), channel_id=1, source_target_pairs={{16,0},{72,8},{32,16},{88,24},{48,32},{104,40},{0,48},{120,56},{80... | collective-permute-start | bytes 442376 | tf_op jit(solution)/shard_map/ppermute | solution.py:376
  13.1 11.2 %collective-permute-start.5 = (bf16[4,576,128]{2,1,0:T(8,128)(2,1)S(1)}, bf16[4,576,128]{2,1,0:T(8,128)(2,1)S(1)}, u32[]{:S(2)}, u32[]{:S(2)}) collective-permute-start(bf16[4,576,128]{2,1,0:T(8,128)(2,1)S(1)} %pad_maximum_fusion.rest_0_), channel_id=1, source_target_pairs={{192,0},{56,8},{208,16},{8,24},{224,32},{24,40},{240,48},{40,56},{... | collective-permute-start | bytes 1769480 | tf_op jit(solution)/shard_map/ppermute | solution.py:376
  14.7 16.9 %collective-permute-start.4 = (bf16[4,576,128]{2,1,0:T(8,128)(2,1)S(1)}, bf16[4,576,128]{2,1,0:T(8,128)(2,1)S(1)}, u32[]{:S(2)}, u32[]{:S(2)}) collective-permute-start(bf16[4,576,128]{2,1,0:T(8,128)(2,1)S(1)} %pad_maximum_fusion.rest_0_), channel_id=1, source_target_pairs={{128,0},{40,8},{144,16},{56,24},{160,32},{8,40},{176,48},{24,56},{... | collective-permute-start | bytes 1769480 | tf_op jit(solution)/shard_map/ppermute | solution.py:376
  17.4 14.2 %collective-permute-start.3 = (bf16[4,576,128]{2,1,0:T(8,128)(2,1)S(1)}, bf16[4,576,128]{2,1,0:T(8,128)(2,1)S(1)}, u32[]{:S(2)}, u32[]{:S(2)}) collective-permute-start(bf16[4,576,128]{2,1,0:T(8,128)(2,1)S(1)} %pad_maximum_fusion.rest_0_), channel_id=1, source_target_pairs={{64,0},{24,8},{80,16},{40,24},{96,32},{56,40},{112,48},{8,56},{128... | collective-permute-start | bytes 1769480 | tf_op jit(solution)/shard_map/ppermute | solution.py:376
  18.9 13.3 %collective-permute-start.6 = (bf16[4,576,128]{2,1,0:T(8,128)(2,1)S(1)}, bf16[4,576,128]{2,1,0:T(8,128)(2,1)S(1)}, u32[]{:S(2)}, u32[]{:S(2)}) collective-permute-start(bf16[4,576,128]{2,1,0:T(8,128)(2,1)S(1)} %pad_maximum_fusion.rest_0_), channel_id=1, source_target_pairs={{0,8},{8,0},{1,9},{9,1},{2,10},{10,2},{3,11},{11,3},{4,12},{12,4},... | collective-permute-start | bytes 1769480 | tf_op jit(solution)/shard_map/ppermute | solution.py:380
  24.3 7.8 %collective-permute-start.9 = (bf16[4,576,128]{2,1,0:T(8,128)(2,1)S(1)}, bf16[4,576,128]{2,1,0:T(8,128)(2,1)S(1)}, u32[]{:S(2)}, u32[]{:S(2)}) collective-permute-start(bf16[4,576,128]{2,1,0:T(8,128)(2,1)S(1)} %collective-permute-done.5.rest_3_), channel_id=1, source_target_pairs={{0,8},{8,0},{1,9},{9,1},{2,10},{10,2},{3,11},{11,3},{4,12},{12,4},... | collective-permute-start | bytes 1769480 | tf_op jit(solution)/shard_map/ppermute | solution.py:380
  31.6 2.0 %collective-permute-start.8 = (bf16[4,576,128]{2,1,0:T(8,128)(2,1)S(1)}, bf16[4,576,128]{2,1,0:T(8,128)(2,1)S(1)}, u32[]{:S(2)}, u32[]{:S(2)}) collective-permute-start(bf16[4,576,128]{2,1,0:T(8,128)(2,1)S(1)} %collective-permute-done.4.rest_2_), channel_id=1, source_target_pairs={{0,8},{8,0},{1,9},{9,1},{2,10},{10,2},{3,11},{11,3},{4,12},{12,4},... | collective-permute-start | bytes 1769480 | tf_op jit(solution)/shard_map/ppermute | solution.py:380
  31.6 2.8 %collective-permute-start.7 = (bf16[4,576,128]{2,1,0:T(8,128)(2,1)S(1)}, bf16[4,576,128]{2,1,0:T(8,128)(2,1)S(1)}, u32[]{:S(2)}, u32[]{:S(2)}) collective-permute-start(bf16[4,576,128]{2,1,0:T(8,128)(2,1)S(1)} %collective-permute-done.3.rest_1_), channel_id=1, source_target_pairs={{0,8},{8,0},{1,9},{9,1},{2,10},{10,2},{3,11},{11,3},{4,12},{12,4},... | collective-permute-start | bytes 1769480 | tf_op jit(solution)/shard_map/ppermute | solution.py:380
  55.5 2.1 %collective-permute-start.10 = (bf16[4,2,288,128]{3,2,1,0:T(8,128)(2,1)S(1)}, bf16[4,2,288,128]{3,2,1,0:T(8,128)(2,1)S(1)}, u32[]{:S(2)}, u32[]{:S(2)}) collective-permute-start(bf16[4,2,288,128]{3,2,1,0:T(8,128)(2,1)S(1)} %get-tuple-element.35), channel_id=1, source_target_pairs={{0,8},{8,0},{1,9},{9,1},{2,10},{10,2},{3,11},{11,3},{4,12},{12,4},... | collective-permute-start | bytes 1769480 | tf_op jit(solution)/shard_map/ppermute | solution.py:380
  57.7 7.8 %copy-start = (s32[64]{0:T(128)S(1)}, s32[64]{0:T(128)}, u32[]{:S(2)}) copy-start(s32[64]{0:T(128)} %order.7) | copy-start | bytes 772
  57.7 2.1 %collective-permute-start.12 = (bf16[4,2,288,128]{3,2,1,0:T(8,128)(2,1)S(1)}, bf16[4,2,288,128]{3,2,1,0:T(8,128)(2,1)S(1)}, u32[]{:S(2)}, u32[]{:S(2)}) collective-permute-start(bf16[4,2,288,128]{3,2,1,0:T(8,128)(2,1)S(1)} %get-tuple-element.19), channel_id=1, source_target_pairs={{0,8},{8,0},{1,9},{9,1},{2,10},{10,2},{3,11},{11,3},{4,12},{12,4},... | collective-permute-start | bytes 1769480 | tf_op jit(solution)/shard_map/ppermute | solution.py:380
  57.9 2.7 %collective-permute-start.13 = (bf16[4,2,288,128]{3,2,1,0:T(8,128)(2,1)S(1)}, bf16[4,2,288,128]{3,2,1,0:T(8,128)(2,1)S(1)}, u32[]{:S(2)}, u32[]{:S(2)}) collective-permute-start(bf16[4,2,288,128]{3,2,1,0:T(8,128)(2,1)S(1)} %get-tuple-element.21), channel_id=1, source_target_pairs={{0,8},{8,0},{1,9},{9,1},{2,10},{10,2},{3,11},{11,3},{4,12},{12,4},... | collective-permute-start | bytes 1769480 | tf_op jit(solution)/shard_map/ppermute | solution.py:380
  58.3 14.7 %collective-permute-start.11 = (bf16[4,2,288,128]{3,2,1,0:T(8,128)(2,1)S(1)}, bf16[4,2,288,128]{3,2,1,0:T(8,128)(2,1)S(1)}, u32[]{:S(2)}, u32[]{:S(2)}) collective-permute-start(bf16[4,2,288,128]{3,2,1,0:T(8,128)(2,1)S(1)} %get-tuple-element.18), channel_id=1, source_target_pairs={{0,8},{8,0},{1,9},{9,1},{2,10},{10,2},{3,11},{11,3},{4,12},{12,4},... | collective-permute-start | bytes 1769480 | tf_op jit(solution)/shard_map/ppermute | solution.py:380
  61.0 17.5 %collective-permute-start.14 = (bf16[4,2,288,128]{3,2,1,0:T(8,128)(2,1)S(1)}, bf16[4,2,288,128]{3,2,1,0:T(8,128)(2,1)S(1)}, u32[]{:S(2)}, u32[]{:S(2)}) collective-permute-start(bf16[4,2,288,128]{3,2,1,0:T(8,128)(2,1)S(1)} %get-tuple-element.23), channel_id=1, source_target_pairs={{192,0},{56,8},{208,16},{8,24},{224,32},{24,40},{240,48},{40,56},{... | collective-permute-start | bytes 1769480 | tf_op jit(solution)/shard_map/ppermute | solution.py:376
  62.0 16.5 %collective-permute-start.15 = (bf16[4,2,288,128]{3,2,1,0:T(8,128)(2,1)S(1)}, bf16[4,2,288,128]{3,2,1,0:T(8,128)(2,1)S(1)}, u32[]{:S(2)}, u32[]{:S(2)}) collective-permute-start(bf16[4,2,288,128]{3,2,1,0:T(8,128)(2,1)S(1)} %fusion.2), channel_id=1, source_target_pairs={{128,0},{40,8},{144,16},{56,24},{160,32},{8,40},{176,48},{24,56},{... | collective-permute-start | bytes 1769480 | tf_op jit(solution)/shard_map/ppermute | solution.py:376
  64.0 15.4 %collective-permute-start.16 = (bf16[4,2,288,128]{3,2,1,0:T(8,128)(2,1)S(1)}, bf16[4,2,288,128]{3,2,1,0:T(8,128)(2,1)S(1)}, u32[]{:S(2)}, u32[]{:S(2)}) collective-permute-start(bf16[4,2,288,128]{3,2,1,0:T(8,128)(2,1)S(1)} %get-tuple-element.25), channel_id=1, source_target_pairs={{64,0},{24,8},{80,16},{40,24},{96,32},{56,40},{112,48},{8,56},{128... | collective-permute-start | bytes 1769480 | tf_op jit(solution)/shard_map/ppermute | solution.py:376
  79.8 6.6 %collective-permute-start.19 = (bf16[2,288,128]{2,1,0:T(8,128)(2,1)S(1)}, bf16[2,288,128]{2,1,0:T(8,128)(2,1)S(1)}, u32[]{:S(2)}, u32[]{:S(2)}) collective-permute-start(bf16[2,288,128]{2,1,0:T(8,128)(2,1)S(1)} %get-tuple-element.36), channel_id=1, source_target_pairs={{16,0},{72,8},{32,16},{88,24},{48,32},{104,40},{0,48},{120,56},{80... | collective-permute-start | bytes 442376 | tf_op jit(solution)/shard_map/ppermute | solution.py:376
  82.2 6.8 %collective-permute-start.18 = (bf16[2,288,128]{2,1,0:T(8,128)(2,1)S(1)}, bf16[2,288,128]{2,1,0:T(8,128)(2,1)S(1)}, u32[]{:S(2)}, u32[]{:S(2)}) collective-permute-start(bf16[2,288,128]{2,1,0:T(8,128)(2,1)S(1)} %get-tuple-element.37), channel_id=1, source_target_pairs={{32,0},{136,8},{48,16},{152,24},{0,32},{168,40},{16,48},{184,56},{... | collective-permute-start | bytes 442376 | tf_op jit(solution)/shard_map/ppermute | solution.py:376
  83.0 7.4 %collective-permute-start.17 = (bf16[2,288,128]{2,1,0:T(8,128)(2,1)S(1)}, bf16[2,288,128]{2,1,0:T(8,128)(2,1)S(1)}, u32[]{:S(2)}, u32[]{:S(2)}) collective-permute-start(bf16[2,288,128]{2,1,0:T(8,128)(2,1)S(1)} %get-tuple-element.38), channel_id=1, source_target_pairs={{48,0},{200,8},{0,16},{216,24},{16,32},{232,40},{32,48},{248,56},{... | collective-permute-start | bytes 442376 | tf_op jit(solution)/shard_map/ppermute | solution.py:376
